TPU v7x, 128 devices: a whole 4x4x4 slice. The times are simulated.
128 devices in a mesh: leaf: 128 (over x, z, y, core).
Axes of the slice: x: 4, y: 4, z: 4, core: 2. Of those that a mesh axis runs over, the one named last changes fastest.
Arguments:
- points: bfloat16 [16, 1048576], P(None, 'leaf'), may hold values from -6 to 6
- coords: float32 [3, 1048576], P(None, 'leaf'), may hold values from 0 to 1, as said below
- basis: bfloat16 [16384, 2048], P('leaf'), may hold values from -0.75 to 0.75
- far_list: int32 [16384, 16], P('leaf'), may hold values from -1 to 16383, as said below
- far_coupling: bfloat16 [16384, 16, 1024], P('leaf'), may hold values from -0.25 to 0.25
- near_list: int32 [16384, 12], P('leaf'), may hold values from -1 to 16383, as said below
- local_transfer: bfloat16 [32512, 1024], P('leaf'), may hold values from -0.875 to 0.875
- top_transfer: bfloat16 [254, 1024], replicated, may hold values from -0.875 to 0.875
- top_coupling: bfloat16 [252, 2, 1024], replicated, may hold values from -0.75 to 0.75
Outputs:
- product: float32 [16, 1048576], P(None, 'leaf')
Inputs may be any that keep to these rules, and one draw needn't show every extreme that they name: `far_list`: -1 marks an empty slot; every other entry is a leaf of the leaf's own device or of a device whose index differs from it in exactly one bit (devices hold 128 leaves each, in order). `near_list`: -1 marks an empty slot; slot 0 holds the leaf itself; every other entry is another leaf at most 8 positions away from it in leaf order. `coords`: the points of leaf i lie in cell i of a k-d split of the unit cube that halves x, y, z in turn, by the bits of i from the most significant.
All inputs are finite; a program needn't handle non-finite values.
Results may differ from a plain program's by a relative error of at most 0.0013.
The roundings to bfloat16 on the way count: a program that leaves them out, or rounds other values in their place, can miss the bound.
Values may be sent and summed in bfloat16 or wider, within the bound.
No kernel may reach another device: no remote copies, remote signals or barrier semaphores. Data moves between devices by JAX's collectives and lax.ppermute only.
A program may use at most 128 MiB of HBM per device.

v0:
```python
import math

import jax
import jax.numpy as jnp
from jax import lax
from jax.sharding import PartitionSpec as P

LEAF = 64
RANK = 32
NF = 16
NN = 12
SPAN = 8


variance = 1.0
nugget = 0.5
decay_rate = math.sqrt(3.0) / 0.3
highest = lax.Precision.HIGHEST


def padded(cells, sides, width):
    for axis, dim in sides:
        count = lax.axis_size(axis)
        ends = count - 1
        head = lax.slice_in_dim(cells, 0, width, axis=dim)
        tail = lax.slice_in_dim(cells, cells.shape[dim] - width, cells.shape[dim], axis=dim)
        cells = jnp.concatenate(
            [
                lax.ppermute(tail, axis, [(i, (i + 1) % count) for i in range(ends)]),
                cells,
                lax.ppermute(head, axis, [((i + 1) % count, i) for i in range(ends)]),
            ],
            axis=dim,
        )
    return cells


def swapped(block, axis, apart):
    count = lax.axis_size(axis)
    route = []
    for low in range(count):
        high = low | 1 << apart
        if high != low and high < count:
            route += [(low, high), (high, low)]
    return lax.ppermute(block, axis, route)


def matern_block(own_coords, part_coords, own_ids, part_ids, present):
    width = own_coords.shape[2]
    squared = jnp.zeros((own_coords.shape[1], width, part_coords.shape[2]), jnp.float32)
    for component in range(3):
        delta = own_coords[component][:, :, None] - part_coords[component][:, None, :]
        squared = squared + delta * delta
    scaled = decay_rate * jnp.sqrt(squared)
    kernel = variance * (1.0 + scaled) * jnp.exp(-scaled)
    column_pos = jnp.arange(part_coords.shape[2], dtype=jnp.int32) % width
    row_pos = jnp.arange(width, dtype=jnp.int32)
    same_leaf = jnp.repeat(part_ids == own_ids[:, None], width, axis=1)
    diagonal = same_leaf[:, None, :] & (column_pos[None, None, :] == row_pos[None, :, None])
    kernel = kernel + nugget * diagonal.astype(jnp.float32)
    live = jnp.repeat(present, width, axis=1).astype(jnp.float32)
    return (kernel * live[:, None, :]).astype(jnp.bfloat16)


def top_start(height, number):
    if height == 0:
        return 0
    return 2 * number - number // 2 ** (height - 1)


def per_device(
    points,
    coords,
    basis,
    far_list,
    far_coupling,
    near_list,
    local_transfer,
    top_transfer,
    top_coupling,
):
    rhs_count = points.shape[0]
    leaf_local = basis.shape[0]
    device = lax.axis_index("leaf")
    devices_all = lax.axis_size("leaf")
    tree_bits = devices_all.bit_length() - 1
    basis_blocks = basis.reshape(leaf_local, LEAF, RANK)
    point_blocks = points.reshape(rhs_count, leaf_local, LEAF)
    leaf_coeff = jnp.einsum(
        "lpk,rlp->lkr", basis_blocks, point_blocks, preferred_element_type=jnp.float32
    ).astype(jnp.bfloat16)
    flat_coeff = leaf_coeff.reshape(leaf_local, RANK * rhs_count)
    ext_points = padded(points, (("leaf", 1),), SPAN * LEAF)
    ext_coords = padded(coords, (("leaf", 1),), SPAN * LEAF)
    present = far_list >= 0
    table = lax.all_gather(flat_coeff, "leaf", axis=0, tiled=True)
    row_index = jnp.where(present, far_list, 0)
    gathered = table[row_index]
    gathered = jnp.where(present[:, :, None], gathered, jnp.zeros_like(gathered))
    gathered = gathered.reshape(leaf_local, NF, RANK, rhs_count)
    coupling = far_coupling.reshape(leaf_local, NF, RANK, RANK)
    far_terms = jnp.einsum("lsab,lsbr->lar", coupling, gathered, preferred_element_type=jnp.float32)
    current = leaf_coeff.astype(jnp.float32)
    offset = 0
    number = leaf_local
    matrices = []
    while number > 1:
        chosen = (
            local_transfer[offset : offset + number].reshape(number, RANK, RANK).astype(jnp.float32)
        )
        matrices.append(chosen)
        partial_value = jnp.einsum("nab,nar->nbr", chosen, current, precision=highest)
        current = partial_value[0::2] + partial_value[1::2]
        offset += number
        number //= 2
    device_coeff = current[0]

    def top_matrix(height, node):
        picked = lax.dynamic_index_in_dim(
            top_transfer, top_start(height, devices_all) + node, 0, keepdims=False
        )
        return picked.reshape(RANK, RANK).astype(jnp.float32)

    top_terms = []
    mine = device_coeff
    before_mine = jnp.zeros_like(mine)
    before_sibling = jnp.zeros_like(mine)
    for height in range(tree_bits):
        received = swapped(jnp.stack([mine, before_mine, before_sibling]), "leaf", height)
        if height >= 1:
            lower = jnp.right_shift(device, height - 1)
            partner_first = lower % 2 == 0
            cousin_left = jnp.where(partner_first, received[1], received[2])
            cousin_right = jnp.where(partner_first, received[2], received[1])
            coupled_height = height - 1
            coupled_picked = lax.dynamic_index_in_dim(
                top_coupling, top_start(coupled_height, devices_all) + lower, 0, keepdims=False
            )
            pair = coupled_picked.reshape(2, RANK, RANK).astype(jnp.float32)
            top_terms.append(
                jnp.dot(pair[0], cousin_left, precision=highest)
                + jnp.dot(pair[1], cousin_right, precision=highest)
            )
        sibling = received[0]
        before_mine = mine
        before_sibling = sibling
        if height <= tree_bits - 3:
            node = jnp.right_shift(device, height)
            own_term = jnp.dot(top_matrix(height, node).T, mine, precision=highest)
            sibling_term = jnp.dot(
                top_matrix(height, jnp.bitwise_xor(node, 1)).T, sibling, precision=highest
            )
            mine = own_term + sibling_term
        else:
            mine = jnp.zeros_like(mine)
    field = top_terms[tree_bits - 2]
    for height in range(tree_bits - 2, 0, -1):
        child = jnp.right_shift(device, height - 1)
        field = top_terms[height - 1] + jnp.dot(
            top_matrix(height - 1, child), field, precision=highest
        )
    field = field[None]
    for depth_num in range(len(matrices) - 1, -1, -1):
        spread = jnp.einsum(
            "nab,nbr->nar", matrices[depth_num], jnp.repeat(field, 2, axis=0), precision=highest
        )
        field = far_terms + spread if depth_num == 0 else spread
    leaf_field = field.astype(jnp.bfloat16)
    far_part = jnp.einsum(
        "lpk,lkr->rlp", basis_blocks, leaf_field, preferred_element_type=jnp.float32
    )
    far_part = far_part.reshape(rhs_count, leaf_local * LEAF)
    ext_leaves = leaf_local + 2 * SPAN
    point_ext = ext_points.reshape(rhs_count, ext_leaves, LEAF)
    coord_ext = ext_coords.reshape(3, ext_leaves, LEAF)
    first_global = device * leaf_local
    block_leaves = min(16, leaf_local)

    def near_block(block_num):
        begin_leaf = block_num * block_leaves
        own_ids = first_global + begin_leaf + jnp.arange(block_leaves, dtype=jnp.int32)
        near_partners = lax.dynamic_slice_in_dim(near_list, begin_leaf, block_leaves, 0)
        near_present = near_partners >= 0
        clamped = jnp.where(near_present, near_partners, own_ids[:, None])
        local_ids = clamped - first_global + SPAN
        own_coords = lax.dynamic_slice_in_dim(coord_ext, begin_leaf + SPAN, block_leaves, 1)
        part_coords = coord_ext[:, local_ids].reshape(3, block_leaves, NN * LEAF)
        part_points = point_ext[:, local_ids].reshape(rhs_count, block_leaves, NN * LEAF)
        kernel = matern_block(own_coords, part_coords, own_ids, clamped, near_present)
        return jnp.einsum("bpq,rbq->rbp", kernel, part_points, preferred_element_type=jnp.float32)

    near_part = lax.map(near_block, jnp.arange(leaf_local // block_leaves, dtype=jnp.int32))
    near_part = jnp.transpose(near_part, (1, 0, 2, 3)).reshape(rhs_count, leaf_local * LEAF)
    return near_part + far_part


def solution(mesh):
    return jax.shard_map(
        per_device,
        mesh=mesh,
        in_specs=(
            P(None, "leaf"),
            P(None, "leaf"),
            P("leaf", None),
            P("leaf", None),
            P("leaf", None, None),
            P("leaf", None),
            P("leaf", None),
            P(),
            P(),
        ),
        out_specs=P(None, "leaf"),
        check_vma=False,
    )
```

profile of v0, /device:TPU:0, one launch (start us, length us, event | category | flops | bytes accessed | tf_op | source)
XLA Modules:
  0.0 252.5 jit_solution(12542205519363582877)
XLA Ops:
  6.5 1.4 copy.76
  8.0 1.7 copy.77
  9.7 1.8 reshape.239
  13.4 1.3 fusion.149
  14.8 1.3 collective-permute-start.1
  16.1 3.6 %collective-permute-start = (bf16[16,512]{1,0:T(8,128)(2,1)}, bf16[16,512]{1,0:T(8,128)(2,1)}, u32[]{:S(2)}, u32[]{:S(2)}) collective-permute-start(bf16[16,512]{1,0:T(8,128)(2,1)} %get-tuple-element.193), channel_id=1, source_target_pairs={{0,1},{1,2},{2,3},{3,4},{4,5},{5,6},{6,7},{7,8},{8,9},{9,10},{10,1... | collective-permute-start | bytes 49160 | tf_op jit(solution)/shard_map/ppermute | solution.py:29
  19.7 1.3 fusion.150
  21.0 1.3 collective-permute-start.3
  22.3 3.8 %collective-permute-start.2 = (f32[3,512]{1,0:T(4,128)}, f32[3,512]{1,0:T(4,128)}, u32[]{:S(2)}, u32[]{:S(2)}) collective-permute-start(f32[3,512]{1,0:T(4,128)} %get-tuple-element.195), channel_id=1, source_target_pairs={{0,1},{1,2},{2,3},{3,4},{4,5},{5,6},{6,7},{7,8},{8,9},{9,10},{10,1... | collective-permute-start | bytes 18440 | tf_op jit(solution)/shard_map/ppermute | solution.py:29
  29.9 1.4 copy.86
  33.4 1.2 collective-permute-start.4
  34.6 6.5 %copy.82 = bf16[128,16,1024]{0,2,1:T(8,128)(2,1)} copy(bf16[128,16,1024]{2,1,0:T(8,128)(2,1)} %param.15) | data formatting | bytes 8388608 | tf_op args[4]
  41.2 23.1 %copy.84 = bf16[128,16,32,32]{3,2,1,0:T(8,128)(2,1)} copy(bf16[128,16,32,32]{0,3,2,1:T(8,128)(2,1)} %bitcast.208) | data formatting | bytes 8388608 | tf_op jit(solution)/shard_map/reshape | solution.py:101
  65.2 1.0 fusion.122
  67.9 1.1 fusion.124
  79.4 1.7 collective-permute-start.5
  82.2 1.6 collective-permute-done.5
  84.5 6.5 %collective-permute-start.6 = (f32[3,32,16]{1,2,0:T(8,128)}, f32[3,32,16]{1,2,0:T(8,128)}, u32[]{:S(2)}, u32[]{:S(2)}) collective-permute-start(f32[3,32,16]{1,2,0:T(8,128)} %pad_maximum_fusion.3), channel_id=1, source_target_pairs={{0,4},{4,0},{1,5},{5,1},{2,6},{6,2},{3,7},{7,3},{8,12},{12,8},{9,1... | collective-permute-start | bytes 18440 | tf_op jit(solution)/shard_map/ppermute | solution.py:45
  93.8 69.6 %while.13 = (s32[]{:T(128)}, f32[8,16,16,64]{3,1,2,0:T(8,128)}, s32[8]{0:T(128)S(1)}, s32[128,12]{0,1:T(8,128)S(1)}, s32[]{:T(128)}, /*index=5*/bf16[16,144,64]{...) while((s32[]{:T(128)}, f32[8,16,16,64]{3,1,2,0:T(8,128)}, ...), condition=%wide.region_1.2_spmd, body=%wide.region_0.1_spmd.sunk | while | flops 38592092 | bytes 4613813 | solution.py:192
  97.4 0.9 gather_fusion.1
  99.0 3.6 %fusion.229 = f32[8,16,16,64]{3,1,2,0:T(8,128)} fusion(f32[8,16,16,64]{3,1,2,0:T(8,128)} %get-tuple-element.272, s32[]{:T(128)S(6)} %copy.114, bf16[16,16,768]{2,0,1:T(8,128)(2,1)S(1)} %reshape.336, f32[16,768]{1,0:T(8,128)S(1)} %convert_element_type.73, f32[16,768]{1,0:T(8,128)S(1)} %sub.206, f32[16,64]{1,0:T(8,128)S(1)} %bitcast.221, ...), kind=kOutput, calls=%fused_computation.8.clone.1 | convolution fusion | flops 38535168 | bytes 794628 | tf_op jit(solution)/shard_map/while/body/eval_jaxpr/bpq,rbq->rbp/dot_general | solution.py:190
  106.1 0.9 gather_fusion.1
  107.7 3.6 %fusion.229 = f32[8,16,16,64]{3,1,2,0:T(8,128)} fusion(f32[8,16,16,64]{3,1,2,0:T(8,128)} %get-tuple-element.272, s32[]{:T(128)S(6)} %copy.114, bf16[16,16,768]{2,0,1:T(8,128)(2,1)S(1)} %reshape.336, f32[16,768]{1,0:T(8,128)S(1)} %convert_element_type.73, f32[16,768]{1,0:T(8,128)S(1)} %sub.206, f32[16,64]{1,0:T(8,128)S(1)} %bitcast.221, ...), kind=kOutput, calls=%fused_computation.8.clone.1 | convolution fusion | flops 38535168 | bytes 794628 | tf_op jit(solution)/shard_map/while/body/eval_jaxpr/bpq,rbq->rbp/dot_general | solution.py:190
  114.8 0.9 gather_fusion.1
  116.4 3.6 %fusion.229 = f32[8,16,16,64]{3,1,2,0:T(8,128)} fusion(f32[8,16,16,64]{3,1,2,0:T(8,128)} %get-tuple-element.272, s32[]{:T(128)S(6)} %copy.114, bf16[16,16,768]{2,0,1:T(8,128)(2,1)S(1)} %reshape.336, f32[16,768]{1,0:T(8,128)S(1)} %convert_element_type.73, f32[16,768]{1,0:T(8,128)S(1)} %sub.206, f32[16,64]{1,0:T(8,128)S(1)} %bitcast.221, ...), kind=kOutput, calls=%fused_computation.8.clone.1 | convolution fusion | flops 38535168 | bytes 794628 | tf_op jit(solution)/shard_map/while/body/eval_jaxpr/bpq,rbq->rbp/dot_general | solution.py:190
  125.1 3.6 %fusion.229 = f32[8,16,16,64]{3,1,2,0:T(8,128)} fusion(f32[8,16,16,64]{3,1,2,0:T(8,128)} %get-tuple-element.272, s32[]{:T(128)S(6)} %copy.114, bf16[16,16,768]{2,0,1:T(8,128)(2,1)S(1)} %reshape.336, f32[16,768]{1,0:T(8,128)S(1)} %convert_element_type.73, f32[16,768]{1,0:T(8,128)S(1)} %sub.206, f32[16,64]{1,0:T(8,128)S(1)} %bitcast.221, ...), kind=kOutput, calls=%fused_computation.8.clone.1 | convolution fusion | flops 38535168 | bytes 794628 | tf_op jit(solution)/shard_map/while/body/eval_jaxpr/bpq,rbq->rbp/dot_general | solution.py:190
  132.2 0.9 gather_fusion.1
  133.8 3.6 %fusion.229 = f32[8,16,16,64]{3,1,2,0:T(8,128)} fusion(f32[8,16,16,64]{3,1,2,0:T(8,128)} %get-tuple-element.272, s32[]{:T(128)S(6)} %copy.114, bf16[16,16,768]{2,0,1:T(8,128)(2,1)S(1)} %reshape.336, f32[16,768]{1,0:T(8,128)S(1)} %convert_element_type.73, f32[16,768]{1,0:T(8,128)S(1)} %sub.206, f32[16,64]{1,0:T(8,128)S(1)} %bitcast.221, ...), kind=kOutput, calls=%fused_computation.8.clone.1 | convolution fusion | flops 38535168 | bytes 794628 | tf_op jit(solution)/shard_map/while/body/eval_jaxpr/bpq,rbq->rbp/dot_general | solution.py:190
  140.9 0.9 gather_fusion.1
  142.5 3.6 %fusion.229 = f32[8,16,16,64]{3,1,2,0:T(8,128)} fusion(f32[8,16,16,64]{3,1,2,0:T(8,128)} %get-tuple-element.272, s32[]{:T(128)S(6)} %copy.114, bf16[16,16,768]{2,0,1:T(8,128)(2,1)S(1)} %reshape.336, f32[16,768]{1,0:T(8,128)S(1)} %convert_element_type.73, f32[16,768]{1,0:T(8,128)S(1)} %sub.206, f32[16,64]{1,0:T(8,128)S(1)} %bitcast.221, ...), kind=kOutput, calls=%fused_computation.8.clone.1 | convolution fusion | flops 38535168 | bytes 794628 | tf_op jit(solution)/shard_map/while/body/eval_jaxpr/bpq,rbq->rbp/dot_general | solution.py:190
  149.6 0.9 gather_fusion.1
  151.2 3.6 %fusion.229 = f32[8,16,16,64]{3,1,2,0:T(8,128)} fusion(f32[8,16,16,64]{3,1,2,0:T(8,128)} %get-tuple-element.272, s32[]{:T(128)S(6)} %copy.114, bf16[16,16,768]{2,0,1:T(8,128)(2,1)S(1)} %reshape.336, f32[16,768]{1,0:T(8,128)S(1)} %convert_element_type.73, f32[16,768]{1,0:T(8,128)S(1)} %sub.206, f32[16,64]{1,0:T(8,128)S(1)} %bitcast.221, ...), kind=kOutput, calls=%fused_computation.8.clone.1 | convolution fusion | flops 38535168 | bytes 794628 | tf_op jit(solution)/shard_map/while/body/eval_jaxpr/bpq,rbq->rbp/dot_general | solution.py:190
  158.3 0.9 gather_fusion.1
  159.9 3.6 %fusion.229 = f32[8,16,16,64]{3,1,2,0:T(8,128)} fusion(f32[8,16,16,64]{3,1,2,0:T(8,128)} %get-tuple-element.272, s32[]{:T(128)S(6)} %copy.114, bf16[16,16,768]{2,0,1:T(8,128)(2,1)S(1)} %reshape.336, f32[16,768]{1,0:T(8,128)S(1)} %convert_element_type.73, f32[16,768]{1,0:T(8,128)S(1)} %sub.206, f32[16,64]{1,0:T(8,128)S(1)} %bitcast.221, ...), kind=kOutput, calls=%fused_computation.8.clone.1 | convolution fusion | flops 38535168 | bytes 794628 | tf_op jit(solution)/shard_map/while/body/eval_jaxpr/bpq,rbq->rbp/dot_general | solution.py:190
  163.7 1.7 copy.74
  167.3 2.0 collective-permute-start.7
  170.2 0.9 collective-permute-done.7
  171.3 7.7 %collective-permute-start.8 = (f32[3,32,16]{1,2,0:T(8,128)S(1)}, f32[3,32,16]{1,2,0:T(8,128)S(1)}, u32[]{:S(2)}, u32[]{:S(2)}) collective-permute-start(f32[3,32,16]{1,2,0:T(8,128)S(1)} %pad_maximum_fusion.5), channel_id=1, source_target_pairs={{0,16},{16,0},{1,17},{17,1},{2,18},{18,2},{3,19},{19,3},{4,20},{20... | collective-permute-start | bytes 18440 | tf_op jit(solution)/shard_map/ppermute | solution.py:45
  179.2 1.6 collective-permute-done.8
  180.9 1.6 collective-permute-start.9
  182.7 2.2 collective-permute-done.9
  184.9 3.2 %collective-permute-start.10 = (f32[3,32,16]{1,2,0:T(8,128)S(1)}, f32[3,32,16]{1,2,0:T(8,128)S(1)}, u32[]{:S(2)}, u32[]{:S(2)}) collective-permute-start(f32[3,32,16]{1,2,0:T(8,128)S(1)} %pad_maximum_fusion.7), channel_id=1, source_target_pairs={{0,64},{64,0},{1,65},{65,1},{2,66},{66,2},{3,67},{67,3},{4,68},{68... | collective-permute-start | bytes 18440 | tf_op jit(solution)/shard_map/ppermute | solution.py:45
  188.3 2.2 collective-permute-done.10
  195.1 1.7 convolution_bitcast_fusion.2
  196.9 15.5 %gather_fusion.2 = bf16[2048,512]{1,0:T(8,128)(2,1)S(1)} fusion(bf16[16384,512]{1,0:T(8,128)(2,1)} %all-gather.2.cloned.1.call-done, s32[2048]{0:T(1024)S(1)} %broadcast_clamp_fusion), kind=kCustom, calls=%fused_computation.2 | custom fusion | bytes 4202496 | tf_op jit(solution)/shard_map/gather | solution.py:98
  212.4 15.5 %gather.20 = bf16[128,16,32,16]{3,2,1,0:T(8,128)(2,1)} reshape(bf16[2048,512]{1,0:T(8,128)(2,1)S(1)} %gather_fusion.2) | data formatting | bytes 4194304 | tf_op jit(solution)/shard_map/gather | solution.py:98
  227.9 14.0 %fusion.17 = f32[128,16,32]{2,1,0:T(8,128)S(1)} fusion(bf16[128,16,32,32]{3,2,1,0:T(8,128)(2,1)} %copy.84, bf16[128,16,32,16]{3,2,1,0:T(8,128)(2,1)} %gather.20, pred[128,16]{1,0:T(8,128)(4,1)S(1)} %copy-done.41), kind=kOutput, calls=%fused_computation.34 | convolution fusion | flops 68157440 | bytes 6555648 | tf_op jit(solution)/shard_map/lsab,lsbr->lar/dot_general | solution.py:102
  242.0 1.8 fusion.20
  (437 shorter events, 64.3 us)
Async XLA Ops:
  6.5 19.6 %copy-start.8 = (bf16[254,1024]{1,0:T(8,128)(2,1)S(1)}, bf16[254,1024]{1,0:T(8,128)(2,1)}, u32[]{:S(2)}) copy-start(bf16[254,1024]{1,0:T(8,128)(2,1)} %param.17) | copy-start | bytes 1560580
  6.5 190.3 %all-gather.2.cloned.1.call-start = ((), (), s32[]{:S(2)}) async-start(), calls=%async_computation | async-start | bytes 16908288 | tf_op jit(solution)/shard_map/all_gather | solution.py:96
  7.9 18.9 %slice-start = ((bf16[254,1024]{1,0:T(8,128)(2,1)}), bf16[4,1024]{1,0:T(4,128)(2,1)S(1)}, s32[]{:S(2)}) async-start(bf16[254,1024]{1,0:T(8,128)(2,1)} %param.17), calls=%async_computation.1 | async-start | bytes 16384 | tf_op jit(solution)/shard_map/slice | solution.py:109
  7.9 19.0 %slice-start.1 = ((bf16[254,1024]{1,0:T(8,128)(2,1)}), bf16[8,1024]{1,0:T(8,128)(2,1)S(1)}, s32[]{:S(2)}) async-start(bf16[254,1024]{1,0:T(8,128)(2,1)} %param.17), calls=%async_computation.2 | async-start | bytes 32768 | tf_op jit(solution)/shard_map/slice | solution.py:109
  7.9 19.8 %slice-start.2 = ((bf16[254,1024]{1,0:T(8,128)(2,1)}), bf16[16,1024]{1,0:T(8,128)(2,1)S(1)}, s32[]{:S(2)}) async-start(bf16[254,1024]{1,0:T(8,128)(2,1)} %param.17), calls=%async_computation.3 | async-start | bytes 65536 | tf_op jit(solution)/shard_map/slice | solution.py:109
  7.9 20.5 %slice-start.3 = ((bf16[254,1024]{1,0:T(8,128)(2,1)}), bf16[32,1024]{1,0:T(8,128)(2,1)S(1)}, s32[]{:S(2)}) async-start(bf16[254,1024]{1,0:T(8,128)(2,1)} %param.17), calls=%async_computation.4 | async-start | bytes 131072 | tf_op jit(solution)/shard_map/slice | solution.py:109
  9.7 20.0 %copy-start.2 = (bf16[128,64,32]{1,2,0:T(8,128)(2,1)}, bf16[128,64,32]{1,2,0:T(8,128)(2,1)S(1)}, u32[]{:S(2)}) copy-start(bf16[128,64,32]{1,2,0:T(8,128)(2,1)S(1)} %copy.77) | copy-start | bytes 1572868
  9.7 19.0 %slice-start.4 = ((bf16[254,1024]{1,0:T(8,128)(2,1)}), bf16[64,1024]{1,0:T(8,128)(2,1)S(1)}, s32[]{:S(2)}) async-start(bf16[254,1024]{1,0:T(8,128)(2,1)} %param.17), calls=%async_computation.5 | async-start | bytes 262144 | tf_op jit(solution)/shard_map/slice | solution.py:109
  12.1 17.5 %slice-start.5 = ((bf16[254,1024]{1,0:T(8,128)(2,1)}), bf16[128,1024]{1,0:T(8,128)(2,1)S(1)}, s32[]{:S(2)}) async-start(bf16[254,1024]{1,0:T(8,128)(2,1)} %param.17), calls=%async_computation.6 | async-start | bytes 524288 | tf_op jit(solution)/shard_map/slice | solution.py:109
  14.8 77.7 %collective-permute-start.1 = (bf16[16,512]{1,0:T(8,128)(2,1)}, bf16[16,512]{1,0:T(8,128)(2,1)}, u32[]{:S(2)}, u32[]{:S(2)}) collective-permute-start(bf16[16,512]{1,0:T(8,128)(2,1)} %get-tuple-element.194), channel_id=1, source_target_pairs={{1,0},{2,1},{3,2},{4,3},{5,4},{6,5},{7,6},{8,7},{9,8},{10,9},{11,1... | collective-permute-start | bytes 49160 | tf_op jit(solution)/shard_map/ppermute | solution.py:31
  16.1 76.4 %collective-permute-start = (bf16[16,512]{1,0:T(8,128)(2,1)}, bf16[16,512]{1,0:T(8,128)(2,1)}, u32[]{:S(2)}, u32[]{:S(2)}) collective-permute-start(bf16[16,512]{1,0:T(8,128)(2,1)} %get-tuple-element.193), channel_id=1, source_target_pairs={{0,1},{1,2},{2,3},{3,4},{4,5},{5,6},{6,7},{7,8},{8,9},{9,10},{10,1... | collective-permute-start | bytes 49160 | tf_op jit(solution)/shard_map/ppermute | solution.py:29
  21.0 60.0 %collective-permute-start.3 = (f32[3,512]{1,0:T(4,128)}, f32[3,512]{1,0:T(4,128)}, u32[]{:S(2)}, u32[]{:S(2)}) collective-permute-start(f32[3,512]{1,0:T(4,128)} %get-tuple-element.196), channel_id=1, source_target_pairs={{1,0},{2,1},{3,2},{4,3},{5,4},{6,5},{7,6},{8,7},{9,8},{10,9},{11,1... | collective-permute-start | bytes 18440 | tf_op jit(solution)/shard_map/ppermute | solution.py:31
  22.3 58.7 %collective-permute-start.2 = (f32[3,512]{1,0:T(4,128)}, f32[3,512]{1,0:T(4,128)}, u32[]{:S(2)}, u32[]{:S(2)}) collective-permute-start(f32[3,512]{1,0:T(4,128)} %get-tuple-element.195), channel_id=1, source_target_pairs={{0,1},{1,2},{2,3},{3,4},{4,5},{5,6},{6,7},{7,8},{8,9},{9,10},{10,1... | collective-permute-start | bytes 18440 | tf_op jit(solution)/shard_map/ppermute | solution.py:29
  33.4 45.9 %collective-permute-start.4 = (f32[3,32,16]{1,2,0:T(8,128)S(1)}, f32[3,32,16]{1,2,0:T(8,128)S(1)}, u32[]{:S(2)}, u32[]{:S(2)}) collective-permute-start(f32[3,32,16]{1,2,0:T(8,128)S(1)} %stack.42), channel_id=1, source_target_pairs={{0,1},{1,0},{2,3},{3,2},{4,5},{5,4},{6,7},{7,6},{8,9},{9,8},{10,11... | collective-permute-start | bytes 18440 | tf_op jit(solution)/shard_map/ppermute | solution.py:45
  41.2 23.1 %copy-start.29 = (s32[128,16]{0,1:T(8,128)S(1)}, s32[128,16]{0,1:T(8,128)}, u32[]{:S(2)}) copy-start(s32[128,16]{0,1:T(8,128)} %param.14) | copy-start | bytes 24580
  41.2 39.9 %copy-start.14 = (f32[3,8192]{1,0:T(4,128)S(1)}, f32[3,8192]{1,0:T(4,128)}, u32[]{:S(2)}) copy-start(f32[3,8192]{1,0:T(4,128)} %param.12) | copy-start | bytes 294916
  41.2 51.3 %copy-start.5 = (bf16[16,8192]{1,0:T(8,128)(2,1)S(1)}, bf16[16,8192]{1,0:T(8,128)(2,1)}, u32[]{:S(2)}) copy-start(bf16[16,8192]{1,0:T(8,128)(2,1)} %param.11) | copy-start | bytes 786436
  64.3 29.5 %copy-start.13 = (s32[128,12]{0,1:T(8,128)S(1)}, s32[128,12]{0,1:T(8,128)}, u32[]{:S(2)}) copy-start(s32[128,12]{0,1:T(8,128)} %param.16) | copy-start | bytes 18436
  66.4 17.4 %copy-start.17 = (bf16[32,32]{1,0:T(8,128)(2,1)}, bf16[32,32]{1,0:T(8,128)(2,1)S(1)}, u32[]{:S(2)}) copy-start(bf16[32,32]{1,0:T(8,128)(2,1)S(1)} %reshape.251) | copy-start | bytes 6148
  66.5 26.0 %copy-start.19 = (bf16[32,32]{1,0:T(8,128)(2,1)}, bf16[32,32]{1,0:T(8,128)(2,1)S(1)}, u32[]{:S(2)}) copy-start(bf16[32,32]{1,0:T(8,128)(2,1)S(1)} %reshape.253) | copy-start | bytes 6148
  79.4 4.4 %collective-permute-start.5 = (f32[3,32,16]{1,2,0:T(8,128)S(1)}, f32[3,32,16]{1,2,0:T(8,128)S(1)}, u32[]{:S(2)}, u32[]{:S(2)}) collective-permute-start(f32[3,32,16]{1,2,0:T(8,128)S(1)} %pad_maximum_fusion.2), channel_id=1, source_target_pairs={{0,2},{2,0},{1,3},{3,1},{4,6},{6,4},{5,7},{7,5},{8,10},{10,8},{9,1... | collective-permute-start | bytes 18440 | tf_op jit(solution)/shard_map/ppermute | solution.py:45
  84.5 81.2 %collective-permute-start.6 = (f32[3,32,16]{1,2,0:T(8,128)}, f32[3,32,16]{1,2,0:T(8,128)}, u32[]{:S(2)}, u32[]{:S(2)}) collective-permute-start(f32[3,32,16]{1,2,0:T(8,128)} %pad_maximum_fusion.3), channel_id=1, source_target_pairs={{0,4},{4,0},{1,5},{5,1},{2,6},{6,2},{3,7},{7,3},{8,12},{12,8},{9,1... | collective-permute-start | bytes 18440 | tf_op jit(solution)/shard_map/ppermute | solution.py:45
  163.5 15.5 %copy-start.22 = (bf16[32,32]{1,0:T(8,128)(2,1)S(1)}, bf16[32,32]{1,0:T(8,128)(2,1)}, u32[]{:S(2)}) copy-start(bf16[32,32]{1,0:T(8,128)(2,1)} %reshape.257) | copy-start | bytes 6148
  163.5 15.6 %copy-start.27 = (bf16[32,32]{1,0:T(8,128)(2,1)S(1)}, bf16[32,32]{1,0:T(8,128)(2,1)}, u32[]{:S(2)}) copy-start(bf16[32,32]{1,0:T(8,128)(2,1)} %squeeze.122) | copy-start | bytes 6148
  163.5 17.3 %copy-start.36 = (bf16[32,32]{1,0:T(8,128)(2,1)S(1)}, bf16[32,32]{1,0:T(8,128)(2,1)}, u32[]{:S(2)}) copy-start(bf16[32,32]{1,0:T(8,128)(2,1)} %reshape.258) | copy-start | bytes 6148
  163.5 19.0 %copy-start.26 = (bf16[32,32]{1,0:T(8,128)(2,1)S(1)}, bf16[32,32]{1,0:T(8,128)(2,1)}, u32[]{:S(2)}) copy-start(bf16[32,32]{1,0:T(8,128)(2,1)} %squeeze.125) | copy-start | bytes 6148
  163.5 21.4 %copy-start.42 = (f32[3]{0:T(128)S(1)}, f32[3]{0:T(128)}, u32[]{:S(2)}) copy-start(f32[3]{0:T(128)} %pad.1.clone) | copy-start | bytes 40
  163.5 24.7 %copy-start.25 = (bf16[32,32]{1,0:T(8,128)(2,1)S(1)}, bf16[32,32]{1,0:T(8,128)(2,1)}, u32[]{:S(2)}) copy-start(bf16[32,32]{1,0:T(8,128)(2,1)} %squeeze.128) | copy-start | bytes 6148
  163.5 27.0 %copy-start.24 = (bf16[32,32]{1,0:T(8,128)(2,1)S(1)}, bf16[32,32]{1,0:T(8,128)(2,1)}, u32[]{:S(2)}) copy-start(bf16[32,32]{1,0:T(8,128)(2,1)} %squeeze.130) | copy-start | bytes 6148
  163.5 27.1 %copy-start.30 = (bf16[32,32]{1,0:T(8,128)(2,1)S(1)}, bf16[32,32]{1,0:T(8,128)(2,1)}, u32[]{:S(2)}) copy-start(bf16[32,32]{1,0:T(8,128)(2,1)} %squeeze.129) | copy-start | bytes 6148
  163.5 27.4 %copy-start.31 = (bf16[32,32]{1,0:T(8,128)(2,1)S(1)}, bf16[32,32]{1,0:T(8,128)(2,1)}, u32[]{:S(2)}) copy-start(bf16[32,32]{1,0:T(8,128)(2,1)} %squeeze.126) | copy-start | bytes 6148
  163.6 27.6 %copy-start.32 = (bf16[32,32]{1,0:T(8,128)(2,1)S(1)}, bf16[32,32]{1,0:T(8,128)(2,1)}, u32[]{:S(2)}) copy-start(bf16[32,32]{1,0:T(8,128)(2,1)} %squeeze.123) | copy-start | bytes 6148
  163.6 27.8 %copy-start.20 = (bf16[32,32]{1,0:T(8,128)(2,1)S(1)}, bf16[32,32]{1,0:T(8,128)(2,1)}, u32[]{:S(2)}) copy-start(bf16[32,32]{1,0:T(8,128)(2,1)} %copy-done.19) | copy-start | bytes 6148
  163.6 27.9 %copy-start.33 = (bf16[32,32]{1,0:T(8,128)(2,1)S(1)}, bf16[32,32]{1,0:T(8,128)(2,1)}, u32[]{:S(2)}) copy-start(bf16[32,32]{1,0:T(8,128)(2,1)} %squeeze.120) | copy-start | bytes 6148
  163.6 28.0 %copy-start.18 = (bf16[32,32]{1,0:T(8,128)(2,1)S(1)}, bf16[32,32]{1,0:T(8,128)(2,1)}, u32[]{:S(2)}) copy-start(bf16[32,32]{1,0:T(8,128)(2,1)} %copy-done.17) | copy-start | bytes 6148
  163.6 28.2 %copy-start.34 = (bf16[32,32]{1,0:T(8,128)(2,1)S(1)}, bf16[32,32]{1,0:T(8,128)(2,1)}, u32[]{:S(2)}) copy-start(bf16[32,32]{1,0:T(8,128)(2,1)} %squeeze.117) | copy-start | bytes 6148
  163.6 29.1 %copy-start.35 = (bf16[32,32]{1,0:T(8,128)(2,1)S(1)}, bf16[32,32]{1,0:T(8,128)(2,1)}, u32[]{:S(2)}) copy-start(bf16[32,32]{1,0:T(8,128)(2,1)} %squeeze.113) | copy-start | bytes 6148
  163.6 29.1 %copy-start.39 = (f32[32,16]{0,1:T(8,128)S(1)}, f32[32,16]{0,1:T(8,128)}, u32[]{:S(2)}) copy-start(f32[32,16]{0,1:T(8,128)} %fusion.65) | copy-start | bytes 6148
  163.6 30.0 %copy-start.16 = (bf16[2,32,32]{2,1,0:T(8,128)(2,1)S(1)}, bf16[2,32,32]{2,1,0:T(8,128)(2,1)}, u32[]{:S(2)}) copy-start(bf16[2,32,32]{2,1,0:T(8,128)(2,1)} %reshape.249) | copy-start | bytes 12292
  163.6 30.1 %copy-start.12 = (bf16[4,32,32]{2,1,0:T(8,128)(2,1)S(1)}, bf16[4,32,32]{2,1,0:T(8,128)(2,1)}, u32[]{:S(2)}) copy-start(bf16[4,32,32]{2,1,0:T(8,128)(2,1)} %copy-done.11) | copy-start | bytes 24580
  163.6 30.3 %copy-start.10 = (bf16[8,32,32]{2,1,0:T(8,128)(2,1)S(1)}, bf16[8,32,32]{2,1,0:T(8,128)(2,1)}, u32[]{:S(2)}) copy-start(bf16[8,32,32]{2,1,0:T(8,128)(2,1)} %reshape.247) | copy-start | bytes 49156
  163.7 30.5 %copy-start.7 = (bf16[16,32,32]{2,1,0:T(8,128)(2,1)S(1)}, bf16[16,32,32]{2,1,0:T(8,128)(2,1)}, u32[]{:S(2)}) copy-start(bf16[16,32,32]{2,1,0:T(8,128)(2,1)} %reshape.246) | copy-start | bytes 98308
  167.3 3.9 %collective-permute-start.7 = (f32[3,32,16]{1,2,0:T(8,128)S(1)}, f32[3,32,16]{1,2,0:T(8,128)S(1)}, u32[]{:S(2)}, u32[]{:S(2)}) collective-permute-start(f32[3,32,16]{1,2,0:T(8,128)S(1)} %pad_maximum_fusion.4), channel_id=1, source_target_pairs={{0,8},{8,0},{1,9},{9,1},{2,10},{10,2},{3,11},{11,3},{4,12},{12,4},... | collective-permute-start | bytes 18440 | tf_op jit(solution)/shard_map/ppermute | solution.py:45
  171.3 9.5 %collective-permute-start.8 = (f32[3,32,16]{1,2,0:T(8,128)S(1)}, f32[3,32,16]{1,2,0:T(8,128)S(1)}, u32[]{:S(2)}, u32[]{:S(2)}) collective-permute-start(f32[3,32,16]{1,2,0:T(8,128)S(1)} %pad_maximum_fusion.5), channel_id=1, source_target_pairs={{0,16},{16,0},{1,17},{17,1},{2,18},{18,2},{3,19},{19,3},{4,20},{20... | collective-permute-start | bytes 18440 | tf_op jit(solution)/shard_map/ppermute | solution.py:45
  180.9 3.9 %collective-permute-start.9 = (f32[3,32,16]{1,2,0:T(8,128)S(1)}, f32[3,32,16]{1,2,0:T(8,128)S(1)}, u32[]{:S(2)}, u32[]{:S(2)}) collective-permute-start(f32[3,32,16]{1,2,0:T(8,128)S(1)} %pad_maximum_fusion.6), channel_id=1, source_target_pairs={{0,32},{32,0},{1,33},{33,1},{2,34},{34,2},{3,35},{35,3},{4,36},{36... | collective-permute-start | bytes 18440 | tf_op jit(solution)/shard_map/ppermute | solution.py:45
  184.9 5.6 %collective-permute-start.10 = (f32[3,32,16]{1,2,0:T(8,128)S(1)}, f32[3,32,16]{1,2,0:T(8,128)S(1)}, u32[]{:S(2)}, u32[]{:S(2)}) collective-permute-start(f32[3,32,16]{1,2,0:T(8,128)S(1)} %pad_maximum_fusion.7), channel_id=1, source_target_pairs={{0,64},{64,0},{1,65},{65,1},{2,66},{66,2},{3,67},{67,3},{4,68},{68... | collective-permute-start | bytes 18440 | tf_op jit(solution)/shard_map/ppermute | solution.py:45
  212.4 15.5 %copy-start.41 = (pred[128,16]{1,0:T(8,128)(4,1)S(1)}, pred[128,16]{1,0:T(8,128)(4,1)}, u32[]{:S(2)}) copy-start(pred[128,16]{1,0:T(8,128)(4,1)} %copy.75) | copy-start | bytes 6148
  227.9 14.1 %copy-start.1 = (bf16[128,32,32]{2,1,0:T(8,128)(2,1)S(1)}, bf16[128,32,32]{2,1,0:T(8,128)(2,1)}, u32[]{:S(2)}) copy-start(bf16[128,32,32]{2,1,0:T(8,128)(2,1)} %copy-done) | copy-start | bytes 786436
  (29 other events, 113.1 us)
Sparse Core Ops, SparseCore 0:
  13.6 82.8 all-gather.1
where the time goes:
time: 254 us; the launch traced here: 253 us
  local copies, waits for them, and re-layouts  127 us (50%)
  matrix products  57.7 us (23%)
  starting transfers between devices  33.9 us (13%)
  between operations  14.2 us (6%)
  waiting for transfers between devices  8.49 us (3%)
  loops' own time  6.12 us (2%)
  other arithmetic  4.71 us (2%)
    gather x2, local copies, waits for them, and re-layouts, per_device(): gathered = table[row_index]  31 us
    dot_general x8, matrix products, near_block(): jnp.einsum('bpq,rbq->rbp', kernel, part_points, preferred_element_type=jn...  28.5 us
    ppermute x7, starting transfers between devices, swapped(): return lax.ppermute(block, axis, route)  23.9 us
    reshape x1, local copies, waits for them, and re-layouts, per_device(): coupling = far_coupling.reshape(leaf_local, NF, RANK, RANK)  23.1 us
    dot_general x1, matrix products, per_device(): jnp.einsum('lsab,lsbr->lar', coupling, gathered, preferred_element_type=j...  14 us
    ppermute x7, waiting for transfers between devices, swapped(): return lax.ppermute(block, axis, route)  8.46 us
    unnamed x90, local copies, waits for them, and re-layouts  8.46 us
    ppermute x2, starting transfers between devices, padded(): lax.ppermute(tail, axis, [(i, (i + 1) % count) for i in range(ends)])  7.45 us
  transfers between devices with their start and end apart: 12, of which 5 were waited for; matrix products, arithmetic and copies ran while one was open for 53% of the time, Pallas kernels for 0%

commit v1 on v0

--- a/solution.py
+++ b/solution.py
@@ -1,8 +1,11 @@
+import functools
 import math
 
 import jax
 import jax.numpy as jnp
 from jax import lax
+from jax.experimental import pallas as pl
+from jax.experimental.pallas import tpu as pltpu
 from jax.sharding import PartitionSpec as P
 
 LEAF = 64
@@ -10,6 +13,7 @@
 NF = 16
 NN = 12
 SPAN = 8
+LEAF_DEV = 128
 
 
 variance = 1.0
@@ -45,21 +49,141 @@
     return lax.ppermute(block, axis, route)
 
 
-def matern_block(own_coords, part_coords, own_ids, part_ids, present):
-    width = own_coords.shape[2]
-    squared = jnp.zeros((own_coords.shape[1], width, part_coords.shape[2]), jnp.float32)
-    for component in range(3):
-        delta = own_coords[component][:, :, None] - part_coords[component][:, None, :]
-        squared = squared + delta * delta
-    scaled = decay_rate * jnp.sqrt(squared)
-    kernel = variance * (1.0 + scaled) * jnp.exp(-scaled)
-    column_pos = jnp.arange(part_coords.shape[2], dtype=jnp.int32) % width
-    row_pos = jnp.arange(width, dtype=jnp.int32)
-    same_leaf = jnp.repeat(part_ids == own_ids[:, None], width, axis=1)
-    diagonal = same_leaf[:, None, :] & (column_pos[None, None, :] == row_pos[None, :, None])
-    kernel = kernel + nugget * diagonal.astype(jnp.float32)
-    live = jnp.repeat(present, width, axis=1).astype(jnp.float32)
-    return (kernel * live[:, None, :]).astype(jnp.bfloat16)
+LOG2E = 1.4426950408889634
+LN2 = 0.6931471805599453
+SCALE = decay_rate * LOG2E
+BLK = 256
+BL = BLK // LEAF
+f32 = jnp.float32
+bf16 = jnp.bfloat16
+
+
+def split3(v):
+    a = v.astype(bf16)
+    rest = v - a.astype(f32)
+    b = rest.astype(bf16)
+    c = (rest - b.astype(f32)).astype(bf16)
+    return a.astype(f32), b.astype(f32), c.astype(f32)
+
+
+def features(coords):
+    v = (coords - 0.5) * SCALE
+    parts = [split3(v[c : c + 1]) for c in range(3)]
+    norm = split3(jnp.sum(v * v, axis=0, keepdims=True))
+    one = jnp.ones_like(norm[0])
+    zero = jnp.zeros_like(one)
+    left = []
+    right = []
+    for one_part in parts:
+        a, b, c = one_part
+        left += [a, a, a, b, b, c]
+        right += [-2.0 * a, -2.0 * b, -2.0 * c, -2.0 * a, -2.0 * b, -2.0 * a]
+    left += list(norm) + [one, one, one] + [zero] * 8
+    right += [one, one, one] + list(norm) + [zero] * 8
+    return jnp.concatenate(left, axis=0), jnp.concatenate(right, axis=0)
+
+
+def matern(squared):
+    m = jnp.maximum(squared, 1e-20)
+    t = m * lax.rsqrt(m)
+    return (variance + (variance * LN2) * t) * jnp.exp2(-t)
+
+
+def near_kernel(blocks, coords_ref, points_ref, rel_ref, out_ref, left_ref, right_ref, weight_ref, acc_ref, kern_ref):
+    lanes_iota = lax.broadcasted_iota(jnp.int32, (32, LEAF_DEV), 1)
+    row_iota = lax.broadcasted_iota(jnp.int32, (32, LEAF_DEV), 0)
+    base = (lanes_iota // BL) * BL - SPAN
+    count = jnp.zeros((32, LEAF_DEV), f32)
+    for s in range(NN):
+        count = count + jnp.where(rel_ref[s : s + 1, :] - base == row_iota, 1.0, 0.0)
+    spread = (
+        lax.broadcasted_iota(jnp.int32, (LEAF_DEV, BLK), 0)
+        == lax.broadcasted_iota(jnp.int32, (LEAF_DEV, BLK), 1) // LEAF
+    ).astype(f32).astype(bf16)
+    total = blocks + 4
+    zero_weight = jnp.zeros((32, BLK), f32)
+    for b in (0, 1, total - 2, total - 1):
+        weight_ref[b] = zero_weight
+    for b in range(blocks):
+        shifted = pltpu.roll(count, (LEAF_DEV - BL * b) % LEAF_DEV, 1) if b else count
+        weight_ref[b + 2] = jnp.dot(shifted.astype(bf16), spread, preferred_element_type=f32)
+
+    @pl.loop(0, total)
+    def _(b):
+        left, right = features(coords_ref[:, pl.ds(pl.multiple_of(b * BLK, BLK), BLK)])
+        left_ref[pl.ds(pl.multiple_of(b * BLK, BLK), BLK), :] = jnp.transpose(left).astype(bf16)
+        right_ref[:, pl.ds(pl.multiple_of(b * BLK, BLK), BLK)] = right.astype(bf16)
+        acc_ref[b] = jnp.zeros((16, BLK), f32)
+
+    leaf_of_lane = lax.broadcasted_iota(jnp.int32, (16, BLK), 1) // LEAF
+
+    def expanded(b):
+        x = points_ref[:, pl.ds(pl.multiple_of(b * BLK, BLK), BLK)]
+        zero = jnp.zeros_like(x)
+        return jnp.concatenate([jnp.where(leaf_of_lane == j, x, zero) for j in range(BL)], axis=0)
+
+    diagonal = [
+        lax.broadcasted_iota(jnp.int32, (64, BLK), 0) + 64 * c
+        == lax.broadcasted_iota(jnp.int32, (64, BLK), 1)
+        for c in range(BLK // 64)
+    ]
+
+    @pl.loop(0, total - 2)
+    def _(i):
+        right = right_ref[:, pl.ds(pl.multiple_of(i * BLK, BLK), BLK)]
+        x_i = expanded(i)
+        acc_i = acc_ref[i]
+        for step in range(3):
+            j = i + step
+            for c in range(BLK // 64):
+                left = left_ref[pl.ds(pl.multiple_of(j * BLK, BLK) + 64 * c, 64), :]
+                block = matern(jnp.dot(left, right, preferred_element_type=f32))
+                if step == 0:
+                    block = block + jnp.where(diagonal[c], nugget, 0.0)
+                kern_ref[step, 64 * c : 64 * c + 64, :] = block.astype(bf16)
+        for step in range(3):
+            j = i + step
+            kern = kern_ref[step]
+            x_j = x_i if step == 0 else expanded(j)
+            part = jnp.dot(x_j, kern, preferred_element_type=f32)
+            weight = weight_ref[i]
+            for k in range(BL):
+                row = SPAN + BL * step + k
+                acc_i = acc_i + part[16 * k : 16 * k + 16] * weight[row : row + 1]
+            if step:
+                part = lax.dot_general(x_i, kern, (((1,), (1,)), ((), ())), preferred_element_type=f32)
+                weight = weight_ref[j]
+                acc = acc_ref[j]
+                for k in range(BL):
+                    row = SPAN - BL * step + k
+                    acc = acc + part[16 * k : 16 * k + 16] * weight[row : row + 1]
+                acc_ref[j] = acc
+        acc_ref[i] = acc_i
+
+    @pl.loop(0, blocks)
+    def _(b):
+        out_ref[:, pl.ds(pl.multiple_of(b * BLK, BLK), BLK)] = acc_ref[b + 2]
+
+
+def near_field(ext_coords, ext_points, near_rel):
+    blocks = LEAF_DEV // BL
+    total = blocks + 4
+    vmem = pl.BlockSpec(memory_space=pltpu.VMEM)
+    return pl.pallas_call(
+        functools.partial(near_kernel, blocks),
+        out_shape=jax.ShapeDtypeStruct((16, LEAF_DEV * LEAF), f32),
+        in_specs=[vmem] * 3,
+        out_specs=vmem,
+        scratch_shapes=[
+            pltpu.VMEM((total * BLK, 32), bf16),
+            pltpu.VMEM((32, total * BLK), bf16),
+            pltpu.VMEM((total, 32, BLK), f32),
+            pltpu.VMEM((total, 16, BLK), f32),
+            pltpu.VMEM((3, BLK, BLK), bf16),
+        ],
+        compiler_params=pltpu.CompilerParams(vmem_limit_bytes=48 * 1024 * 1024),
+        cost_estimate=pl.CostEstimate(flops=2_000_000_000, bytes_accessed=2_000_000, transcendentals=13_000_000),
+    )(ext_coords, ext_points, near_rel)
 
 
 def top_start(height, number):
@@ -170,27 +294,9 @@
         "lpk,lkr->rlp", basis_blocks, leaf_field, preferred_element_type=jnp.float32
     )
     far_part = far_part.reshape(rhs_count, leaf_local * LEAF)
-    ext_leaves = leaf_local + 2 * SPAN
-    point_ext = ext_points.reshape(rhs_count, ext_leaves, LEAF)
-    coord_ext = ext_coords.reshape(3, ext_leaves, LEAF)
     first_global = device * leaf_local
-    block_leaves = min(16, leaf_local)
-
-    def near_block(block_num):
-        begin_leaf = block_num * block_leaves
-        own_ids = first_global + begin_leaf + jnp.arange(block_leaves, dtype=jnp.int32)
-        near_partners = lax.dynamic_slice_in_dim(near_list, begin_leaf, block_leaves, 0)
-        near_present = near_partners >= 0
-        clamped = jnp.where(near_present, near_partners, own_ids[:, None])
-        local_ids = clamped - first_global + SPAN
-        own_coords = lax.dynamic_slice_in_dim(coord_ext, begin_leaf + SPAN, block_leaves, 1)
-        part_coords = coord_ext[:, local_ids].reshape(3, block_leaves, NN * LEAF)
-        part_points = point_ext[:, local_ids].reshape(rhs_count, block_leaves, NN * LEAF)
-        kernel = matern_block(own_coords, part_coords, own_ids, clamped, near_present)
-        return jnp.einsum("bpq,rbq->rbp", kernel, part_points, preferred_element_type=jnp.float32)
-
-    near_part = lax.map(near_block, jnp.arange(leaf_local // block_leaves, dtype=jnp.int32))
-    near_part = jnp.transpose(near_part, (1, 0, 2, 3)).reshape(rhs_count, leaf_local * LEAF)
+    near_rel = jnp.transpose(jnp.where(near_list >= 0, near_list - first_global, -1000))
+    near_part = near_field(ext_coords, ext_points, near_rel)
     return near_part + far_part
 
 

time: 254 us -> 220 us (0.87)
  matrix products: 57.7 us -> 29.8 us
  Pallas kernels: 0 us -> 27 us
  local copies, waits for them, and re-layouts: 127 us -> 101 us
  loops' own time: 6.12 us -> 0 us
    dot_general x8 -> x0, matrix products: 28.5 us -> none  [near_block(): jnp.einsum('bpq,rbq->rbp', kernel, part_points, preferred_element_type=jn...]
    pallas_call x0 -> x1, Pallas kernels: none -> 27 us  [near_field(): pl.pallas_call(functools.partial(near_kernel, blocks), out_shape=jax.Shap...]
    gather x24 -> x0, local copies, waits for them, and re-layouts: 13.6 us -> none  [the longest x16 7.32 us: near_block(): part_coords = coord_ext[:, local_ids].reshape(3, block_leaves, NN * LEAF)]
    reshape x19 -> x0, local copies, waits for them, and re-layouts: 7.94 us -> none  [the longest x16 7.04 us: near_block(): point_ext[:, local_ids].reshape(rhs_count, block_leaves, NN * LEAF)]
    dynamic_slice x24 -> x0, local copies, waits for them, and re-layouts: 6.45 us -> none  [the longest x8 5.17 us: per_device(): lax.map(near_block, jnp.arange(leaf_local // block_leaves, dtype=jnp.int32))]
    another operation x1 -> x0, loops' own time: 6.12 us -> none  [per_device(): lax.map(near_block, jnp.arange(leaf_local // block_leaves, dtype=jnp.int32))]
    slice x13 -> x7, local copies, waits for them, and re-layouts: 0.05 us -> 5.65 us  [per_device(): local_transfer[offset:offset + number].reshape(number, RANK, RANK)]
    gather x2, local copies, waits for them, and re-layouts: 31 us -> 35 us  [per_device(): gathered = table[row_index]]
  transfers between devices with their start and end apart: 12 -> 12, of which waited for: 5 -> 5; matrix products, arithmetic and copies ran while one was open for 53% -> 34% of each run, Pallas kernels for 0% -> 12%
where the time goes in v1:
time: 220 us; the launch traced here: 218 us
  local copies, waits for them, and re-layouts  101 us (46%)
  starting transfers between devices  33.8 us (15%)
  matrix products  29.8 us (14%)
  Pallas kernels  27 us (12%)
  between operations  14 us (6%)
  waiting for transfers between devices  8.94 us (4%)
  other arithmetic  3.42 us (2%)
    gather x2, local copies, waits for them, and re-layouts, per_device(): gathered = table[row_index]  35 us
    pallas_call x1, Pallas kernels, near_field(): pl.pallas_call(functools.partial(near_kernel, blocks), out_shape=jax.Shap...  27 us
    ppermute x7, starting transfers between devices, swapped(): return lax.ppermute(block, axis, route)  23.7 us
    reshape x1, local copies, waits for them, and re-layouts, per_device(): coupling = far_coupling.reshape(leaf_local, NF, RANK, RANK)  23.1 us
    dot_general x1, matrix products, per_device(): jnp.einsum('lsab,lsbr->lar', coupling, gathered, preferred_element_type=j...  13.9 us
    unnamed x56, local copies, waits for them, and re-layouts  9.11 us
    ppermute x7, waiting for transfers between devices, swapped(): return lax.ppermute(block, axis, route)  8.89 us
    ppermute x2, starting transfers between devices, padded(): lax.ppermute(tail, axis, [(i, (i + 1) % count) for i in range(ends)])  7.46 us
  transfers between devices with their start and end apart: 12, of which 5 were waited for; matrix products, arithmetic and copies ran while one was open for 34% of the time, Pallas kernels for 12%

profile of v1, /device:TPU:0, one launch (start us, length us, event | category | flops | bytes accessed | tf_op | source)
XLA Modules:
  0.0 217.7 jit_solution(3316409367939462105)
XLA Ops:
  6.5 1.3 copy.53
  7.9 1.7 copy.54
  9.6 1.5 reshape.154
  12.2 0.8 copy.57
  13.0 1.3 fusion.136
  14.3 1.3 collective-permute-start.1
  15.6 3.6 %collective-permute-start = (f32[3,512]{1,0:T(4,128)}, f32[3,512]{1,0:T(4,128)}, u32[]{:S(2)}, u32[]{:S(2)}) collective-permute-start(f32[3,512]{1,0:T(4,128)} %get-tuple-element.29), channel_id=1, source_target_pairs={{0,1},{1,2},{2,3},{3,4},{4,5},{5,6},{6,7},{7,8},{8,9},{9,10},{10,1... | collective-permute-start | bytes 18440 | tf_op jit(solution)/shard_map/ppermute | solution.py:33
  19.3 1.4 fusion.135
  20.6 1.3 collective-permute-start.3
  21.9 3.8 %collective-permute-start.2 = (bf16[16,512]{1,0:T(8,128)(2,1)}, bf16[16,512]{1,0:T(8,128)(2,1)}, u32[]{:S(2)}, u32[]{:S(2)}) collective-permute-start(bf16[16,512]{1,0:T(8,128)(2,1)} %get-tuple-element.27), channel_id=1, source_target_pairs={{0,1},{1,2},{2,3},{3,4},{4,5},{5,6},{6,7},{7,8},{8,9},{9,10},{10,1... | collective-permute-start | bytes 49160 | tf_op jit(solution)/shard_map/ppermute | solution.py:33
  27.9 0.8 slice.205
  28.7 0.8 slice.202
  29.5 0.9 slice.199
  30.4 1.0 slice.196
  34.0 0.8 copy.65
  34.8 0.8 copy.72
  35.7 2.4 %copy.63 = bf16[128,32,32]{2,1,0:T(8,128)(2,1)S(1)} copy(bf16[128,32,32]{0,2,1:T(8,128)(2,1)} %bitcast.172) | data formatting | bytes 524288 | tf_op jit(solution)/shard_map/reshape | solution.py:233
  39.6 1.0 convolution_bitcast_fusion.9
  40.6 0.9 convolution_bitcast_fusion.11
  41.5 0.8 convolution_bitcast_fusion.13
  42.4 1.2 collective-permute-start.4
  43.6 6.7 %copy.59 = bf16[128,16,1024]{0,2,1:T(8,128)(2,1)} copy(bf16[128,16,1024]{2,1,0:T(8,128)(2,1)} %param.13) | data formatting | bytes 8388608 | tf_op args[4]
  50.3 23.1 %copy.61 = bf16[128,16,32,32]{3,2,1,0:T(8,128)(2,1)} copy(bf16[128,16,32,32]{0,3,2,1:T(8,128)(2,1)} %bitcast.166) | data formatting | bytes 8388608 | tf_op jit(solution)/shard_map/reshape | solution.py:225
  74.2 1.0 fusion.109
  77.7 1.1 fusion.111
  88.8 1.6 collective-permute-start.5
  90.4 1.0 pad_maximum_fusion.1.coords_ref
  91.4 1.3 collective-permute-done.5
  92.8 6.6 %collective-permute-start.6 = (f32[3,32,16]{1,2,0:T(8,128)S(1)}, f32[3,32,16]{1,2,0:T(8,128)S(1)}, u32[]{:S(2)}, u32[]{:S(2)}) collective-permute-start(f32[3,32,16]{1,2,0:T(8,128)S(1)} %pad_maximum_fusion.3), channel_id=1, source_target_pairs={{0,4},{4,0},{1,5},{5,1},{2,6},{6,2},{3,7},{7,3},{8,12},{12,8},{9,1... | collective-permute-start | bytes 18440 | tf_op jit(solution)/shard_map/ppermute | solution.py:49
  99.8 0.8 pad_maximum_fusion.points_ref
  100.5 27.0 %shard_map.91 = f32[16,8192]{1,0:T(8,128)S(1)} custom-call(f32[3,9216]{1,0:T(4,128)S(1)} %pad_maximum_fusion.1.coords_ref, bf16[16,9216]{1,0:T(8,128)(2,1)S(1)} %pad_maximum_fusion.points_ref, s32[12,128]{1,0:T(8,128)S(1)} %select_bitcast_fusion.rel_ref), custom_call_target="tpu_custom_call" | custom-call | flops 2000000000 | bytes 2000000 | tf_op jit(solution)/shard_map/pallas_call | solution.py:172
  127.8 2.0 collective-permute-start.7
  130.0 1.7 collective-permute-done.7
  131.8 7.8 %collective-permute-start.8 = (f32[3,32,16]{1,2,0:T(8,128)S(1)}, f32[3,32,16]{1,2,0:T(8,128)S(1)}, u32[]{:S(2)}, u32[]{:S(2)}) collective-permute-start(f32[3,32,16]{1,2,0:T(8,128)S(1)} %pad_maximum_fusion.5), channel_id=1, source_target_pairs={{0,16},{16,0},{1,17},{17,1},{2,18},{18,2},{3,19},{19,3},{4,20},{20... | collective-permute-start | bytes 18440 | tf_op jit(solution)/shard_map/ppermute | solution.py:49
  139.8 1.6 collective-permute-done.8
  141.5 1.6 collective-permute-start.9
  143.3 2.2 collective-permute-done.9
  145.5 3.0 %collective-permute-start.10 = (f32[3,32,16]{1,2,0:T(8,128)S(1)}, f32[3,32,16]{1,2,0:T(8,128)S(1)}, u32[]{:S(2)}, u32[]{:S(2)}) collective-permute-start(f32[3,32,16]{1,2,0:T(8,128)S(1)} %pad_maximum_fusion.7), channel_id=1, source_target_pairs={{0,64},{64,0},{1,65},{65,1},{2,66},{66,2},{3,67},{67,3},{4,68},{68... | collective-permute-start | bytes 18440 | tf_op jit(solution)/shard_map/ppermute | solution.py:49
  148.6 2.2 %collective-permute-done.10 = f32[3,32,16]{1,2,0:T(8,128)S(1)} collective-permute-done((f32[3,32,16]{1,2,0:T(8,128)S(1)}, f32[3,32,16]{1,2,0:T(8,128)S(1)}, u32[]{:S(2)}, u32[]{:S(2)}) %collective-permute-start.10) | collective-permute-done | bytes 6176 | tf_op jit(solution)/shard_map/ppermute | solution.py:49
  152.5 0.9 convolution_bitcast_fusion.12
  153.4 0.9 convolution_bitcast_fusion.10
  154.3 1.0 convolution_bitcast_fusion.8
  156.3 1.7 convolution_bitcast_fusion.2
  158.1 17.1 %gather_fusion = bf16[2048,512]{1,0:T(8,128)(2,1)} fusion(bf16[16384,512]{1,0:T(8,128)(2,1)} %all-gather.2.cloned.1.call-done, s32[2048]{0:T(1024)S(1)} %broadcast_clamp_fusion), kind=kCustom, calls=%fused_computation | custom fusion | bytes 4202496 | tf_op jit(solution)/shard_map/gather | solution.py:222
  175.2 17.9 %gather.6 = bf16[128,16,32,16]{3,2,1,0:T(8,128)(2,1)} reshape(bf16[2048,512]{1,0:T(8,128)(2,1)} %gather_fusion) | data formatting | bytes 4194304 | tf_op jit(solution)/shard_map/gather | solution.py:222
  193.1 13.9 %fusion.4 = f32[128,16,32]{2,1,0:T(8,128)S(1)} fusion(bf16[128,16,32,32]{3,2,1,0:T(8,128)(2,1)} %copy.61, bf16[128,16,32,16]{3,2,1,0:T(8,128)(2,1)} %gather.6, pred[128,16]{1,0:T(8,128)(4,1)S(1)} %copy-done.25), kind=kOutput, calls=%fused_computation.5 | convolution fusion | flops 68157440 | bytes 6555648 | tf_op jit(solution)/shard_map/lsab,lsbr->lar/dot_general | solution.py:226
  207.1 1.8 fusion.7
  210.0 0.8 add.272
  (158 shorter events, 26.2 us)
Async XLA Ops:
  6.5 151.5 %all-gather.2.cloned.1.call-start = ((), (), s32[]{:S(2)}) async-start(), calls=%async_computation | async-start | bytes 16908288 | tf_op jit(solution)/shard_map/all_gather | solution.py:220
  14.3 76.0 %collective-permute-start.1 = (f32[3,512]{1,0:T(4,128)}, f32[3,512]{1,0:T(4,128)}, u32[]{:S(2)}, u32[]{:S(2)}) collective-permute-start(f32[3,512]{1,0:T(4,128)} %get-tuple-element.30), channel_id=1, source_target_pairs={{1,0},{2,1},{3,2},{4,3},{5,4},{6,5},{7,6},{8,7},{9,8},{10,9},{11,1... | collective-permute-start | bytes 18440 | tf_op jit(solution)/shard_map/ppermute | solution.py:35
  15.6 74.7 %collective-permute-start = (f32[3,512]{1,0:T(4,128)}, f32[3,512]{1,0:T(4,128)}, u32[]{:S(2)}, u32[]{:S(2)}) collective-permute-start(f32[3,512]{1,0:T(4,128)} %get-tuple-element.29), channel_id=1, source_target_pairs={{0,1},{1,2},{2,3},{3,4},{4,5},{5,6},{6,7},{7,8},{8,9},{9,10},{10,1... | collective-permute-start | bytes 18440 | tf_op jit(solution)/shard_map/ppermute | solution.py:33
  20.6 79.1 %collective-permute-start.3 = (bf16[16,512]{1,0:T(8,128)(2,1)}, bf16[16,512]{1,0:T(8,128)(2,1)}, u32[]{:S(2)}, u32[]{:S(2)}) collective-permute-start(bf16[16,512]{1,0:T(8,128)(2,1)} %get-tuple-element.28), channel_id=1, source_target_pairs={{1,0},{2,1},{3,2},{4,3},{5,4},{6,5},{7,6},{8,7},{9,8},{10,9},{11,1... | collective-permute-start | bytes 49160 | tf_op jit(solution)/shard_map/ppermute | solution.py:35
  21.9 77.8 %collective-permute-start.2 = (bf16[16,512]{1,0:T(8,128)(2,1)}, bf16[16,512]{1,0:T(8,128)(2,1)}, u32[]{:S(2)}, u32[]{:S(2)}) collective-permute-start(bf16[16,512]{1,0:T(8,128)(2,1)} %get-tuple-element.27), channel_id=1, source_target_pairs={{0,1},{1,2},{2,3},{3,4},{4,5},{5,6},{6,7},{7,8},{8,9},{9,10},{10,1... | collective-permute-start | bytes 49160 | tf_op jit(solution)/shard_map/ppermute | solution.py:33
  38.4 34.9 %copy-start.15 = (s32[128,16]{0,1:T(8,128)S(1)}, s32[128,16]{0,1:T(8,128)}, u32[]{:S(2)}) copy-start(s32[128,16]{0,1:T(8,128)} %param.12) | copy-start | bytes 24580
  38.5 61.3 %copy-start.1 = (bf16[16,8192]{1,0:T(8,128)(2,1)S(1)}, bf16[16,8192]{1,0:T(8,128)(2,1)}, u32[]{:S(2)}) copy-start(bf16[16,8192]{1,0:T(8,128)(2,1)} %param.9) | copy-start | bytes 786436
  42.4 46.2 %collective-permute-start.4 = (f32[3,32,16]{1,2,0:T(8,128)S(1)}, f32[3,32,16]{1,2,0:T(8,128)S(1)}, u32[]{:S(2)}, u32[]{:S(2)}) collective-permute-start(f32[3,32,16]{1,2,0:T(8,128)S(1)} %stack.42), channel_id=1, source_target_pairs={{0,1},{1,0},{2,3},{3,2},{4,5},{5,4},{6,7},{7,6},{8,9},{9,8},{10,11... | collective-permute-start | bytes 18440 | tf_op jit(solution)/shard_map/ppermute | solution.py:49
  75.3 13.3 %copy-start.2 = (bf16[32,32]{1,0:T(8,128)(2,1)}, bf16[32,32]{1,0:T(8,128)(2,1)S(1)}, u32[]{:S(2)}) copy-start(bf16[32,32]{1,0:T(8,128)(2,1)S(1)} %reshape.157) | copy-start | bytes 6148
  75.4 24.3 %copy-start.4 = (bf16[32,32]{1,0:T(8,128)(2,1)}, bf16[32,32]{1,0:T(8,128)(2,1)S(1)}, u32[]{:S(2)}) copy-start(bf16[32,32]{1,0:T(8,128)(2,1)S(1)} %reshape.166) | copy-start | bytes 6148
  75.5 24.2 %copy-start.6 = (bf16[32,32]{1,0:T(8,128)(2,1)}, bf16[32,32]{1,0:T(8,128)(2,1)S(1)}, u32[]{:S(2)}) copy-start(bf16[32,32]{1,0:T(8,128)(2,1)S(1)} %reshape.168) | copy-start | bytes 6148
  88.5 39.1 %copy-start.24 = (bf16[32,32]{1,0:T(8,128)(2,1)S(1)}, bf16[32,32]{1,0:T(8,128)(2,1)}, u32[]{:S(2)}) copy-start(bf16[32,32]{1,0:T(8,128)(2,1)} %reshape.169) | copy-start | bytes 6148
  88.5 41.3 %copy-start.8 = (bf16[32,32]{1,0:T(8,128)(2,1)S(1)}, bf16[32,32]{1,0:T(8,128)(2,1)}, u32[]{:S(2)}) copy-start(bf16[32,32]{1,0:T(8,128)(2,1)} %reshape.170) | copy-start | bytes 6148
  88.5 41.4 %copy-start.14 = (bf16[32,32]{1,0:T(8,128)(2,1)S(1)}, bf16[32,32]{1,0:T(8,128)(2,1)}, u32[]{:S(2)}) copy-start(bf16[32,32]{1,0:T(8,128)(2,1)} %squeeze.107) | copy-start | bytes 6148
  88.5 43.2 %copy-start.23 = (bf16[32,32]{1,0:T(8,128)(2,1)S(1)}, bf16[32,32]{1,0:T(8,128)(2,1)}, u32[]{:S(2)}) copy-start(bf16[32,32]{1,0:T(8,128)(2,1)} %reshape.171) | copy-start | bytes 6148
  88.5 51.1 %copy-start.9 = (bf16[32,32]{1,0:T(8,128)(2,1)S(1)}, bf16[32,32]{1,0:T(8,128)(2,1)}, u32[]{:S(2)}) copy-start(bf16[32,32]{1,0:T(8,128)(2,1)} %reshape.172) | copy-start | bytes 6148
  88.5 51.2 %copy-start.13 = (bf16[32,32]{1,0:T(8,128)(2,1)S(1)}, bf16[32,32]{1,0:T(8,128)(2,1)}, u32[]{:S(2)}) copy-start(bf16[32,32]{1,0:T(8,128)(2,1)} %squeeze.110) | copy-start | bytes 6148
  88.5 52.9 %copy-start.21 = (bf16[32,32]{1,0:T(8,128)(2,1)S(1)}, bf16[32,32]{1,0:T(8,128)(2,1)}, u32[]{:S(2)}) copy-start(bf16[32,32]{1,0:T(8,128)(2,1)} %reshape.173) | copy-start | bytes 6148
  88.5 54.6 %copy-start.12 = (bf16[32,32]{1,0:T(8,128)(2,1)S(1)}, bf16[32,32]{1,0:T(8,128)(2,1)}, u32[]{:S(2)}) copy-start(bf16[32,32]{1,0:T(8,128)(2,1)} %squeeze.113) | copy-start | bytes 6148
  88.5 60.0 %copy-start.11 = (bf16[32,32]{1,0:T(8,128)(2,1)S(1)}, bf16[32,32]{1,0:T(8,128)(2,1)}, u32[]{:S(2)}) copy-start(bf16[32,32]{1,0:T(8,128)(2,1)} %squeeze.116) | copy-start | bytes 6148
  88.5 62.3 %copy-start.10 = (bf16[32,32]{1,0:T(8,128)(2,1)S(1)}, bf16[32,32]{1,0:T(8,128)(2,1)}, u32[]{:S(2)}) copy-start(bf16[32,32]{1,0:T(8,128)(2,1)} %squeeze.118) | copy-start | bytes 6148
  88.5 62.4 %copy-start.16 = (bf16[32,32]{1,0:T(8,128)(2,1)S(1)}, bf16[32,32]{1,0:T(8,128)(2,1)}, u32[]{:S(2)}) copy-start(bf16[32,32]{1,0:T(8,128)(2,1)} %squeeze.117) | copy-start | bytes 6148
  88.5 62.7 %copy-start.17 = (bf16[32,32]{1,0:T(8,128)(2,1)S(1)}, bf16[32,32]{1,0:T(8,128)(2,1)}, u32[]{:S(2)}) copy-start(bf16[32,32]{1,0:T(8,128)(2,1)} %squeeze.114) | copy-start | bytes 6148
  88.6 63.0 %copy-start.18 = (bf16[32,32]{1,0:T(8,128)(2,1)S(1)}, bf16[32,32]{1,0:T(8,128)(2,1)}, u32[]{:S(2)}) copy-start(bf16[32,32]{1,0:T(8,128)(2,1)} %squeeze.111) | copy-start | bytes 6148
  88.6 63.2 %copy-start.19 = (bf16[32,32]{1,0:T(8,128)(2,1)S(1)}, bf16[32,32]{1,0:T(8,128)(2,1)}, u32[]{:S(2)}) copy-start(bf16[32,32]{1,0:T(8,128)(2,1)} %squeeze.108) | copy-start | bytes 6148
  88.6 63.5 %copy-start.20 = (bf16[32,32]{1,0:T(8,128)(2,1)S(1)}, bf16[32,32]{1,0:T(8,128)(2,1)}, u32[]{:S(2)}) copy-start(bf16[32,32]{1,0:T(8,128)(2,1)} %squeeze.105) | copy-start | bytes 6148
  88.6 63.8 %copy-start.22 = (bf16[32,32]{1,0:T(8,128)(2,1)S(1)}, bf16[32,32]{1,0:T(8,128)(2,1)}, u32[]{:S(2)}) copy-start(bf16[32,32]{1,0:T(8,128)(2,1)} %squeeze.101) | copy-start | bytes 6148
  88.6 63.6 %copy-start.3 = (bf16[32,32]{1,0:T(8,128)(2,1)S(1)}, bf16[32,32]{1,0:T(8,128)(2,1)}, u32[]{:S(2)}) copy-start(bf16[32,32]{1,0:T(8,128)(2,1)} %copy-done.2) | copy-start | bytes 6148
  88.8 3.9 %collective-permute-start.5 = (f32[3,32,16]{1,2,0:T(8,128)S(1)}, f32[3,32,16]{1,2,0:T(8,128)S(1)}, u32[]{:S(2)}, u32[]{:S(2)}) collective-permute-start(f32[3,32,16]{1,2,0:T(8,128)S(1)} %pad_maximum_fusion.2), channel_id=1, source_target_pairs={{0,2},{2,0},{1,3},{3,1},{4,6},{6,4},{5,7},{7,5},{8,10},{10,8},{9,1... | collective-permute-start | bytes 18440 | tf_op jit(solution)/shard_map/ppermute | solution.py:49
  92.8 34.7 %collective-permute-start.6 = (f32[3,32,16]{1,2,0:T(8,128)S(1)}, f32[3,32,16]{1,2,0:T(8,128)S(1)}, u32[]{:S(2)}, u32[]{:S(2)}) collective-permute-start(f32[3,32,16]{1,2,0:T(8,128)S(1)} %pad_maximum_fusion.3), channel_id=1, source_target_pairs={{0,4},{4,0},{1,5},{5,1},{2,6},{6,2},{3,7},{7,3},{8,12},{12,8},{9,1... | collective-permute-start | bytes 18440 | tf_op jit(solution)/shard_map/ppermute | solution.py:49
  100.5 51.1 %copy-start.7 = (bf16[32,32]{1,0:T(8,128)(2,1)S(1)}, bf16[32,32]{1,0:T(8,128)(2,1)}, u32[]{:S(2)}) copy-start(bf16[32,32]{1,0:T(8,128)(2,1)} %copy-done.6) | copy-start | bytes 6148
  100.5 51.4 %copy-start.5 = (bf16[32,32]{1,0:T(8,128)(2,1)S(1)}, bf16[32,32]{1,0:T(8,128)(2,1)}, u32[]{:S(2)}) copy-start(bf16[32,32]{1,0:T(8,128)(2,1)} %copy-done.4) | copy-start | bytes 6148
  127.8 3.9 %collective-permute-start.7 = (f32[3,32,16]{1,2,0:T(8,128)S(1)}, f32[3,32,16]{1,2,0:T(8,128)S(1)}, u32[]{:S(2)}, u32[]{:S(2)}) collective-permute-start(f32[3,32,16]{1,2,0:T(8,128)S(1)} %pad_maximum_fusion.4), channel_id=1, source_target_pairs={{0,8},{8,0},{1,9},{9,1},{2,10},{10,2},{3,11},{11,3},{4,12},{12,4},... | collective-permute-start | bytes 18440 | tf_op jit(solution)/shard_map/ppermute | solution.py:49
  131.8 9.6 %collective-permute-start.8 = (f32[3,32,16]{1,2,0:T(8,128)S(1)}, f32[3,32,16]{1,2,0:T(8,128)S(1)}, u32[]{:S(2)}, u32[]{:S(2)}) collective-permute-start(f32[3,32,16]{1,2,0:T(8,128)S(1)} %pad_maximum_fusion.5), channel_id=1, source_target_pairs={{0,16},{16,0},{1,17},{17,1},{2,18},{18,2},{3,19},{19,3},{4,20},{20... | collective-permute-start | bytes 18440 | tf_op jit(solution)/shard_map/ppermute | solution.py:49
  141.5 3.9 %collective-permute-start.9 = (f32[3,32,16]{1,2,0:T(8,128)S(1)}, f32[3,32,16]{1,2,0:T(8,128)S(1)}, u32[]{:S(2)}, u32[]{:S(2)}) collective-permute-start(f32[3,32,16]{1,2,0:T(8,128)S(1)} %pad_maximum_fusion.6), channel_id=1, source_target_pairs={{0,32},{32,0},{1,33},{33,1},{2,34},{34,2},{3,35},{35,3},{4,36},{36... | collective-permute-start | bytes 18440 | tf_op jit(solution)/shard_map/ppermute | solution.py:49
  145.5 5.3 %collective-permute-start.10 = (f32[3,32,16]{1,2,0:T(8,128)S(1)}, f32[3,32,16]{1,2,0:T(8,128)S(1)}, u32[]{:S(2)}, u32[]{:S(2)}) collective-permute-start(f32[3,32,16]{1,2,0:T(8,128)S(1)} %pad_maximum_fusion.7), channel_id=1, source_target_pairs={{0,64},{64,0},{1,65},{65,1},{2,66},{66,2},{3,67},{67,3},{4,68},{68... | collective-permute-start | bytes 18440 | tf_op jit(solution)/shard_map/ppermute | solution.py:49
  158.0 35.0 %copy-start.25 = (pred[128,16]{1,0:T(8,128)(4,1)S(1)}, pred[128,16]{1,0:T(8,128)(4,1)}, u32[]{:S(2)}) copy-start(pred[128,16]{1,0:T(8,128)(4,1)} %copy.52) | copy-start | bytes 6148
  193.1 13.9 %copy-start = (f32[64,32,16]{1,2,0:T(8,128)S(1)}, f32[64,32,16]{1,2,0:T(8,128)}, u32[]{:S(2)}) copy-start(f32[64,32,16]{1,2,0:T(8,128)} %convolution_bitcast_fusion.2) | copy-start | bytes 393220
Sparse Core Ops, SparseCore 0:
  13.1 82.7 all-gather.1

commit v2 on v1

--- a/solution.py
+++ b/solution.py
@@ -14,6 +14,7 @@
 NN = 12
 SPAN = 8
 LEAF_DEV = 128
+N_DEV = 128
 
 
 variance = 1.0
@@ -37,16 +38,6 @@
             axis=dim,
         )
     return cells
-
-
-def swapped(block, axis, apart):
-    count = lax.axis_size(axis)
-    route = []
-    for low in range(count):
-        high = low | 1 << apart
-        if high != low and high < count:
-            route += [(low, high), (high, low)]
-    return lax.ppermute(block, axis, route)
 
 
 LOG2E = 1.4426950408889634
@@ -186,6 +177,356 @@
     )(ext_coords, ext_points, near_rel)
 
 
+TABLE = LEAF_DEV * RANK
+STATE = 256
+WIDTH = TABLE + STATE
+GROUPS = LEAF_DEV // 8
+UPPER = 17
+PARTNERS = (1, 2, 6, 8, 24, 32, 96)
+
+
+def iota(shape, dim):
+    return lax.broadcasted_iota(jnp.int32, shape, dim)
+
+
+def where_eq(a, b):
+    return jnp.where(a == b, 1.0, 0.0).astype(bf16)
+
+
+def dot(a, b):
+    return jnp.dot(a, b, preferred_element_type=f32)
+
+
+def dot_nt(a, b):
+    return lax.dot_general(a, b, (((1,), (1,)), ((), ())), preferred_element_type=f32)
+
+
+def halves(v):
+    high = v.astype(bf16)
+    low = (v - high.astype(f32)).astype(bf16)
+    return jnp.concatenate([high, low], axis=0)
+
+
+def joined(v):
+    rows = v.shape[0] // 2
+    return v[:rows] + v[rows:]
+
+
+def pack_state(first, second, third):
+    parts = []
+    for v in (first, second, third):
+        high = v.astype(bf16).astype(f32)
+        parts += [high, v - high]
+    left = parts[0] + pltpu.roll(parts[1], 32, 1) + pltpu.roll(parts[2], 64, 1) + pltpu.roll(parts[3], 96, 1)
+    right = parts[4] + pltpu.roll(parts[5], 32, 1)
+    return jnp.concatenate([left, right], axis=1).astype(bf16)
+
+
+def unpack_state(state):
+    lanes = iota((16, 128), 1)
+    left = state[:, :128].astype(f32)
+    right = state[:, 128:].astype(f32)
+    pair_left = left + pltpu.roll(left, 96, 1)
+    pair_right = right + pltpu.roll(right, 96, 1)
+    keep = lanes < RANK
+    return (
+        jnp.where(keep, pair_left, 0.0),
+        jnp.where(keep, pltpu.roll(pair_left, 64, 1), 0.0),
+        jnp.where(keep, pair_right, 0.0),
+    )
+
+
+def up_kernel(points_ref, basis_ref, local_ref, pair_ref, couple_ref, payload_ref, ub_ref, bd_ref, bdup_ref, em_ref, sm_ref, rep_ref, x_ref, c_ref, y_ref):
+    step = pl.program_id(0)
+    lanes = iota((8, 256), 1) % 8
+    rows = iota((8, 256), 0)
+
+    @pl.when(step == 0)
+    def _():
+        rep_ref[...] = where_eq(iota((128, 1024), 0), iota((128, 1024), 1) // 8)
+        column = iota((512, 512), 1)
+        perm = where_eq(iota((512, 512), 0), (column % 8) * LEAF + column // 8)
+        stacked = jnp.concatenate([points_ref[:, 512 * g : 512 * g + 512] for g in range(GROUPS)], axis=0)
+        x_ref[...] = dot(stacked, perm).astype(bf16)
+        fold_row = iota((1024, 128), 0) % RANK
+        fold_col = iota((1024, 128), 1)
+        fold_first = where_eq(fold_row, fold_col)
+        fold_second = where_eq(fold_row + RANK, fold_col)
+        own = iota((RANK, 1024), 1) // RANK == iota((RANK, 1024), 0)
+        pairs = pair_ref[...].astype(f32)
+        couples = couple_ref[...].astype(f32)
+
+        def opened(values, k):
+            return jnp.where(own, values[k : k + 1, :], 0.0).astype(bf16)
+
+        em_ref[...] = dot(jnp.concatenate([opened(pairs, k) for k in range(10)], axis=0), fold_first).astype(bf16)
+        sm_ref[...] = (
+            dot(jnp.concatenate([opened(couples, 2 * k) for k in range(6)], axis=0), fold_first)
+            + dot(jnp.concatenate([opened(couples, 2 * k + 1) for k in range(6)], axis=0), fold_second)
+        ).astype(bf16)
+
+    basis = basis_ref[...]
+    wide = dot(jnp.concatenate([basis[:, 128 * k : 128 * k + 128] for k in range(16)], axis=0), rep_ref[...])
+    keep = lanes == rows
+    for e in range(2):
+        for p in range(0, LEAF, 2):
+            both = []
+            for q in (p, p + 1):
+                k, low = q // 4, q % 4
+                both.append(jnp.where(keep, wide[16 * k + 8 * e : 16 * k + 8 * e + 8, 256 * low : 256 * low + 256], 0.0))
+            ub_ref[e, 8 * p : 8 * p + 16, :] = jnp.concatenate(both, axis=0).astype(bf16)
+    local = local_ref[pl.ds(pl.multiple_of(16 * step, 16), 16), :]
+    wide = dot(jnp.concatenate([local[:, 128 * k : 128 * k + 128] for k in range(8)], axis=0), rep_ref[...])
+    total = jnp.zeros((16, 256), f32)
+    for e in range(2):
+        keep = lanes == rows // 2 + 4 * e
+        for a in range(0, RANK, 2):
+            both = []
+            for q in (a, a + 1):
+                k, low = q // 4, q % 4
+                both.append(jnp.where(keep, wide[16 * k + 8 * e : 16 * k + 8 * e + 8, 256 * low : 256 * low + 256], 0.0))
+            bd_ref[e, 8 * a : 8 * a + 16, :] = jnp.concatenate(both, axis=0).astype(bf16)
+        own = x_ref[pl.ds(pl.multiple_of(32 * step + 16 * e, 16), 16), :]
+        coeff = dot(own, ub_ref[e]).astype(bf16)
+        payload_ref[:, pl.ds(pl.multiple_of(512 * step + 256 * e, 256), 256)] = coeff
+        total = total + dot(coeff, bd_ref[e])
+    c_ref[pl.ds(pl.multiple_of(16 * step, 16), 16), :] = total
+
+    @pl.when(step == GROUPS // 2 - 1)
+    def _():
+        for k in range(8):
+            y_ref[k, 0:126, :] = dot(local_ref[128:254, 128 * k : 128 * k + 128], rep_ref[...])
+        tile = 0
+        for level_tiles in (8, 4, 2, 1):
+            for q in range(level_tiles):
+                fill_upper(y_ref, bdup_ref, tile, tile, lanes == rows // 2 + 4 * (q % 2))
+                tile += 1
+        fill_upper(y_ref, bdup_ref, 15, 15, (lanes == rows // 2 + 4) & (rows < 4))
+        fill_upper(y_ref, bdup_ref, 16, 15, (lanes == 0) & (rows >= 4) & (rows < 6))
+        current = [c_ref[16 * q : 16 * q + 16, :] for q in range(8)]
+        tile = 0
+        for level_tiles in (8, 4, 2, 1, 1, 1):
+            parts = [joined(dot(halves(current[q]), bdup_ref[tile + q])) for q in range(level_tiles)]
+            tile += level_tiles
+            if level_tiles > 1:
+                current = [parts[2 * q] + parts[2 * q + 1] for q in range(level_tiles // 2)]
+            else:
+                current = parts
+        squeeze = where_eq(iota((256, 128), 0), iota((256, 128), 1) * 8)
+        mine = joined(dot(halves(current[0]), squeeze))
+        zero = jnp.zeros_like(mine)
+        payload_ref[:, TABLE:] = pack_state(mine, zero, zero)
+
+
+def fill_upper(y_ref, bdup_ref, target, tile, keep):
+    for a in range(0, RANK, 2):
+        both = []
+        for q in (a, a + 1):
+            k, low = q // 4, q % 4
+            both.append(jnp.where(keep, y_ref[k, 8 * tile : 8 * tile + 8, 256 * low : 256 * low + 256], 0.0))
+        bdup_ref[target, 8 * a : 8 * a + 16, :] = jnp.concatenate(both, axis=0).astype(bf16)
+
+
+def upward(points, basis, local_transfer, pairs, couples):
+    full = lambda *shape: pl.BlockSpec(shape, lambda i: (0,) * len(shape))
+    return pl.pallas_call(
+        up_kernel,
+        grid=(GROUPS // 2,),
+        out_shape=(
+            jax.ShapeDtypeStruct((16, WIDTH), bf16),
+            jax.ShapeDtypeStruct((GROUPS, 512, 256), bf16),
+            jax.ShapeDtypeStruct((GROUPS, 256, 256), bf16),
+            jax.ShapeDtypeStruct((UPPER, 256, 256), bf16),
+            jax.ShapeDtypeStruct((320, 128), bf16),
+            jax.ShapeDtypeStruct((192, 128), bf16),
+        ),
+        in_specs=[
+            full(16, LEAF_DEV * LEAF),
+            pl.BlockSpec((16, LEAF * RANK), lambda i: (i, 0)),
+            full(254, 1024),
+            full(10, 1024),
+            full(12, 1024),
+        ],
+        out_specs=(
+            full(16, WIDTH),
+            pl.BlockSpec((2, 512, 256), lambda i: (i, 0, 0)),
+            pl.BlockSpec((2, 256, 256), lambda i: (i, 0, 0)),
+            full(UPPER, 256, 256),
+            full(320, 128),
+            full(192, 128),
+        ),
+        scratch_shapes=[
+            pltpu.VMEM((128, 1024), bf16),
+            pltpu.VMEM((256, 512), bf16),
+            pltpu.VMEM((128, 256), f32),
+            pltpu.VMEM((8, 128, 1024), f32),
+        ],
+        compiler_params=pltpu.CompilerParams(vmem_limit_bytes=48 * 1024 * 1024),
+        cost_estimate=pl.CostEstimate(flops=1_000_000_000, bytes_accessed=10_000_000, transcendentals=0),
+    )(points, basis, local_transfer, pairs, couples)
+
+
+def step_kernel(height, bits_ref, first_ref, payload_ref, received_ref, em_ref, next_ref):
+    forward = height % 2 == 1
+    next_ref[:, :TABLE] = received_ref[:, :TABLE] if forward else first_ref[:, :TABLE]
+    mine, _, _ = unpack_state(payload_ref[:, TABLE:])
+    sibling, _, _ = unpack_state(received_ref[:, TABLE:])
+    if height <= 4:
+        first = bits_ref[height] == 0
+        left = jnp.where(first, mine, sibling)
+        right = jnp.where(first, sibling, mine)
+        both = (left + pltpu.roll(right, 32, 1))[:, : 2 * RANK]
+        parent = joined(dot(halves(both), em_ref[64 * height : 64 * height + 64, :]))
+    else:
+        parent = jnp.zeros_like(mine)
+    next_ref[:, TABLE:] = pack_state(parent, mine, sibling)
+
+
+def tree_step(height, bits, first, payload, received, em):
+    vmem = pl.BlockSpec(memory_space=pltpu.VMEM)
+    return pl.pallas_call(
+        functools.partial(step_kernel, height),
+        out_shape=jax.ShapeDtypeStruct((16, WIDTH), bf16),
+        in_specs=[pl.BlockSpec(memory_space=pltpu.SMEM)] + [vmem] * 4,
+        out_specs=vmem,
+        cost_estimate=pl.CostEstimate(flops=1_000_000, bytes_accessed=400_000, transcendentals=0),
+    )(bits, first, payload, received, em)
+
+
+def regroup_kernel(c_ref, out_ref, x_ref):
+    flat = c_ref[...].astype(f32).reshape(128, 1024)
+    for k in range(8):
+        x_ref[k] = flat[:, 128 * k : 128 * k + 128]
+    lanes = iota((8, 128), 1)
+    low_half = lanes < 64
+    even = (lanes // RANK) % 2 == 0
+    for s_high in range(4):
+        for a_high in range(8):
+            v = [
+                x_ref[a_high, pl.ds(4 * s_high + k, 8, stride=NF), :]
+                for k in range(4)
+            ]
+            u0 = jnp.where(low_half, v[0], pltpu.roll(v[2], 64, 1))
+            u2 = jnp.where(low_half, pltpu.roll(v[0], 64, 1), v[2])
+            u1 = jnp.where(low_half, v[1], pltpu.roll(v[3], 64, 1))
+            u3 = jnp.where(low_half, pltpu.roll(v[1], 64, 1), v[3])
+            w = []
+            for p, q in ((u0, u1), (u2, u3)):
+                w.append(jnp.where(even, p, pltpu.roll(q, 32, 1)))
+                w.append(jnp.where(even, pltpu.roll(p, 96, 1), q))
+            lane = 128 * s_high
+            row = 32 * a_high
+            out_ref[0, row : row + 16, lane : lane + 128] = jnp.concatenate(w[:2], axis=0).astype(bf16)
+            out_ref[0, row + 16 : row + 32, lane : lane + 128] = jnp.concatenate(w[2:], axis=0).astype(bf16)
+
+
+def regroup(far_coupling):
+    return pl.pallas_call(
+        regroup_kernel,
+        grid=(GROUPS,),
+        out_shape=jax.ShapeDtypeStruct((GROUPS, 256, 512), bf16),
+        in_specs=[pl.BlockSpec((8, NF, 1024), lambda i: (i, 0, 0))],
+        out_specs=pl.BlockSpec((1, 256, 512), lambda i: (i, 0, 0)),
+        scratch_shapes=[pltpu.VMEM((8, 128, 128), f32)],
+        compiler_params=pltpu.CompilerParams(vmem_limit_bytes=32 * 1024 * 1024),
+        cost_estimate=pl.CostEstimate(flops=30_000_000, bytes_accessed=8_400_000, transcendentals=0),
+    )(far_coupling)
+
+
+def down_kernel(bits_ref, index_ref, payload_ref, *refs):
+    received = refs[:7]
+    em_ref, sm_ref, bdup_ref, d_ref, ub_ref, bd_ref, near_ref, out_ref, table_ref, field_ref, far_ref, gather_ref = refs[7:]
+    step = pl.program_id(0)
+
+    @pl.when(step == 0)
+    def _():
+        column = iota((256, 1024), 1)
+        repeat = where_eq(iota((256, 1024), 0), (column % RANK) * 8 + column // 128)
+        for k, ref in enumerate((payload_ref,) + received):
+            stacked = jnp.concatenate([ref[:, 256 * g : 256 * g + 256] for g in range(GROUPS)], axis=0)
+            wide = dot(stacked, repeat).astype(bf16)
+            for m in range(8):
+                table_ref[2048 * k + 256 * m : 2048 * k + 256 * m + 256, :] = wide[:, 128 * m : 128 * m + 128]
+        table_ref[16384:16400, :] = jnp.zeros((16, 128), bf16)
+        terms = []
+        for height in range(1, 7):
+            _, before_mine, before_sibling = unpack_state(received[height][:, TABLE:])
+            plain = (bits_ref[height - 1] == 0) == (height % 2 == 1)
+            left = jnp.where(plain, before_mine, before_sibling)
+            right = jnp.where(plain, before_sibling, before_mine)
+            both = left + pltpu.roll(right, 32, 1)
+            terms.append(joined(dot_nt(halves(both), sm_ref[32 * height - 32 : 32 * height, :])))
+        field = terms[5]
+        for height in range(5, 0, -1):
+            row = pl.multiple_of(64 * (height - 1) + 32 * bits_ref[height - 1], 32)
+            matrix = em_ref[pl.ds(row, 32), 0:RANK]
+            field = terms[height - 1] + joined(dot_nt(halves(field), matrix))
+        stretch = where_eq(iota((RANK, 256), 0) * 8, iota((RANK, 256), 1))
+        fields = [joined(dot(halves(field), stretch))]
+        tile = UPPER
+        for level_tiles in (1, 1, 1, 2, 4, 8):
+            tile -= level_tiles
+            fields = [
+                joined(dot_nt(halves(fields[q // 2 if level_tiles > 1 else 0]), bdup_ref[tile + q]))
+                for q in range(level_tiles)
+            ]
+        for q in range(8):
+            field_ref[32 * q : 32 * q + 32, :] = halves(fields[q])
+
+    block = iota((16, 128), 1) // RANK
+    for leaf in range(8):
+        for s_high in range(4):
+            merged = None
+            for low in range(4):
+                entry = index_ref[(8 * step + leaf) * NF + 4 * s_high + low]
+                value = table_ref[pl.ds(pl.multiple_of(entry * 16, 16), 16), :]
+                merged = value if low == 0 else jnp.where(block == low, value, merged)
+            gather_ref[16 * leaf : 16 * leaf + 16, 128 * s_high : 128 * s_high + 128] = merged
+    result = dot_nt(gather_ref[...], d_ref[0])
+    which = iota((16, 256), 1) % 8
+    far = result[0:16]
+    for leaf in range(1, 8):
+        far = jnp.where(which == leaf, result[16 * leaf : 16 * leaf + 16], far)
+    parent = field_ref[pl.ds(pl.multiple_of(32 * (step // 2), 32), 32), :]
+    leaf_field = (far + joined(dot_nt(parent, bd_ref[0]))).astype(bf16)
+    part = dot_nt(leaf_field, ub_ref[0])
+    high = part.astype(bf16)
+    far_ref[pl.ds(pl.multiple_of(16 * step, 16), 16), :] = high
+    far_ref[pl.ds(pl.multiple_of(256 + 16 * step, 16), 16), :] = (part - high.astype(f32)).astype(bf16)
+
+    @pl.when(step == GROUPS - 1)
+    def _():
+        column = iota((512, 512), 1)
+        perm = where_eq(iota((512, 512), 0), (column % LEAF) * 8 + column // LEAF)
+        whole = joined(dot(far_ref[...], perm))
+        for g in range(GROUPS):
+            out_ref[:, 512 * g : 512 * g + 512] = near_ref[:, 512 * g : 512 * g + 512] + whole[16 * g : 16 * g + 16, :]
+
+
+def downward(bits, index, payload, received, em, sm, bdup, d, ub, bd, near):
+    full = lambda *shape: pl.BlockSpec(shape, lambda i: (0,) * len(shape))
+    smem = pl.BlockSpec(memory_space=pltpu.SMEM)
+    each = lambda *shape: pl.BlockSpec((1,) + shape, lambda i: (i, 0, 0))
+    return pl.pallas_call(
+        down_kernel,
+        grid=(GROUPS,),
+        out_shape=jax.ShapeDtypeStruct((16, LEAF_DEV * LEAF), f32),
+        in_specs=[smem, smem]
+        + [full(16, WIDTH)] * 8
+        + [full(320, 128), full(192, 128), full(UPPER, 256, 256)]
+        + [each(256, 512), each(512, 256), each(256, 256), full(16, LEAF_DEV * LEAF)],
+        out_specs=full(16, LEAF_DEV * LEAF),
+        scratch_shapes=[
+            pltpu.VMEM((16400, 128), bf16),
+            pltpu.VMEM((256, 256), bf16),
+            pltpu.VMEM((512, 512), bf16),
+            pltpu.VMEM((128, 512), bf16),
+        ],
+        compiler_params=pltpu.CompilerParams(vmem_limit_bytes=48 * 1024 * 1024),
+        cost_estimate=pl.CostEstimate(flops=3_000_000_000, bytes_accessed=16_000_000, transcendentals=0),
+    )(bits, index, payload, *received, em, sm, bdup, d, ub, bd, near)
+
+
 def top_start(height, number):
     if height == 0:
         return 0
@@ -203,101 +544,34 @@
     top_transfer,
     top_coupling,
 ):
-    rhs_count = points.shape[0]
-    leaf_local = basis.shape[0]
     device = lax.axis_index("leaf")
-    devices_all = lax.axis_size("leaf")
-    tree_bits = devices_all.bit_length() - 1
-    basis_blocks = basis.reshape(leaf_local, LEAF, RANK)
-    point_blocks = points.reshape(rhs_count, leaf_local, LEAF)
-    leaf_coeff = jnp.einsum(
-        "lpk,rlp->lkr", basis_blocks, point_blocks, preferred_element_type=jnp.float32
-    ).astype(jnp.bfloat16)
-    flat_coeff = leaf_coeff.reshape(leaf_local, RANK * rhs_count)
+    bits = jnp.right_shift(device, jnp.arange(8, dtype=jnp.int32)) & 1
+    starts = jnp.array([top_start(h, N_DEV) for h in range(6)], jnp.int32)
+    heights = jnp.arange(6, dtype=jnp.int32)
+    nodes = starts + jnp.right_shift(device, heights)
+    pair_rows = (starts + (jnp.right_shift(device, heights) & -2))[:5]
+    pair_rows = (pair_rows[:, None] + jnp.arange(2, dtype=jnp.int32)[None, :]).reshape(10)
+    pairs = top_transfer[pair_rows]
+    couples = top_coupling[nodes].reshape(12, RANK * RANK)
+    owner = jnp.bitwise_xor(jnp.right_shift(far_list, 7), device)
+    slot = sum((owner >> k > 0).astype(jnp.int32) for k in range(7))
+    within = far_list & (LEAF_DEV - 1)
+    entry = slot * LEAF_DEV + (within & 7) * GROUPS + (within >> 3)
+    index = jnp.where(far_list >= 0, entry, 8 * LEAF_DEV).reshape(LEAF_DEV * NF)
+    payload, ub, bd, bdup, em, sm = upward(points, basis, local_transfer, pairs, couples)
+    first = payload
+    received = []
+    for height, mask in enumerate(PARTNERS):
+        route = [(i, i ^ mask) for i in range(N_DEV)]
+        received.append(lax.ppermute(payload, "leaf", route))
+        if height < 6:
+            payload = tree_step(height, bits, first, payload, received[height], em)
     ext_points = padded(points, (("leaf", 1),), SPAN * LEAF)
     ext_coords = padded(coords, (("leaf", 1),), SPAN * LEAF)
-    present = far_list >= 0
-    table = lax.all_gather(flat_coeff, "leaf", axis=0, tiled=True)
-    row_index = jnp.where(present, far_list, 0)
-    gathered = table[row_index]
-    gathered = jnp.where(present[:, :, None], gathered, jnp.zeros_like(gathered))
-    gathered = gathered.reshape(leaf_local, NF, RANK, rhs_count)
-    coupling = far_coupling.reshape(leaf_local, NF, RANK, RANK)
-    far_terms = jnp.einsum("lsab,lsbr->lar", coupling, gathered, preferred_element_type=jnp.float32)
-    current = leaf_coeff.astype(jnp.float32)
-    offset = 0
-    number = leaf_local
-    matrices = []
-    while number > 1:
-        chosen = (
-            local_transfer[offset : offset + number].reshape(number, RANK, RANK).astype(jnp.float32)
-        )
-        matrices.append(chosen)
-        partial_value = jnp.einsum("nab,nar->nbr", chosen, current, precision=highest)
-        current = partial_value[0::2] + partial_value[1::2]
-        offset += number
-        number //= 2
-    device_coeff = current[0]
-
-    def top_matrix(height, node):
-        picked = lax.dynamic_index_in_dim(
-            top_transfer, top_start(height, devices_all) + node, 0, keepdims=False
-        )
-        return picked.reshape(RANK, RANK).astype(jnp.float32)
-
-    top_terms = []
-    mine = device_coeff
-    before_mine = jnp.zeros_like(mine)
-    before_sibling = jnp.zeros_like(mine)
-    for height in range(tree_bits):
-        received = swapped(jnp.stack([mine, before_mine, before_sibling]), "leaf", height)
-        if height >= 1:
-            lower = jnp.right_shift(device, height - 1)
-            partner_first = lower % 2 == 0
-            cousin_left = jnp.where(partner_first, received[1], received[2])
-            cousin_right = jnp.where(partner_first, received[2], received[1])
-            coupled_height = height - 1
-            coupled_picked = lax.dynamic_index_in_dim(
-                top_coupling, top_start(coupled_height, devices_all) + lower, 0, keepdims=False
-            )
-            pair = coupled_picked.reshape(2, RANK, RANK).astype(jnp.float32)
-            top_terms.append(
-                jnp.dot(pair[0], cousin_left, precision=highest)
-                + jnp.dot(pair[1], cousin_right, precision=highest)
-            )
-        sibling = received[0]
-        before_mine = mine
-        before_sibling = sibling
-        if height <= tree_bits - 3:
-            node = jnp.right_shift(device, height)
-            own_term = jnp.dot(top_matrix(height, node).T, mine, precision=highest)
-            sibling_term = jnp.dot(
-                top_matrix(height, jnp.bitwise_xor(node, 1)).T, sibling, precision=highest
-            )
-            mine = own_term + sibling_term
-        else:
-            mine = jnp.zeros_like(mine)
-    field = top_terms[tree_bits - 2]
-    for height in range(tree_bits - 2, 0, -1):
-        child = jnp.right_shift(device, height - 1)
-        field = top_terms[height - 1] + jnp.dot(
-            top_matrix(height - 1, child), field, precision=highest
-        )
-    field = field[None]
-    for depth_num in range(len(matrices) - 1, -1, -1):
-        spread = jnp.einsum(
-            "nab,nbr->nar", matrices[depth_num], jnp.repeat(field, 2, axis=0), precision=highest
-        )
-        field = far_terms + spread if depth_num == 0 else spread
-    leaf_field = field.astype(jnp.bfloat16)
-    far_part = jnp.einsum(
-        "lpk,lkr->rlp", basis_blocks, leaf_field, preferred_element_type=jnp.float32
-    )
-    far_part = far_part.reshape(rhs_count, leaf_local * LEAF)
-    first_global = device * leaf_local
-    near_rel = jnp.transpose(jnp.where(near_list >= 0, near_list - first_global, -1000))
+    near_rel = jnp.transpose(jnp.where(near_list >= 0, near_list - device * LEAF_DEV, -1000))
     near_part = near_field(ext_coords, ext_points, near_rel)
-    return near_part + far_part
+    d = regroup(far_coupling)
+    return downward(bits, index, first, received, em, sm, bdup, d, ub, bd, near_part)
 
 
 def solution(mesh):

time: 220 us -> 142 us (0.65)
  local copies, waits for them, and re-layouts: 101 us -> 21 us
  Pallas kernels: 27 us -> 75.8 us
  matrix products: 29.8 us -> 0 us
  between operations: 14 us -> 0.27 us
  starting transfers between devices: 33.8 us -> 30.2 us
    pallas_call x0 -> x9, Pallas kernels: none -> 48.7 us  [the longest x1 17.3 us: downward(): pl.pallas_call(down_kernel, grid=(GROUPS,), out_shape=jax.ShapeDtypeStruc...]
    reshape x22 -> x2, local copies, waits for them, and re-layouts: 36.7 us -> 0.1 us  [the longest x1 0.08 us: per_device(): index = jnp.where(far_list >= 0, entry, 8 * LEAF_DEV).reshape(LEAF_DEV * NF)]
    gather x2, local copies, waits for them, and re-layouts: 35 us -> 2.3 us  [the longest x1 1.7 us: per_device(): pairs = top_transfer[pair_rows]]
    dot_general x44 -> x0, matrix products: 29.8 us -> none  [the longest x1 13.9 us: per_device(): jnp.einsum('lsab,lsbr->lar', coupling, gathered, preferred_element_type=j...]
    squeeze x12 -> x0, local copies, waits for them, and re-layouts: 7.47 us -> none  [the longest x6 4.03 us: per_device(): pair[0]]
    slice x14 -> x0, local copies, waits for them, and re-layouts: 6.79 us -> none  [the longest x7 5.65 us: per_device(): local_transfer[offset:offset + number].reshape(number, RANK, RANK)]
    unnamed x56 -> x62, local copies, waits for them, and re-layouts: 9.11 us -> 15.7 us
    ppermute x2, starting transfers between devices: 7.46 us -> 5.11 us  [padded(): lax.ppermute(tail, axis, [(i, (i + 1) % count) for i in range(ends)])]
  transfers between devices with their start and end apart: 12 -> 11, of which waited for: 5 -> 3; matrix products, arithmetic and copies ran while one was open for 34% -> 5% of each run, Pallas kernels for 12% -> 34%
where the time goes in v2:
time: 142 us; the launch traced here: 141 us
  Pallas kernels  75.8 us (53%)
  starting transfers between devices  30.2 us (21%)
  local copies, waits for them, and re-layouts  21 us (15%)
  waiting for transfers between devices  8.67 us (6%)
  other arithmetic  4.66 us (3%)
    pallas_call x1, Pallas kernels, near_field(): pl.pallas_call(functools.partial(near_kernel, blocks), out_shape=jax.Shap...  27 us
    ppermute x7, starting transfers between devices, per_device(): received.append(lax.ppermute(payload, 'leaf', route))  22.6 us
    pallas_call x1, Pallas kernels, downward(): pl.pallas_call(down_kernel, grid=(GROUPS,), out_shape=jax.ShapeDtypeStruc...  17.3 us
    unnamed x62, local copies, waits for them, and re-layouts  15.7 us
    pallas_call x6, Pallas kernels, tree_step(): pl.pallas_call(functools.partial(step_kernel, height), out_shape=jax.Shap...  12.4 us
    pallas_call x1, Pallas kernels, regroup(): pl.pallas_call(regroup_kernel, grid=(GROUPS,), out_shape=jax.ShapeDtypeSt...  10.3 us
    pallas_call x1, Pallas kernels, upward(): pl.pallas_call(up_kernel, grid=(GROUPS // 2,), out_shape=(jax.ShapeDtypeS...  8.69 us
    ppermute x7, waiting for transfers between devices, per_device(): received.append(lax.ppermute(payload, 'leaf', route))  8.66 us
  transfers between devices with their start and end apart: 11, of which 3 were waited for; matrix products, arithmetic and copies ran while one was open for 5% of the time, Pallas kernels for 34%

profile of v2, /device:TPU:0, one launch (start us, length us, event | category | flops | bytes accessed | tf_op | source)
XLA Modules:
  0.0 140.6 jit_solution(12574985875283013857)
XLA Ops:
  0.0 0.7 compare_select_fusion
  1.2 0.6 gather_fusion.1
  1.9 1.7 %gather_fusion = bf16[10,1024]{1,0:T(8,128)(2,1)S(1)} fusion(bf16[254,1024]{1,0:T(8,128)(2,1)} %param.17, s32[1024]{0:T(1024)S(1)} %pad_clamp_fusion.1), kind=kCustom, calls=%fused_computation | custom fusion | bytes 41000 | tf_op jit(solution)/shard_map/gather | solution.py:554
  3.6 0.9 copy-done.21
  4.5 1.0 copy-done.27
  5.6 1.0 copy-done.28
  6.6 8.7 %shard_map.100 = (bf16[16,4352]{1,0:T(8,128)(2,1)S(1)}, bf16[16,512,256]{2,1,0:T(8,128)(2,1)}, bf16[16,256,256]{2,1,0:T(8,128)(2,1)S(1)}, bf16[17,256,256]{2,1,0...) custom-call(bf16[16,8192]{1,0:T(8,128)(2,1)S(1)} %copy-done.21, ...), custom_call_target="tpu_custom_call" | custom-call | flops 1000000000 | bytes 10000000 | tf_op jit(solution)/shard_map/pallas_call | solution.py:332
  15.3 0.6 copy-done.5
  15.9 1.3 copy-done.7
  17.3 0.6 copy-done.23
  17.9 1.4 fusion.2
  19.2 3.0 %collective-permute-start.7 = (f32[3,512]{1,0:T(4,128)}, f32[3,512]{1,0:T(4,128)}, u32[]{:S(2)}, u32[]{:S(2)}) collective-permute-start(f32[3,512]{1,0:T(4,128)} %get-tuple-element.19), channel_id=1, source_target_pairs={{0,1},{1,2},{2,3},{3,4},{4,5},{5,6},{6,7},{7,8},{8,9},{9,10},{10,1... | collective-permute-start | bytes 18440 | tf_op jit(solution)/shard_map/ppermute | solution.py:34
  22.2 1.3 collective-permute-start.8
  23.5 0.5 shift-right-arithmetic_and_fusion.bits_ref
  24.0 0.6 copy-done.9
  24.7 2.1 %shard_map.101.payload_ref = bf16[16,4352]{1,0:T(8,128)(2,1)} custom-call(s32[8]{0:T(128)} %shift-right-arithmetic_and_fusion.bits_ref, bf16[16,4352]{1,0:T(8,128)(2,1)} %copy-done.2, bf16[16,4352]{1,0:T(8,128)(2,1)} %copy-done.2, bf16[16,4352]{1,0:T(8,128)(2,1)} %copy-done.9, bf16[320,128]{1,0:T(8,128)(2,1)} %copy-done.5), custom_call_target="tpu_custom_call" | custom-call | flops 1000000 | bytes 400000 | tf_op jit(solution)/shard_map/pallas_call | solution.py:387
  26.8 3.0 %collective-permute-start.1 = (bf16[16,4352]{1,0:T(8,128)(2,1)}, bf16[16,4352]{1,0:T(8,128)(2,1)S(1)}, u32[]{:S(2)}, u32[]{:S(2)}) collective-permute-start(bf16[16,4352]{1,0:T(8,128)(2,1)} %shard_map.101.payload_ref), channel_id=1, source_target_pairs={{0,2},{1,3},{2,0},{3,1},{4,6},{5,7},{6,4},{7,5},{8,10},{9,11},{10,... | collective-permute-start | bytes 417800 | tf_op jit(solution)/shard_map/ppermute | solution.py:566
  29.8 1.3 fusion.1
  31.1 2.2 %collective-permute-start.9 = (bf16[16,512]{1,0:T(8,128)(2,1)}, bf16[16,512]{1,0:T(8,128)(2,1)}, u32[]{:S(2)}, u32[]{:S(2)}) collective-permute-start(bf16[16,512]{1,0:T(8,128)(2,1)} %get-tuple-element.17), channel_id=1, source_target_pairs={{0,1},{1,2},{2,3},{3,4},{4,5},{5,6},{6,7},{7,8},{8,9},{9,10},{10,1... | collective-permute-start | bytes 49160 | tf_op jit(solution)/shard_map/ppermute | solution.py:34
  33.3 1.3 collective-permute-start.10
  34.6 0.6 copy-done.11
  35.2 2.1 %shard_map.102.payload_ref = bf16[16,4352]{1,0:T(8,128)(2,1)} custom-call(s32[8]{0:T(128)} %shift-right-arithmetic_and_fusion.bits_ref, bf16[16,4352]{1,0:T(8,128)(2,1)} %copy-done.2, bf16[16,4352]{1,0:T(8,128)(2,1)} %shard_map.101.payload_ref, bf16[16,4352]{1,0:T(8,128)(2,1)} %copy-done.11, bf16[320,128]{1,0:T(8,128)(2,1)} %copy-done.5), custom_call_target="tpu_custom_call" | custom-call | flops 1000000 | bytes 400000 | tf_op jit(solution)/shard_map/pallas_call | solution.py:387
  37.3 4.3 %collective-permute-start.2 = (bf16[16,4352]{1,0:T(8,128)(2,1)}, bf16[16,4352]{1,0:T(8,128)(2,1)S(1)}, u32[]{:S(2)}, u32[]{:S(2)}) collective-permute-start(bf16[16,4352]{1,0:T(8,128)(2,1)} %shard_map.102.payload_ref), channel_id=1, source_target_pairs={{0,6},{1,7},{2,4},{3,5},{4,2},{5,3},{6,0},{7,1},{8,14},{9,15},{10,... | collective-permute-start | bytes 417800 | tf_op jit(solution)/shard_map/ppermute | solution.py:566
  41.6 4.1 %collective-permute-done.2.received_ref.refs_2_ = bf16[16,4352]{1,0:T(8,128)(2,1)S(1)} collective-permute-done((bf16[16,4352]{1,0:T(8,128)(2,1)}, bf16[16,4352]{1,0:T(8,128)(2,1)S(1)}, u32[]{:S(2)}, u32[]{:S(2)}) %collective-permute-start.2) | collective-permute-done | bytes 139296 | tf_op jit(solution)/shard_map/ppermute | solution.py:566
  45.8 0.6 copy-done.13
  46.4 2.1 %shard_map.103.payload_ref = bf16[16,4352]{1,0:T(8,128)(2,1)} custom-call(s32[8]{0:T(128)} %shift-right-arithmetic_and_fusion.bits_ref, bf16[16,4352]{1,0:T(8,128)(2,1)} %copy-done.2, bf16[16,4352]{1,0:T(8,128)(2,1)} %shard_map.102.payload_ref, bf16[16,4352]{1,0:T(8,128)(2,1)} %copy-done.13, bf16[320,128]{1,0:T(8,128)(2,1)} %copy-done.5), custom_call_target="tpu_custom_call" | custom-call | flops 1000000 | bytes 400000 | tf_op jit(solution)/shard_map/pallas_call | solution.py:387
  48.5 4.7 %collective-permute-start.3 = (bf16[16,4352]{1,0:T(8,128)(2,1)}, bf16[16,4352]{1,0:T(8,128)(2,1)S(1)}, u32[]{:S(2)}, u32[]{:S(2)}) collective-permute-start(bf16[16,4352]{1,0:T(8,128)(2,1)} %shard_map.103.payload_ref), channel_id=1, source_target_pairs={{0,8},{1,9},{2,10},{3,11},{4,12},{5,13},{6,14},{7,15},{8,0},{9,1},... | collective-permute-start | bytes 417800 | tf_op jit(solution)/shard_map/ppermute | solution.py:566
  53.2 0.6 select_bitcast_fusion.rel_ref
  54.0 2.2 %copy-done.4 = bf16[128,16,1024]{2,1,0:T(8,128)(2,1)S(1)} copy-done((bf16[128,16,1024]{2,1,0:T(8,128)(2,1)S(1)}, bf16[128,16,1024]{2,1,0:T(8,128)(2,1)}, u32[]{:S(2)}) %copy-start.4) | copy-done | bytes 4194328
  56.2 10.3 %shard_map.107.refs_10_ = bf16[16,256,512]{2,1,0:T(8,128)(2,1)S(1)} custom-call(bf16[128,16,1024]{2,1,0:T(8,128)(2,1)S(1)} %copy-done.4), custom_call_target="tpu_custom_call" | custom-call | flops 30000000 | bytes 8400000 | tf_op jit(solution)/shard_map/pallas_call | solution.py:424
  66.5 2.0 %copy-done.1 = bf16[16,256,512]{2,1,0:T(8,128)(2,1)} copy-done((bf16[16,256,512]{2,1,0:T(8,128)(2,1)}, bf16[16,256,512]{2,1,0:T(8,128)(2,1)S(1)}, u32[]{:S(2)}) %copy-start.1) | copy-done | bytes 4194328
  68.6 0.7 copy-done.15
  69.2 2.1 %shard_map.104.payload_ref = bf16[16,4352]{1,0:T(8,128)(2,1)} custom-call(s32[8]{0:T(128)} %shift-right-arithmetic_and_fusion.bits_ref, bf16[16,4352]{1,0:T(8,128)(2,1)} %copy-done.2, bf16[16,4352]{1,0:T(8,128)(2,1)} %shard_map.103.payload_ref, bf16[16,4352]{1,0:T(8,128)(2,1)} %copy-done.15, bf16[320,128]{1,0:T(8,128)(2,1)} %copy-done.5), custom_call_target="tpu_custom_call" | custom-call | flops 1000000 | bytes 400000 | tf_op jit(solution)/shard_map/pallas_call | solution.py:387
  71.3 2.5 %collective-permute-start.4 = (bf16[16,4352]{1,0:T(8,128)(2,1)}, bf16[16,4352]{1,0:T(8,128)(2,1)S(1)}, u32[]{:S(2)}, u32[]{:S(2)}) collective-permute-start(bf16[16,4352]{1,0:T(8,128)(2,1)} %shard_map.104.payload_ref), channel_id=1, source_target_pairs={{0,24},{1,25},{2,26},{3,27},{4,28},{5,29},{6,30},{7,31},{8,16},{9,... | collective-permute-start | bytes 417800 | tf_op jit(solution)/shard_map/ppermute | solution.py:566
  73.8 1.0 pad_maximum_fusion.1.coords_ref
  74.8 3.0 %collective-permute-done.4.received_ref.refs_4_ = bf16[16,4352]{1,0:T(8,128)(2,1)S(1)} collective-permute-done((bf16[16,4352]{1,0:T(8,128)(2,1)}, bf16[16,4352]{1,0:T(8,128)(2,1)S(1)}, u32[]{:S(2)}, u32[]{:S(2)}) %collective-permute-start.4) | collective-permute-done | bytes 139296 | tf_op jit(solution)/shard_map/ppermute | solution.py:566
  77.8 0.6 copy-done.17
  78.4 2.1 %shard_map.105.payload_ref = bf16[16,4352]{1,0:T(8,128)(2,1)} custom-call(s32[8]{0:T(128)} %shift-right-arithmetic_and_fusion.bits_ref, bf16[16,4352]{1,0:T(8,128)(2,1)} %copy-done.2, bf16[16,4352]{1,0:T(8,128)(2,1)} %shard_map.104.payload_ref, bf16[16,4352]{1,0:T(8,128)(2,1)} %copy-done.17, bf16[320,128]{1,0:T(8,128)(2,1)} %copy-done.5), custom_call_target="tpu_custom_call" | custom-call | flops 1000000 | bytes 400000 | tf_op jit(solution)/shard_map/pallas_call | solution.py:387
  80.5 4.4 %collective-permute-start.5 = (bf16[16,4352]{1,0:T(8,128)(2,1)}, bf16[16,4352]{1,0:T(8,128)(2,1)S(1)}, u32[]{:S(2)}, u32[]{:S(2)}) collective-permute-start(bf16[16,4352]{1,0:T(8,128)(2,1)} %shard_map.105.payload_ref), channel_id=1, source_target_pairs={{0,32},{1,33},{2,34},{3,35},{4,36},{5,37},{6,38},{7,39},{8,40},{9,... | collective-permute-start | bytes 417800 | tf_op jit(solution)/shard_map/ppermute | solution.py:566
  84.9 1.7 %pad_maximum_fusion.points_ref = bf16[16,9216]{1,0:T(8,128)(2,1)} fusion(bf16[16,512]{1,0:T(8,128)(2,1)} %collective-permute-done.10, bf16[16,8192]{1,0:T(8,128)(2,1)} %points_ref.1, bf16[16,512]{1,0:T(8,128)(2,1)} %collective-permute-done.9), kind=kLoop, calls=%fused_computation.2 | loop fusion | flops 884736 | bytes 589824 | tf_op jit(solution)/shard_map/concatenate | solution.py:32
  86.6 1.5 %collective-permute-done.5.received_ref.refs_5_ = bf16[16,4352]{1,0:T(8,128)(2,1)S(1)} collective-permute-done((bf16[16,4352]{1,0:T(8,128)(2,1)}, bf16[16,4352]{1,0:T(8,128)(2,1)S(1)}, u32[]{:S(2)}, u32[]{:S(2)}) %collective-permute-start.5) | collective-permute-done | bytes 139296 | tf_op jit(solution)/shard_map/ppermute | solution.py:566
  88.2 0.7 copy-done.19
  88.8 1.9 %shard_map.106 = bf16[16,4352]{1,0:T(8,128)(2,1)} custom-call(s32[8]{0:T(128)} %shift-right-arithmetic_and_fusion.bits_ref, bf16[16,4352]{1,0:T(8,128)(2,1)} %copy-done.2, bf16[16,4352]{1,0:T(8,128)(2,1)} %shard_map.105.payload_ref, bf16[16,4352]{1,0:T(8,128)(2,1)} %copy-done.19, bf16[320,128]{1,0:T(8,128)(2,1)} %copy-done.5), custom_call_target="tpu_custom_call" | custom-call | flops 1000000 | bytes 400000 | tf_op jit(solution)/shard_map/pallas_call | solution.py:387
  90.8 3.7 %collective-permute-start.6 = (bf16[16,4352]{1,0:T(8,128)(2,1)}, bf16[16,4352]{1,0:T(8,128)(2,1)S(1)}, u32[]{:S(2)}, u32[]{:S(2)}) collective-permute-start(bf16[16,4352]{1,0:T(8,128)(2,1)} %shard_map.106), channel_id=1, source_target_pairs={{0,96},{1,97},{2,98},{3,99},{4,100},{5,101},{6,102},{7,103},{8,104... | collective-permute-start | bytes 417800 | tf_op jit(solution)/shard_map/ppermute | solution.py:566
  94.5 1.0 copy-done.22
  95.4 0.7 copy-done.26
  96.1 27.0 %shard_map.108.refs_13_ = f32[16,8192]{1,0:T(8,128)S(1)} custom-call(f32[3,9216]{1,0:T(4,128)S(1)} %pad_maximum_fusion.1.coords_ref, bf16[16,9216]{1,0:T(8,128)(2,1)S(1)} %copy-done.22, s32[12,128]{1,0:T(8,128)S(1)} %copy-done.26), custom_call_target="tpu_custom_call" | custom-call | flops 2000000000 | bytes 2000000 | tf_op jit(solution)/shard_map/pallas_call | solution.py:163
  123.3 17.3 %shard_map.109 = f32[16,8192]{1,0:T(8,128)} custom-call(s32[8]{0:T(128)S(1)} %copy-done.25, s32[2048]{0:T(1024)S(1)} %reshape.37.index_ref, bf16[16,4352]{1,0:T(8,128)(2,1)S(1)} %copy-done.3, bf16[16,4352]{1,0:T(8,128)(2,1)S(1)} %copy-done.10, bf16[16,4352]{1,0:T(8,128)(2,1)S(1)} %copy-done.12, bf16[16,4352]{1,0:T(8,128)(2,1)S(1)} %copy-done.14, ...), custom_call_target="tpu_custom_call" | custom-call | flops 3000000000 | bytes 16000000 | tf_op jit(solution)/shard_map/pallas_call | solution.py:510
  (64 shorter events, 0.8 us)
Async XLA Ops:
  0.0 1.2 copy-start
  0.0 41.6 %copy-start.29 = (s32[128,16]{0,1:T(8,128)S(1)}, s32[128,16]{0,1:T(8,128)}, u32[]{:S(2)}) copy-start(s32[128,16]{0,1:T(8,128)} %param.13) | copy-start | bytes 24580
  0.0 53.2 %copy-start.30 = (s32[128,12]{0,1:T(8,128)S(1)}, s32[128,12]{0,1:T(8,128)}, u32[]{:S(2)}) copy-start(s32[128,12]{0,1:T(8,128)} %param.15) | copy-start | bytes 18436
  3.6 1.0 copy-start.21
  4.5 1.0 copy-start.27
  5.6 1.0 copy-start.28
  15.3 0.6 copy-start.5
  15.9 1.3 copy-start.7
  17.3 0.6 copy-start.23
  17.9 6.2 %copy-start.2 = (bf16[16,4352]{1,0:T(8,128)(2,1)}, bf16[16,4352]{1,0:T(8,128)(2,1)S(1)}, u32[]{:S(2)}) copy-start(bf16[16,4352]{1,0:T(8,128)(2,1)S(1)} %get-tuple-element.11.first_ref.payload_ref) | copy-start | bytes 417796
  17.9 6.2 %collective-permute-start = (bf16[16,4352]{1,0:T(8,128)(2,1)S(1)}, bf16[16,4352]{1,0:T(8,128)(2,1)S(1)}, u32[]{:S(2)}, u32[]{:S(2)}) collective-permute-start(bf16[16,4352]{1,0:T(8,128)(2,1)S(1)} %get-tuple-element.11.first_ref.payload_ref), channel_id=1, source_target_pairs={{0,1},{1,0},{2,3},{3,2},{4,5},{5,4},{6,7},{7,6},{8,9},{9,8},{10,11... | collective-permute-start | bytes 417800 | tf_op jit(solution)/shard_map/ppermute | solution.py:566
  19.2 54.6 %collective-permute-start.7 = (f32[3,512]{1,0:T(4,128)}, f32[3,512]{1,0:T(4,128)}, u32[]{:S(2)}, u32[]{:S(2)}) collective-permute-start(f32[3,512]{1,0:T(4,128)} %get-tuple-element.19), channel_id=1, source_target_pairs={{0,1},{1,2},{2,3},{3,4},{4,5},{5,6},{6,7},{7,8},{8,9},{9,10},{10,1... | collective-permute-start | bytes 18440 | tf_op jit(solution)/shard_map/ppermute | solution.py:34
  22.2 51.6 %collective-permute-start.8 = (f32[3,512]{1,0:T(4,128)}, f32[3,512]{1,0:T(4,128)}, u32[]{:S(2)}, u32[]{:S(2)}) collective-permute-start(f32[3,512]{1,0:T(4,128)} %get-tuple-element.20), channel_id=1, source_target_pairs={{1,0},{2,1},{3,2},{4,3},{5,4},{6,5},{7,6},{8,7},{9,8},{10,9},{11,1... | collective-permute-start | bytes 18440 | tf_op jit(solution)/shard_map/ppermute | solution.py:36
  24.0 0.6 copy-start.9
  26.8 7.8 %collective-permute-start.1 = (bf16[16,4352]{1,0:T(8,128)(2,1)}, bf16[16,4352]{1,0:T(8,128)(2,1)S(1)}, u32[]{:S(2)}, u32[]{:S(2)}) collective-permute-start(bf16[16,4352]{1,0:T(8,128)(2,1)} %shard_map.101.payload_ref), channel_id=1, source_target_pairs={{0,2},{1,3},{2,0},{3,1},{4,6},{5,7},{6,4},{7,5},{8,10},{9,11},{10,... | collective-permute-start | bytes 417800 | tf_op jit(solution)/shard_map/ppermute | solution.py:566
  31.1 53.8 %collective-permute-start.9 = (bf16[16,512]{1,0:T(8,128)(2,1)}, bf16[16,512]{1,0:T(8,128)(2,1)}, u32[]{:S(2)}, u32[]{:S(2)}) collective-permute-start(bf16[16,512]{1,0:T(8,128)(2,1)} %get-tuple-element.17), channel_id=1, source_target_pairs={{0,1},{1,2},{2,3},{3,4},{4,5},{5,6},{6,7},{7,8},{8,9},{9,10},{10,1... | collective-permute-start | bytes 49160 | tf_op jit(solution)/shard_map/ppermute | solution.py:34
  33.3 51.6 %collective-permute-start.10 = (bf16[16,512]{1,0:T(8,128)(2,1)}, bf16[16,512]{1,0:T(8,128)(2,1)}, u32[]{:S(2)}, u32[]{:S(2)}) collective-permute-start(bf16[16,512]{1,0:T(8,128)(2,1)} %get-tuple-element.18), channel_id=1, source_target_pairs={{1,0},{2,1},{3,2},{4,3},{5,4},{6,5},{7,6},{8,7},{9,8},{10,9},{11,1... | collective-permute-start | bytes 49160 | tf_op jit(solution)/shard_map/ppermute | solution.py:36
  34.6 0.7 copy-start.11
  37.3 8.4 %collective-permute-start.2 = (bf16[16,4352]{1,0:T(8,128)(2,1)}, bf16[16,4352]{1,0:T(8,128)(2,1)S(1)}, u32[]{:S(2)}, u32[]{:S(2)}) collective-permute-start(bf16[16,4352]{1,0:T(8,128)(2,1)} %shard_map.102.payload_ref), channel_id=1, source_target_pairs={{0,6},{1,7},{2,4},{3,5},{4,2},{5,3},{6,0},{7,1},{8,14},{9,15},{10,... | collective-permute-start | bytes 417800 | tf_op jit(solution)/shard_map/ppermute | solution.py:566
  45.8 0.6 copy-start.13
  48.5 20.1 %collective-permute-start.3 = (bf16[16,4352]{1,0:T(8,128)(2,1)}, bf16[16,4352]{1,0:T(8,128)(2,1)S(1)}, u32[]{:S(2)}, u32[]{:S(2)}) collective-permute-start(bf16[16,4352]{1,0:T(8,128)(2,1)} %shard_map.103.payload_ref), channel_id=1, source_target_pairs={{0,8},{1,9},{2,10},{3,11},{4,12},{5,13},{6,14},{7,15},{8,0},{9,1},... | collective-permute-start | bytes 417800 | tf_op jit(solution)/shard_map/ppermute | solution.py:566
  54.0 2.2 %copy-start.4 = (bf16[128,16,1024]{2,1,0:T(8,128)(2,1)S(1)}, bf16[128,16,1024]{2,1,0:T(8,128)(2,1)}, u32[]{:S(2)}) copy-start(bf16[128,16,1024]{2,1,0:T(8,128)(2,1)} %c_ref.1) | copy-start | bytes 12582916
  66.5 2.0 %copy-start.1 = (bf16[16,256,512]{2,1,0:T(8,128)(2,1)}, bf16[16,256,512]{2,1,0:T(8,128)(2,1)S(1)}, u32[]{:S(2)}) copy-start(bf16[16,256,512]{2,1,0:T(8,128)(2,1)S(1)} %shard_map.107.refs_10_) | copy-start | bytes 12582916
  68.6 0.7 copy-start.15
  71.3 6.5 %collective-permute-start.4 = (bf16[16,4352]{1,0:T(8,128)(2,1)}, bf16[16,4352]{1,0:T(8,128)(2,1)S(1)}, u32[]{:S(2)}, u32[]{:S(2)}) collective-permute-start(bf16[16,4352]{1,0:T(8,128)(2,1)} %shard_map.104.payload_ref), channel_id=1, source_target_pairs={{0,24},{1,25},{2,26},{3,27},{4,28},{5,29},{6,30},{7,31},{8,16},{9,... | collective-permute-start | bytes 417800 | tf_op jit(solution)/shard_map/ppermute | solution.py:566
  77.8 0.7 copy-start.17
  80.5 7.6 %collective-permute-start.5 = (bf16[16,4352]{1,0:T(8,128)(2,1)}, bf16[16,4352]{1,0:T(8,128)(2,1)S(1)}, u32[]{:S(2)}, u32[]{:S(2)}) collective-permute-start(bf16[16,4352]{1,0:T(8,128)(2,1)} %shard_map.105.payload_ref), channel_id=1, source_target_pairs={{0,32},{1,33},{2,34},{3,35},{4,36},{5,37},{6,38},{7,39},{8,40},{9,... | collective-permute-start | bytes 417800 | tf_op jit(solution)/shard_map/ppermute | solution.py:566
  88.1 0.7 copy-start.19
  90.7 32.5 %copy-start.3 = (bf16[16,4352]{1,0:T(8,128)(2,1)S(1)}, bf16[16,4352]{1,0:T(8,128)(2,1)}, u32[]{:S(2)}) copy-start(bf16[16,4352]{1,0:T(8,128)(2,1)} %copy-done.2) | copy-start | bytes 417796
  90.7 32.5 %copy-start.6 = (bf16[320,128]{1,0:T(8,128)(2,1)S(1)}, bf16[320,128]{1,0:T(8,128)(2,1)}, u32[]{:S(2)}) copy-start(bf16[320,128]{1,0:T(8,128)(2,1)} %copy-done.5) | copy-start | bytes 245764
  90.7 32.5 %copy-start.8 = (bf16[16,256,256]{2,1,0:T(8,128)(2,1)S(1)}, bf16[16,256,256]{2,1,0:T(8,128)(2,1)}, u32[]{:S(2)}) copy-start(bf16[16,256,256]{2,1,0:T(8,128)(2,1)} %copy-done.7) | copy-start | bytes 6291460
  90.7 32.5 %copy-start.10 = (bf16[16,4352]{1,0:T(8,128)(2,1)S(1)}, bf16[16,4352]{1,0:T(8,128)(2,1)}, u32[]{:S(2)}) copy-start(bf16[16,4352]{1,0:T(8,128)(2,1)} %copy-done.9) | copy-start | bytes 417796
  90.7 32.5 %copy-start.12 = (bf16[16,4352]{1,0:T(8,128)(2,1)S(1)}, bf16[16,4352]{1,0:T(8,128)(2,1)}, u32[]{:S(2)}) copy-start(bf16[16,4352]{1,0:T(8,128)(2,1)} %copy-done.11) | copy-start | bytes 417796
  90.8 32.5 %copy-start.14 = (bf16[16,4352]{1,0:T(8,128)(2,1)S(1)}, bf16[16,4352]{1,0:T(8,128)(2,1)}, u32[]{:S(2)}) copy-start(bf16[16,4352]{1,0:T(8,128)(2,1)} %copy-done.13) | copy-start | bytes 417796
  90.8 32.5 %copy-start.16 = (bf16[16,4352]{1,0:T(8,128)(2,1)S(1)}, bf16[16,4352]{1,0:T(8,128)(2,1)}, u32[]{:S(2)}) copy-start(bf16[16,4352]{1,0:T(8,128)(2,1)} %copy-done.15) | copy-start | bytes 417796
  90.8 32.5 %copy-start.18 = (bf16[16,4352]{1,0:T(8,128)(2,1)S(1)}, bf16[16,4352]{1,0:T(8,128)(2,1)}, u32[]{:S(2)}) copy-start(bf16[16,4352]{1,0:T(8,128)(2,1)} %copy-done.17) | copy-start | bytes 417796
  90.8 32.5 %copy-start.20 = (bf16[16,4352]{1,0:T(8,128)(2,1)S(1)}, bf16[16,4352]{1,0:T(8,128)(2,1)}, u32[]{:S(2)}) copy-start(bf16[16,4352]{1,0:T(8,128)(2,1)} %copy-done.19) | copy-start | bytes 417796
  90.8 32.4 %collective-permute-start.6 = (bf16[16,4352]{1,0:T(8,128)(2,1)}, bf16[16,4352]{1,0:T(8,128)(2,1)S(1)}, u32[]{:S(2)}, u32[]{:S(2)}) collective-permute-start(bf16[16,4352]{1,0:T(8,128)(2,1)} %shard_map.106), channel_id=1, source_target_pairs={{0,96},{1,97},{2,98},{3,99},{4,100},{5,101},{6,102},{7,103},{8,104... | collective-permute-start | bytes 417800 | tf_op jit(solution)/shard_map/ppermute | solution.py:566
  94.5 1.0 copy-start.22
  95.4 0.7 copy-start.26
  96.1 27.1 %copy-start.24 = (bf16[192,128]{1,0:T(8,128)(2,1)S(1)}, bf16[192,128]{1,0:T(8,128)(2,1)}, u32[]{:S(2)}) copy-start(bf16[192,128]{1,0:T(8,128)(2,1)} %copy-done.23) | copy-start | bytes 147460
  96.1 27.2 %copy-start.25 = (s32[8]{0:T(128)S(1)}, s32[8]{0:T(128)}, u32[]{:S(2)}) copy-start(s32[8]{0:T(128)} %shift-right-arithmetic_and_fusion.bits_ref) | copy-start | bytes 100

commit v3 on v2

--- a/solution.py
+++ b/solution.py
@@ -23,55 +23,52 @@
 highest = lax.Precision.HIGHEST
 
 
-def padded(cells, sides, width):
-    for axis, dim in sides:
-        count = lax.axis_size(axis)
-        ends = count - 1
-        head = lax.slice_in_dim(cells, 0, width, axis=dim)
-        tail = lax.slice_in_dim(cells, cells.shape[dim] - width, cells.shape[dim], axis=dim)
-        cells = jnp.concatenate(
-            [
-                lax.ppermute(tail, axis, [(i, (i + 1) % count) for i in range(ends)]),
-                cells,
-                lax.ppermute(head, axis, [((i + 1) % count, i) for i in range(ends)]),
-            ],
-            axis=dim,
-        )
-    return cells
-
-
 LOG2E = 1.4426950408889634
 LN2 = 0.6931471805599453
 SCALE = decay_rate * LOG2E
 BLK = 256
 BL = BLK // LEAF
+FEAT = 64
 f32 = jnp.float32
 bf16 = jnp.bfloat16
 
 
 def split3(v):
-    a = v.astype(bf16)
-    rest = v - a.astype(f32)
-    b = rest.astype(bf16)
-    c = (rest - b.astype(f32)).astype(bf16)
-    return a.astype(f32), b.astype(f32), c.astype(f32)
-
-
-def features(coords):
-    v = (coords - 0.5) * SCALE
-    parts = [split3(v[c : c + 1]) for c in range(3)]
+    a = v.astype(bf16).astype(f32)
+    rest = v - a
+    b = rest.astype(bf16).astype(f32)
+    c = (rest - b).astype(bf16).astype(f32)
+    return a, b, c
+
+
+def scaled(coords):
+    return (coords - 0.5) * SCALE
+
+
+def widened(v):
+    return jnp.concatenate([v, jnp.zeros((5, v.shape[1]), f32)], axis=0)
+
+
+def features(parts):
+    a, b, c = parts
+    n = a.shape[1]
+    v = a + b + c
     norm = split3(jnp.sum(v * v, axis=0, keepdims=True))
-    one = jnp.ones_like(norm[0])
-    zero = jnp.zeros_like(one)
-    left = []
-    right = []
-    for one_part in parts:
-        a, b, c = one_part
-        left += [a, a, a, b, b, c]
-        right += [-2.0 * a, -2.0 * b, -2.0 * c, -2.0 * a, -2.0 * b, -2.0 * a]
-    left += list(norm) + [one, one, one] + [zero] * 8
-    right += [one, one, one] + list(norm) + [zero] * 8
-    return jnp.concatenate(left, axis=0), jnp.concatenate(right, axis=0)
+    row = lax.broadcasted_iota(jnp.int32, (8, n), 0)
+
+    def place(first, second):
+        out = jnp.zeros((8, n), f32)
+        for k in range(3):
+            out = jnp.where(row == k, first[k], out)
+            out = jnp.where(row == k + 3, second[k], out)
+        return out
+
+    ones = [jnp.ones((1, n), f32)] * 3
+    zero = jnp.zeros((8, n), f32)
+    left = jnp.concatenate([a, a, a, b, b, c, place(norm, ones), zero], axis=0)
+    a2, b2, c2 = -2.0 * a, -2.0 * b, -2.0 * c
+    right = jnp.concatenate([a2, b2, c2, a2, b2, a2, place(ones, norm), zero], axis=0)
+    return left, right
 
 
 def matern(squared):
@@ -80,85 +77,110 @@
     return (variance + (variance * LN2) * t) * jnp.exp2(-t)
 
 
-def near_kernel(blocks, coords_ref, points_ref, rel_ref, out_ref, left_ref, right_ref, weight_ref, acc_ref, kern_ref):
-    lanes_iota = lax.broadcasted_iota(jnp.int32, (32, LEAF_DEV), 1)
-    row_iota = lax.broadcasted_iota(jnp.int32, (32, LEAF_DEV), 0)
-    base = (lanes_iota // BL) * BL - SPAN
+def expanded(x):
+    leaf_of_lane = lax.broadcasted_iota(jnp.int32, (16, BLK), 1) // LEAF
+    zero = jnp.zeros_like(x)
+    return jnp.concatenate([jnp.where(leaf_of_lane == j, x, zero) for j in range(BL)], axis=0)
+
+
+def slot_counts(rel_ref):
+    leaf = lax.broadcasted_iota(jnp.int32, (32, LEAF_DEV), 1)
+    row = lax.broadcasted_iota(jnp.int32, (32, LEAF_DEV), 0)
+    base = (leaf // BL) * BL - SPAN
     count = jnp.zeros((32, LEAF_DEV), f32)
     for s in range(NN):
-        count = count + jnp.where(rel_ref[s : s + 1, :] - base == row_iota, 1.0, 0.0)
+        count = count + jnp.where(rel_ref[s : s + 1, :] - base == row, 1.0, 0.0)
+    return count
+
+
+def spread_counts(count, b):
     spread = (
         lax.broadcasted_iota(jnp.int32, (LEAF_DEV, BLK), 0)
         == lax.broadcasted_iota(jnp.int32, (LEAF_DEV, BLK), 1) // LEAF
     ).astype(f32).astype(bf16)
-    total = blocks + 4
-    zero_weight = jnp.zeros((32, BLK), f32)
-    for b in (0, 1, total - 2, total - 1):
-        weight_ref[b] = zero_weight
+    shifted = pltpu.roll(count, (LEAF_DEV - BL * b) % LEAF_DEV, 1) if b else count
+    return jnp.dot(shifted.astype(bf16), spread, preferred_element_type=f32)
+
+
+def weighed(acc, part, weight, offset):
+    for k in range(BL):
+        acc = acc + part[16 * k : 16 * k + 16] * weight[SPAN + offset + k : SPAN + offset + k + 1]
+    return acc
+
+
+def near_kernel(blocks, coords_ref, points_ref, rel_ref, out_ref, left_ref, right_ref, weight_ref, acc_ref, x_ref, *kerns):
+    total = blocks + 2
+    count = slot_counts(rel_ref)
     for b in range(blocks):
-        shifted = pltpu.roll(count, (LEAF_DEV - BL * b) % LEAF_DEV, 1) if b else count
-        weight_ref[b + 2] = jnp.dot(shifted.astype(bf16), spread, preferred_element_type=f32)
+        weight_ref[b] = spread_counts(count, b)
+    for b in (blocks, blocks + 1):
+        weight_ref[b] = jnp.zeros((32, BLK), f32)
+    x_ref[:, : blocks * BLK] = points_ref[...]
+    x_ref[:, blocks * BLK :] = jnp.zeros((16, 2 * BLK), bf16)
+    left_ref[blocks * BLK :, :] = jnp.zeros((2 * BLK, FEAT), bf16)
+
+    @pl.loop(0, blocks // 2)
+    def _(b):
+        at = pl.multiple_of(2 * b * BLK, BLK)
+        left, right = features(split3(widened(scaled(coords_ref[:, pl.ds(at, 2 * BLK)]))))
+        left_ref[pl.ds(at, 2 * BLK), :] = jnp.transpose(left).astype(bf16)
+        right_ref[:, pl.ds(at, 2 * BLK)] = right.astype(bf16)
 
     @pl.loop(0, total)
     def _(b):
-        left, right = features(coords_ref[:, pl.ds(pl.multiple_of(b * BLK, BLK), BLK)])
-        left_ref[pl.ds(pl.multiple_of(b * BLK, BLK), BLK), :] = jnp.transpose(left).astype(bf16)
-        right_ref[:, pl.ds(pl.multiple_of(b * BLK, BLK), BLK)] = right.astype(bf16)
         acc_ref[b] = jnp.zeros((16, BLK), f32)
 
-    leaf_of_lane = lax.broadcasted_iota(jnp.int32, (16, BLK), 1) // LEAF
-
-    def expanded(b):
-        x = points_ref[:, pl.ds(pl.multiple_of(b * BLK, BLK), BLK)]
-        zero = jnp.zeros_like(x)
-        return jnp.concatenate([jnp.where(leaf_of_lane == j, x, zero) for j in range(BL)], axis=0)
-
+    rows = 128
     diagonal = [
-        lax.broadcasted_iota(jnp.int32, (64, BLK), 0) + 64 * c
-        == lax.broadcasted_iota(jnp.int32, (64, BLK), 1)
-        for c in range(BLK // 64)
+        lax.broadcasted_iota(jnp.int32, (rows, BLK), 0) + rows * c
+        == lax.broadcasted_iota(jnp.int32, (rows, BLK), 1)
+        for c in range(BLK // rows)
     ]
 
-    @pl.loop(0, total - 2)
-    def _(i):
-        right = right_ref[:, pl.ds(pl.multiple_of(i * BLK, BLK), BLK)]
-        x_i = expanded(i)
+    def block_x(b):
+        return expanded(x_ref[:, pl.ds(pl.multiple_of(b * BLK, BLK), BLK)])
+
+    def evaluate(n, step, next_ref):
+        right = right_ref[:, pl.ds(pl.multiple_of(n * BLK, BLK), BLK)]
+        for c in range(BLK // rows):
+            left = left_ref[pl.ds(pl.multiple_of((n + step) * BLK, BLK) + rows * c, rows), :]
+            block = matern(jnp.dot(left, right, preferred_element_type=f32))
+            if step == 0:
+                block = block + jnp.where(diagonal[c], nugget, 0.0)
+            next_ref[step, rows * c : rows * c + rows, :] = block.astype(bf16)
+
+    def both(i, kern_ref, n, next_ref):
         acc_i = acc_ref[i]
-        for step in range(3):
-            j = i + step
-            for c in range(BLK // 64):
-                left = left_ref[pl.ds(pl.multiple_of(j * BLK, BLK) + 64 * c, 64), :]
-                block = matern(jnp.dot(left, right, preferred_element_type=f32))
-                if step == 0:
-                    block = block + jnp.where(diagonal[c], nugget, 0.0)
-                kern_ref[step, 64 * c : 64 * c + 64, :] = block.astype(bf16)
+        x_i = block_x(i)
+        weight_i = weight_ref[i]
         for step in range(3):
             j = i + step
             kern = kern_ref[step]
-            x_j = x_i if step == 0 else expanded(j)
-            part = jnp.dot(x_j, kern, preferred_element_type=f32)
-            weight = weight_ref[i]
-            for k in range(BL):
-                row = SPAN + BL * step + k
-                acc_i = acc_i + part[16 * k : 16 * k + 16] * weight[row : row + 1]
+            part = jnp.dot(x_i if step == 0 else block_x(j), kern, preferred_element_type=f32)
             if step:
-                part = lax.dot_general(x_i, kern, (((1,), (1,)), ((), ())), preferred_element_type=f32)
-                weight = weight_ref[j]
-                acc = acc_ref[j]
-                for k in range(BL):
-                    row = SPAN - BL * step + k
-                    acc = acc + part[16 * k : 16 * k + 16] * weight[row : row + 1]
-                acc_ref[j] = acc
+                mirror = lax.dot_general(x_i, kern, (((1,), (1,)), ((), ())), preferred_element_type=f32)
+            evaluate(n, step, next_ref)
+            acc_i = weighed(acc_i, part, weight_i, BL * step)
+            if step:
+                acc_ref[j] = weighed(acc_ref[j], mirror, weight_ref[j], -BL * step)
         acc_ref[i] = acc_i
+
+    for step in range(3):
+        evaluate(0, step, kerns[0])
+
+    @pl.loop(0, blocks // 2)
+    def _(m):
+        both(2 * m, kerns[0], 2 * m + 1, kerns[1])
+        both(2 * m + 1, kerns[1], jnp.minimum(2 * m + 2, blocks - 1), kerns[0])
 
     @pl.loop(0, blocks)
     def _(b):
-        out_ref[:, pl.ds(pl.multiple_of(b * BLK, BLK), BLK)] = acc_ref[b + 2]
-
-
-def near_field(ext_coords, ext_points, near_rel):
+        out_ref[:, pl.ds(pl.multiple_of(b * BLK, BLK), BLK)] = acc_ref[b]
+
+
+def near_field(coords, points, near_rel):
     blocks = LEAF_DEV // BL
-    total = blocks + 4
+    total = blocks + 2
     vmem = pl.BlockSpec(memory_space=pltpu.VMEM)
     return pl.pallas_call(
         functools.partial(near_kernel, blocks),
@@ -166,20 +188,50 @@
         in_specs=[vmem] * 3,
         out_specs=vmem,
         scratch_shapes=[
-            pltpu.VMEM((total * BLK, 32), bf16),
-            pltpu.VMEM((32, total * BLK), bf16),
+            pltpu.VMEM((total * BLK, FEAT), bf16),
+            pltpu.VMEM((FEAT, total * BLK), bf16),
             pltpu.VMEM((total, 32, BLK), f32),
             pltpu.VMEM((total, 16, BLK), f32),
+            pltpu.VMEM((16, total * BLK), bf16),
+            pltpu.VMEM((3, BLK, BLK), bf16),
             pltpu.VMEM((3, BLK, BLK), bf16),
         ],
-        compiler_params=pltpu.CompilerParams(vmem_limit_bytes=48 * 1024 * 1024),
+        compiler_params=pltpu.CompilerParams(vmem_limit_bytes=32 * 1024 * 1024),
         cost_estimate=pl.CostEstimate(flops=2_000_000_000, bytes_accessed=2_000_000, transcendentals=13_000_000),
-    )(ext_coords, ext_points, near_rel)
+    )(coords, points, near_rel)
+
+
+EDGES = ((0, -2, 0), (0, -1, 1), (1, -2, 1), (30, 2, 0), (31, 1, 0), (31, 2, 1))
+
+
+def edge_products(left_halo, right_halo, coords_ref, rel_ref, add):
+    count = slot_counts(rel_ref)
+    halo_rows = []
+    for halo in (left_halo, right_halo):
+        splits = halo[:, SPAN * LEAF :].astype(f32)
+        parts = [widened(splits[3 * k : 3 * k + 3]) for k in range(3)]
+        halo_rows.append(jnp.transpose(features(parts)[0]).astype(bf16))
+    for own in (0, 1, 30, 31):
+        right = features(split3(widened(scaled(coords_ref[:, BLK * own : BLK * own + BLK]))))[1].astype(bf16)
+        weight = spread_counts(count, own)
+        acc = jnp.zeros((16, BLK), f32)
+        for edge_own, offset, at in EDGES:
+            if edge_own == own:
+                side = 0 if offset < 0 else 1
+                halo = (left_halo, right_halo)[side]
+                left = halo_rows[side][BLK * at : BLK * at + BLK]
+                kern = matern(jnp.dot(left, right, preferred_element_type=f32)).astype(bf16)
+                part = jnp.dot(expanded(halo[:, BLK * at : BLK * at + BLK]), kern, preferred_element_type=f32)
+                acc = weighed(acc, part, weight, BL * offset)
+        add(own, acc)
 
 
 TABLE = LEAF_DEV * RANK
 STATE = 256
-WIDTH = TABLE + STATE
+HALO = 2 * SPAN * LEAF
+EDGE = TABLE + STATE
+WIDTH = EDGE + HALO
+FIRST = WIDTH + HALO
 GROUPS = LEAF_DEV // 8
 UPPER = 17
 PARTNERS = (1, 2, 6, 8, 24, 32, 96)
@@ -236,7 +288,7 @@
     )
 
 
-def up_kernel(points_ref, basis_ref, local_ref, pair_ref, couple_ref, payload_ref, ub_ref, bd_ref, bdup_ref, em_ref, sm_ref, rep_ref, x_ref, c_ref, y_ref):
+def up_kernel(bits_ref, points_ref, coords_ref, basis_ref, local_ref, payload_ref, ub_ref, bd_ref, bdup_ref, rep_ref, x_ref, c_ref, y_ref):
     step = pl.program_id(0)
     lanes = iota((8, 256), 1) % 8
     rows = iota((8, 256), 0)
@@ -248,23 +300,6 @@
         perm = where_eq(iota((512, 512), 0), (column % 8) * LEAF + column // 8)
         stacked = jnp.concatenate([points_ref[:, 512 * g : 512 * g + 512] for g in range(GROUPS)], axis=0)
         x_ref[...] = dot(stacked, perm).astype(bf16)
-        fold_row = iota((1024, 128), 0) % RANK
-        fold_col = iota((1024, 128), 1)
-        fold_first = where_eq(fold_row, fold_col)
-        fold_second = where_eq(fold_row + RANK, fold_col)
-        own = iota((RANK, 1024), 1) // RANK == iota((RANK, 1024), 0)
-        pairs = pair_ref[...].astype(f32)
-        couples = couple_ref[...].astype(f32)
-
-        def opened(values, k):
-            return jnp.where(own, values[k : k + 1, :], 0.0).astype(bf16)
-
-        em_ref[...] = dot(jnp.concatenate([opened(pairs, k) for k in range(10)], axis=0), fold_first).astype(bf16)
-        sm_ref[...] = (
-            dot(jnp.concatenate([opened(couples, 2 * k) for k in range(6)], axis=0), fold_first)
-            + dot(jnp.concatenate([opened(couples, 2 * k + 1) for k in range(6)], axis=0), fold_second)
-        ).astype(bf16)
-
     basis = basis_ref[...]
     wide = dot(jnp.concatenate([basis[:, 128 * k : 128 * k + 128] for k in range(16)], axis=0), rep_ref[...])
     keep = lanes == rows
@@ -315,7 +350,49 @@
         squeeze = where_eq(iota((256, 128), 0), iota((256, 128), 1) * 8)
         mine = joined(dot(halves(current[0]), squeeze))
         zero = jnp.zeros_like(mine)
-        payload_ref[:, TABLE:] = pack_state(mine, zero, zero)
+        payload_ref[:, TABLE:EDGE] = pack_state(mine, zero, zero)
+        head = side(points_ref, coords_ref, 0)
+        tail = side(points_ref, coords_ref, (LEAF_DEV - SPAN) * LEAF)
+        even = bits_ref[0] == 0
+        payload_ref[:, EDGE:WIDTH] = jnp.where(even, tail, head)
+        payload_ref[:, WIDTH:] = jnp.where(even, head, tail)
+
+
+def side(points_ref, coords_ref, start):
+    end = start + SPAN * LEAF
+    parts = split3(scaled(coords_ref[:, start:end]))
+    rows = jnp.concatenate(list(parts) + [jnp.zeros((7, SPAN * LEAF), f32)], axis=0)
+    return jnp.concatenate([points_ref[:, start:end], rows.astype(bf16)], axis=1)
+
+
+def open_kernel(pair_ref, couple_ref, em_ref, sm_ref):
+    fold_row = iota((1024, 128), 0) % RANK
+    fold_col = iota((1024, 128), 1)
+    fold_first = where_eq(fold_row, fold_col)
+    fold_second = where_eq(fold_row + RANK, fold_col)
+    own = iota((RANK, 1024), 1) // RANK == iota((RANK, 1024), 0)
+    pairs = pair_ref[...].astype(f32)
+    couples = couple_ref[...].astype(f32)
+
+    def opened(values, k):
+        return jnp.where(own, values[k : k + 1, :], 0.0).astype(bf16)
+
+    em_ref[...] = dot(jnp.concatenate([opened(pairs, k) for k in range(10)], axis=0), fold_first).astype(bf16)
+    sm_ref[...] = (
+        dot(jnp.concatenate([opened(couples, 2 * k) for k in range(6)], axis=0), fold_first)
+        + dot(jnp.concatenate([opened(couples, 2 * k + 1) for k in range(6)], axis=0), fold_second)
+    ).astype(bf16)
+
+
+def opened_top(pairs, couples):
+    vmem = pl.BlockSpec(memory_space=pltpu.VMEM)
+    return pl.pallas_call(
+        open_kernel,
+        out_shape=(jax.ShapeDtypeStruct((320, 128), bf16), jax.ShapeDtypeStruct((192, 128), bf16)),
+        in_specs=[vmem] * 2,
+        out_specs=(vmem, vmem),
+        cost_estimate=pl.CostEstimate(flops=1_000_000, bytes_accessed=400_000, transcendentals=0),
+    )(pairs, couples)
 
 
 def fill_upper(y_ref, bdup_ref, target, tile, keep):
@@ -327,33 +404,29 @@
         bdup_ref[target, 8 * a : 8 * a + 16, :] = jnp.concatenate(both, axis=0).astype(bf16)
 
 
-def upward(points, basis, local_transfer, pairs, couples):
+def upward(bits, points, coords, basis, local_transfer):
     full = lambda *shape: pl.BlockSpec(shape, lambda i: (0,) * len(shape))
     return pl.pallas_call(
         up_kernel,
         grid=(GROUPS // 2,),
         out_shape=(
-            jax.ShapeDtypeStruct((16, WIDTH), bf16),
+            jax.ShapeDtypeStruct((16, FIRST), bf16),
             jax.ShapeDtypeStruct((GROUPS, 512, 256), bf16),
             jax.ShapeDtypeStruct((GROUPS, 256, 256), bf16),
             jax.ShapeDtypeStruct((UPPER, 256, 256), bf16),
-            jax.ShapeDtypeStruct((320, 128), bf16),
-            jax.ShapeDtypeStruct((192, 128), bf16),
         ),
         in_specs=[
+            pl.BlockSpec(memory_space=pltpu.SMEM),
             full(16, LEAF_DEV * LEAF),
+            full(3, LEAF_DEV * LEAF),
             pl.BlockSpec((16, LEAF * RANK), lambda i: (i, 0)),
             full(254, 1024),
-            full(10, 1024),
-            full(12, 1024),
         ],
         out_specs=(
-            full(16, WIDTH),
+            full(16, FIRST),
             pl.BlockSpec((2, 512, 256), lambda i: (i, 0, 0)),
             pl.BlockSpec((2, 256, 256), lambda i: (i, 0, 0)),
             full(UPPER, 256, 256),
-            full(320, 128),
-            full(192, 128),
         ),
         scratch_shapes=[
             pltpu.VMEM((128, 1024), bf16),
@@ -363,14 +436,16 @@
         ],
         compiler_params=pltpu.CompilerParams(vmem_limit_bytes=48 * 1024 * 1024),
         cost_estimate=pl.CostEstimate(flops=1_000_000_000, bytes_accessed=10_000_000, transcendentals=0),
-    )(points, basis, local_transfer, pairs, couples)
+    )(bits, points, coords, basis, local_transfer)
 
 
 def step_kernel(height, bits_ref, first_ref, payload_ref, received_ref, em_ref, next_ref):
     forward = height % 2 == 1
     next_ref[:, :TABLE] = received_ref[:, :TABLE] if forward else first_ref[:, :TABLE]
-    mine, _, _ = unpack_state(payload_ref[:, TABLE:])
-    sibling, _, _ = unpack_state(received_ref[:, TABLE:])
+    start = WIDTH if height == 0 else EDGE
+    next_ref[:, EDGE:] = payload_ref[:, EDGE:WIDTH] if forward else received_ref[:, start : start + HALO]
+    mine, _, _ = unpack_state(payload_ref[:, TABLE:EDGE])
+    sibling, _, _ = unpack_state(received_ref[:, TABLE:EDGE])
     if height <= 4:
         first = bits_ref[height] == 0
         left = jnp.where(first, mine, sibling)
@@ -379,7 +454,7 @@
         parent = joined(dot(halves(both), em_ref[64 * height : 64 * height + 64, :]))
     else:
         parent = jnp.zeros_like(mine)
-    next_ref[:, TABLE:] = pack_state(parent, mine, sibling)
+    next_ref[:, TABLE:EDGE] = pack_state(parent, mine, sibling)
 
 
 def tree_step(height, bits, first, payload, received, em):
@@ -435,7 +510,7 @@
 
 def down_kernel(bits_ref, index_ref, payload_ref, *refs):
     received = refs[:7]
-    em_ref, sm_ref, bdup_ref, d_ref, ub_ref, bd_ref, near_ref, out_ref, table_ref, field_ref, far_ref, gather_ref = refs[7:]
+    em_ref, sm_ref, bdup_ref, coords_ref, rel_ref, d_ref, ub_ref, bd_ref, near_ref, out_ref, table_ref, field_ref, far_ref, gather_ref, edge_ref = refs[7:]
     step = pl.program_id(0)
 
     @pl.when(step == 0)
@@ -450,7 +525,7 @@
         table_ref[16384:16400, :] = jnp.zeros((16, 128), bf16)
         terms = []
         for height in range(1, 7):
-            _, before_mine, before_sibling = unpack_state(received[height][:, TABLE:])
+            _, before_mine, before_sibling = unpack_state(received[height][:, TABLE:EDGE])
             plain = (bits_ref[height - 1] == 0) == (height % 2 == 1)
             left = jnp.where(plain, before_mine, before_sibling)
             right = jnp.where(plain, before_sibling, before_mine)
@@ -470,6 +545,18 @@
                 joined(dot_nt(halves(fields[q // 2 if level_tiles > 1 else 0]), bdup_ref[tile + q]))
                 for q in range(level_tiles)
             ]
+        near_side = received[0][:, EDGE:WIDTH]
+        far_side = received[1][:, EDGE:WIDTH]
+        for height in range(2, 7):
+            far_side = jnp.where(bits_ref[7] == height, received[height][:, EDGE:WIDTH], far_side)
+        even = bits_ref[0] == 0
+        left_halo = jnp.where(even, far_side, near_side)
+        right_halo = jnp.where(even, near_side, far_side)
+
+        def add(own, acc):
+            edge_ref[own % 4] = acc
+
+        edge_products(left_halo, right_halo, coords_ref, rel_ref, add)
         for q in range(8):
             field_ref[32 * q : 32 * q + 32, :] = halves(fields[q])
 
@@ -500,10 +587,15 @@
         perm = where_eq(iota((512, 512), 0), (column % LEAF) * 8 + column // LEAF)
         whole = joined(dot(far_ref[...], perm))
         for g in range(GROUPS):
-            out_ref[:, 512 * g : 512 * g + 512] = near_ref[:, 512 * g : 512 * g + 512] + whole[16 * g : 16 * g + 16, :]
-
-
-def downward(bits, index, payload, received, em, sm, bdup, d, ub, bd, near):
+            value = near_ref[:, 512 * g : 512 * g + 512] + whole[16 * g : 16 * g + 16, :]
+            if g == 0:
+                value = value + jnp.concatenate([edge_ref[0], edge_ref[1]], axis=1)
+            if g == GROUPS - 1:
+                value = value + jnp.concatenate([edge_ref[2], edge_ref[3]], axis=1)
+            out_ref[:, 512 * g : 512 * g + 512] = value
+
+
+def downward(bits, index, payload, received, em, sm, bdup, coords, near_rel, d, ub, bd, near):
     full = lambda *shape: pl.BlockSpec(shape, lambda i: (0,) * len(shape))
     smem = pl.BlockSpec(memory_space=pltpu.SMEM)
     each = lambda *shape: pl.BlockSpec((1,) + shape, lambda i: (i, 0, 0))
@@ -512,8 +604,10 @@
         grid=(GROUPS,),
         out_shape=jax.ShapeDtypeStruct((16, LEAF_DEV * LEAF), f32),
         in_specs=[smem, smem]
-        + [full(16, WIDTH)] * 8
+        + [full(16, FIRST)] * 2
+        + [full(16, WIDTH)] * 6
         + [full(320, 128), full(192, 128), full(UPPER, 256, 256)]
+        + [full(3, LEAF_DEV * LEAF), full(NN, LEAF_DEV)]
         + [each(256, 512), each(512, 256), each(256, 256), full(16, LEAF_DEV * LEAF)],
         out_specs=full(16, LEAF_DEV * LEAF),
         scratch_shapes=[
@@ -521,10 +615,11 @@
             pltpu.VMEM((256, 256), bf16),
             pltpu.VMEM((512, 512), bf16),
             pltpu.VMEM((128, 512), bf16),
+            pltpu.VMEM((4, 16, BLK), f32),
         ],
         compiler_params=pltpu.CompilerParams(vmem_limit_bytes=48 * 1024 * 1024),
         cost_estimate=pl.CostEstimate(flops=3_000_000_000, bytes_accessed=16_000_000, transcendentals=0),
-    )(bits, index, payload, *received, em, sm, bdup, d, ub, bd, near)
+    )(bits, index, payload, *received, em, sm, bdup, coords, near_rel, d, ub, bd, near)
 
 
 def top_start(height, number):
@@ -545,7 +640,10 @@
     top_coupling,
 ):
     device = lax.axis_index("leaf")
-    bits = jnp.right_shift(device, jnp.arange(8, dtype=jnp.int32)) & 1
+    outer = jnp.bitwise_xor(device, device + 2 * (device & 1) - 1)
+    level = sum((outer >> k > 0).astype(jnp.int32) for k in range(7)) - 1
+    number = jnp.arange(8, dtype=jnp.int32)
+    bits = jnp.where(number == 7, jnp.maximum(level, 1), jnp.right_shift(device, number) & 1)
     starts = jnp.array([top_start(h, N_DEV) for h in range(6)], jnp.int32)
     heights = jnp.arange(6, dtype=jnp.int32)
     nodes = starts + jnp.right_shift(device, heights)
@@ -558,7 +656,8 @@
     within = far_list & (LEAF_DEV - 1)
     entry = slot * LEAF_DEV + (within & 7) * GROUPS + (within >> 3)
     index = jnp.where(far_list >= 0, entry, 8 * LEAF_DEV).reshape(LEAF_DEV * NF)
-    payload, ub, bd, bdup, em, sm = upward(points, basis, local_transfer, pairs, couples)
+    payload, ub, bd, bdup = upward(bits, points, coords, basis, local_transfer)
+    em, sm = opened_top(pairs, couples)
     first = payload
     received = []
     for height, mask in enumerate(PARTNERS):
@@ -566,12 +665,10 @@
         received.append(lax.ppermute(payload, "leaf", route))
         if height < 6:
             payload = tree_step(height, bits, first, payload, received[height], em)
-    ext_points = padded(points, (("leaf", 1),), SPAN * LEAF)
-    ext_coords = padded(coords, (("leaf", 1),), SPAN * LEAF)
     near_rel = jnp.transpose(jnp.where(near_list >= 0, near_list - device * LEAF_DEV, -1000))
-    near_part = near_field(ext_coords, ext_points, near_rel)
+    near_part = near_field(coords, points, near_rel)
     d = regroup(far_coupling)
-    return downward(bits, index, first, received, em, sm, bdup, d, ub, bd, near_part)
+    return downward(bits, index, first, received, em, sm, bdup, coords, near_rel, d, ub, bd, near_part)
 
 
 def solution(mesh):

time: 142 us -> 126 us (0.89)
  starting transfers between devices: 30.2 us -> 15 us
  waiting for transfers between devices: 8.67 us -> 17.6 us
  Pallas kernels: 75.8 us -> 67.9 us
    pallas_call x1, Pallas kernels: 27 us -> 14.5 us  [near_field(): pl.pallas_call(functools.partial(near_kernel, blocks), out_shape=jax.Shap...]
    ppermute x7, waiting for transfers between devices: 8.66 us -> 17.6 us  [per_device(): received.append(lax.ppermute(payload, 'leaf', route))]
    ppermute x4 -> x0, starting transfers between devices: 7.67 us -> none  [the longest x2 5.11 us: padded(): lax.ppermute(tail, axis, [(i, (i + 1) % count) for i in range(ends)])]
    ppermute x7, starting transfers between devices: 22.6 us -> 15 us  [per_device(): received.append(lax.ppermute(payload, 'leaf', route))]
    slice x2 -> x0, local copies, waits for them, and re-layouts: 2.7 us -> none  [padded(): lax.slice_in_dim(cells, cells.shape[dim] - width, cells.shape[dim], axis=...]
    concatenate x2 -> x0, other arithmetic: 2.66 us -> none  [padded(): jnp.concatenate([lax.ppermute(tail, axis, [(i, (i + 1) % count) for i in...]
    pallas_call x1, Pallas kernels: 17.3 us -> 19.4 us  [downward(): pl.pallas_call(down_kernel, grid=(GROUPS,), out_shape=jax.ShapeDtypeStruc...]
    pallas_call x0 -> x1, Pallas kernels: none -> 1.94 us  [opened_top(): pl.pallas_call(open_kernel, out_shape=(jax.ShapeDtypeStruct((320, 128), b...]
  transfers between devices with their start and end apart: 11 -> 7, of which waited for: 3 -> 4; matrix products, arithmetic and copies ran while one was open for 5% -> 8% of each run, Pallas kernels for 34% -> 21%
where the time goes in v3:
time: 126 us; the launch traced here: 125 us
  Pallas kernels  67.9 us (54%)
  local copies, waits for them, and re-layouts  20.3 us (16%)
  waiting for transfers between devices  17.6 us (14%)
  starting transfers between devices  15 us (12%)
  other arithmetic  3.75 us (3%)
    pallas_call x1, Pallas kernels, downward(): pl.pallas_call(down_kernel, grid=(GROUPS,), out_shape=jax.ShapeDtypeStruc...  19.4 us
    ppermute x7, waiting for transfers between devices, per_device(): received.append(lax.ppermute(payload, 'leaf', route))  17.6 us
    ppermute x7, starting transfers between devices, per_device(): received.append(lax.ppermute(payload, 'leaf', route))  15 us
    unnamed x60, local copies, waits for them, and re-layouts  14.6 us
    pallas_call x1, Pallas kernels, near_field(): pl.pallas_call(functools.partial(near_kernel, blocks), out_shape=jax.Shap...  14.5 us
    pallas_call x6, Pallas kernels, tree_step(): pl.pallas_call(functools.partial(step_kernel, height), out_shape=jax.Shap...  12.9 us
    pallas_call x1, Pallas kernels, regroup(): pl.pallas_call(regroup_kernel, grid=(GROUPS,), out_shape=jax.ShapeDtypeSt...  10.3 us
    pallas_call x1, Pallas kernels, upward(): pl.pallas_call(up_kernel, grid=(GROUPS // 2,), out_shape=(jax.ShapeDtypeS...  8.84 us
  transfers between devices with their start and end apart: 7, of which 4 were waited for; matrix products, arithmetic and copies ran while one was open for 8% of the time, Pallas kernels for 21%

profile of v3, /device:TPU:0, one launch (start us, length us, event | category | flops | bytes accessed | tf_op | source)
XLA Modules:
  0.0 124.9 jit_solution(2305225527472535096)
XLA Ops:
  0.0 0.0 copy-start.19
  0.0 1.0 copy-done.19
  1.0 1.0 copy-done.24
  2.0 1.0 copy-done.25
  3.1 0.9 copy-done.26
  4.0 8.8 %shard_map.100 = (bf16[16,6400]{1,0:T(8,128)(2,1)S(1)}, bf16[16,512,256]{2,1,0:T(8,128)(2,1)}, bf16[16,256,256]{2,1,0:T(8,128)(2,1)S(1)}, bf16[17,256,256]{2,1,0:T(8,128)(2,1)S(1)}) custom-call(s32[8]{0:T(128)S(1)} %compare_select_fusion.2.bits_ref, bf16[16,8192]{1,0:T(8,128)(2,1)S(1)} %copy-done.26, f32[3,8192]{1,0:T(4,128)S(1)} %copy-done.19, ...), custom_call_target="tpu_custom_call" | custom-call | flops 1000000000 | bytes 10000000 | tf_op jit(solution)/shard_map/pallas_call | solution.py:409
  12.9 1.4 %copy-done.6 = bf16[17,256,256]{2,1,0:T(8,128)(2,1)} copy-done((bf16[17,256,256]{2,1,0:T(8,128)(2,1)}, bf16[17,256,256]{2,1,0:T(8,128)(2,1)S(1)}, u32[]{:S(2)}) %copy-start.6) | copy-done | bytes 2228248
  14.3 1.2 compare_select_fusion
  15.5 0.1 iota_add_fusion
  15.6 0.7 add.109
  16.2 1.2 fusion
  17.4 0.6 pad_clamp_fusion
  18.1 1.2 gather_fusion.1
  19.3 1.4 %reshape.38.couple_ref = bf16[12,1024]{1,0:T(8,128)(2,1)} reshape(bf16[6,2,1024]{2,1,0:T(2,128)(2,1)} %gather_fusion.1) | data formatting | bytes 49152 | tf_op jit(solution)/shard_map/reshape | solution.py:653
  20.6 0.6 pad_clamp_fusion.1
  21.2 2.3 %gather_fusion = bf16[10,1024]{1,0:T(8,128)(2,1)} fusion(bf16[254,1024]{1,0:T(8,128)(2,1)} %param.17, s32[1024]{0:T(1024)S(1)} %pad_clamp_fusion.1), kind=kCustom, calls=%fused_computation | custom fusion | bytes 41000 | tf_op jit(solution)/shard_map/gather | solution.py:652
  23.5 1.9 %shard_map.101 = (bf16[320,128]{1,0:T(8,128)(2,1)}, bf16[192,128]{1,0:T(8,128)(2,1)}) custom-call(bf16[10,1024]{1,0:T(8,128)(2,1)} %gather_fusion, bf16[12,1024]{1,0:T(8,128)(2,1)} %reshape.38.couple_ref), custom_call_target="tpu_custom_call" | custom-call | flops 1000000 | bytes 400000 | tf_op jit(solution)/shard_map/pallas_call | solution.py:389
  25.5 0.0 collective-permute-done.received_ref.refs_0_
  25.5 0.7 copy-done.7
  26.1 2.2 %shard_map.102.payload_ref = bf16[16,5376]{1,0:T(8,128)(2,1)} custom-call(s32[8]{0:T(128)} %copy-done.22, bf16[16,6400]{1,0:T(8,128)(2,1)} %copy-done.2, bf16[16,6400]{1,0:T(8,128)(2,1)} %copy-done.2, bf16[16,6400]{1,0:T(8,128)(2,1)} %copy-done.7, bf16[320,128]{1,0:T(8,128)(2,1)} %get-tuple-element.12.em_ref.refs_7_), custom_call_target="tpu_custom_call" | custom-call | flops 1000000 | bytes 400000 | tf_op jit(solution)/shard_map/pallas_call | solution.py:462
  28.4 1.7 %collective-permute-start.1 = (bf16[16,5376]{1,0:T(8,128)(2,1)}, bf16[16,5376]{1,0:T(8,128)(2,1)S(1)}, u32[]{:S(2)}, u32[]{:S(2)}) collective-permute-start(bf16[16,5376]{1,0:T(8,128)(2,1)} %shard_map.102.payload_ref), channel_id=1, source_target_pairs={{0,2},{1,3},{2,0},{3,1},{4,6},{5,7},{6,4},{7,5},{8,10},{9,11},{10,... | collective-permute-start | bytes 516104 | tf_op jit(solution)/shard_map/ppermute | solution.py:665
  30.0 5.3 %collective-permute-done.1.received_ref.refs_1_ = bf16[16,5376]{1,0:T(8,128)(2,1)S(1)} collective-permute-done((bf16[16,5376]{1,0:T(8,128)(2,1)}, bf16[16,5376]{1,0:T(8,128)(2,1)S(1)}, u32[]{:S(2)}, u32[]{:S(2)}) %collective-permute-start.1) | collective-permute-done | bytes 172064 | tf_op jit(solution)/shard_map/ppermute | solution.py:665
  35.3 0.7 copy-done.9
  36.0 2.2 %shard_map.103.payload_ref = bf16[16,5376]{1,0:T(8,128)(2,1)} custom-call(s32[8]{0:T(128)} %copy-done.22, bf16[16,6400]{1,0:T(8,128)(2,1)} %copy-done.2, bf16[16,5376]{1,0:T(8,128)(2,1)} %shard_map.102.payload_ref, bf16[16,5376]{1,0:T(8,128)(2,1)} %copy-done.9, bf16[320,128]{1,0:T(8,128)(2,1)} %get-tuple-element.12.em_ref.refs_7_), custom_call_target="tpu_custom_call" | custom-call | flops 1000000 | bytes 400000 | tf_op jit(solution)/shard_map/pallas_call | solution.py:462
  38.2 3.1 %collective-permute-start.2 = (bf16[16,5376]{1,0:T(8,128)(2,1)}, bf16[16,5376]{1,0:T(8,128)(2,1)S(1)}, u32[]{:S(2)}, u32[]{:S(2)}) collective-permute-start(bf16[16,5376]{1,0:T(8,128)(2,1)} %shard_map.103.payload_ref), channel_id=1, source_target_pairs={{0,6},{1,7},{2,4},{3,5},{4,2},{5,3},{6,0},{7,1},{8,14},{9,15},{10,... | collective-permute-start | bytes 516104 | tf_op jit(solution)/shard_map/ppermute | solution.py:665
  41.3 4.5 %collective-permute-done.2.received_ref.refs_2_ = bf16[16,5376]{1,0:T(8,128)(2,1)S(1)} collective-permute-done((bf16[16,5376]{1,0:T(8,128)(2,1)}, bf16[16,5376]{1,0:T(8,128)(2,1)S(1)}, u32[]{:S(2)}, u32[]{:S(2)}) %collective-permute-start.2) | collective-permute-done | bytes 172064 | tf_op jit(solution)/shard_map/ppermute | solution.py:665
  45.7 0.7 copy-done.11
  46.4 2.2 %shard_map.104.payload_ref = bf16[16,5376]{1,0:T(8,128)(2,1)} custom-call(s32[8]{0:T(128)} %copy-done.22, bf16[16,6400]{1,0:T(8,128)(2,1)} %copy-done.2, bf16[16,5376]{1,0:T(8,128)(2,1)} %shard_map.103.payload_ref, bf16[16,5376]{1,0:T(8,128)(2,1)} %copy-done.11, bf16[320,128]{1,0:T(8,128)(2,1)} %get-tuple-element.12.em_ref.refs_7_), custom_call_target="tpu_custom_call" | custom-call | flops 1000000 | bytes 400000 | tf_op jit(solution)/shard_map/pallas_call | solution.py:462
  48.6 1.9 %collective-permute-start.3 = (bf16[16,5376]{1,0:T(8,128)(2,1)}, bf16[16,5376]{1,0:T(8,128)(2,1)S(1)}, u32[]{:S(2)}, u32[]{:S(2)}) collective-permute-start(bf16[16,5376]{1,0:T(8,128)(2,1)} %shard_map.104.payload_ref), channel_id=1, source_target_pairs={{0,8},{1,9},{2,10},{3,11},{4,12},{5,13},{6,14},{7,15},{8,0},{9,1},... | collective-permute-start | bytes 516104 | tf_op jit(solution)/shard_map/ppermute | solution.py:665
  50.5 3.7 %collective-permute-done.3.received_ref.refs_3_ = bf16[16,5376]{1,0:T(8,128)(2,1)S(1)} collective-permute-done((bf16[16,5376]{1,0:T(8,128)(2,1)}, bf16[16,5376]{1,0:T(8,128)(2,1)S(1)}, u32[]{:S(2)}, u32[]{:S(2)}) %collective-permute-start.3) | collective-permute-done | bytes 172064 | tf_op jit(solution)/shard_map/ppermute | solution.py:665
  54.2 0.7 copy-done.13
  54.8 2.2 %shard_map.105.payload_ref = bf16[16,5376]{1,0:T(8,128)(2,1)} custom-call(s32[8]{0:T(128)} %copy-done.22, bf16[16,6400]{1,0:T(8,128)(2,1)} %copy-done.2, bf16[16,5376]{1,0:T(8,128)(2,1)} %shard_map.104.payload_ref, bf16[16,5376]{1,0:T(8,128)(2,1)} %copy-done.13, bf16[320,128]{1,0:T(8,128)(2,1)} %get-tuple-element.12.em_ref.refs_7_), custom_call_target="tpu_custom_call" | custom-call | flops 1000000 | bytes 400000 | tf_op jit(solution)/shard_map/pallas_call | solution.py:462
  57.0 4.0 %collective-permute-start.4 = (bf16[16,5376]{1,0:T(8,128)(2,1)}, bf16[16,5376]{1,0:T(8,128)(2,1)S(1)}, u32[]{:S(2)}, u32[]{:S(2)}) collective-permute-start(bf16[16,5376]{1,0:T(8,128)(2,1)} %shard_map.105.payload_ref), channel_id=1, source_target_pairs={{0,24},{1,25},{2,26},{3,27},{4,28},{5,29},{6,30},{7,31},{8,16},{9,... | collective-permute-start | bytes 516104 | tf_op jit(solution)/shard_map/ppermute | solution.py:665
  61.1 0.1 copy.11
  61.2 0.1 reshape.37.index_ref
  61.3 2.2 %copy-done.4 = bf16[128,16,1024]{2,1,0:T(8,128)(2,1)S(1)} copy-done((bf16[128,16,1024]{2,1,0:T(8,128)(2,1)S(1)}, bf16[128,16,1024]{2,1,0:T(8,128)(2,1)}, u32[]{:S(2)}) %copy-start.4) | copy-done | bytes 4194328
  63.5 10.3 %shard_map.108.refs_12_ = bf16[16,256,512]{2,1,0:T(8,128)(2,1)S(1)} custom-call(bf16[128,16,1024]{2,1,0:T(8,128)(2,1)S(1)} %copy-done.4), custom_call_target="tpu_custom_call" | custom-call | flops 30000000 | bytes 8400000 | tf_op jit(solution)/shard_map/pallas_call | solution.py:499
  73.8 2.0 %copy-done.1 = bf16[16,256,512]{2,1,0:T(8,128)(2,1)} copy-done((bf16[16,256,512]{2,1,0:T(8,128)(2,1)}, bf16[16,256,512]{2,1,0:T(8,128)(2,1)S(1)}, u32[]{:S(2)}) %copy-start.1) | copy-done | bytes 4194328
  75.8 0.7 copy-done.15
  76.5 2.2 %shard_map.106.payload_ref = bf16[16,5376]{1,0:T(8,128)(2,1)} custom-call(s32[8]{0:T(128)} %copy-done.22, bf16[16,6400]{1,0:T(8,128)(2,1)} %copy-done.2, bf16[16,5376]{1,0:T(8,128)(2,1)} %shard_map.105.payload_ref, bf16[16,5376]{1,0:T(8,128)(2,1)} %copy-done.15, bf16[320,128]{1,0:T(8,128)(2,1)} %get-tuple-element.12.em_ref.refs_7_), custom_call_target="tpu_custom_call" | custom-call | flops 1000000 | bytes 400000 | tf_op jit(solution)/shard_map/pallas_call | solution.py:462
  78.7 1.5 %collective-permute-start.5 = (bf16[16,5376]{1,0:T(8,128)(2,1)}, bf16[16,5376]{1,0:T(8,128)(2,1)S(1)}, u32[]{:S(2)}, u32[]{:S(2)}) collective-permute-start(bf16[16,5376]{1,0:T(8,128)(2,1)} %shard_map.106.payload_ref), channel_id=1, source_target_pairs={{0,32},{1,33},{2,34},{3,35},{4,36},{5,37},{6,38},{7,39},{8,40},{9,... | collective-permute-start | bytes 516104 | tf_op jit(solution)/shard_map/ppermute | solution.py:665
  80.2 4.1 %collective-permute-done.5.received_ref.refs_5_ = bf16[16,5376]{1,0:T(8,128)(2,1)S(1)} collective-permute-done((bf16[16,5376]{1,0:T(8,128)(2,1)}, bf16[16,5376]{1,0:T(8,128)(2,1)S(1)}, u32[]{:S(2)}, u32[]{:S(2)}) %collective-permute-start.5) | collective-permute-done | bytes 172064 | tf_op jit(solution)/shard_map/ppermute | solution.py:665
  84.3 0.7 copy-done.17
  85.0 2.0 %shard_map.107 = bf16[16,5376]{1,0:T(8,128)(2,1)} custom-call(s32[8]{0:T(128)} %copy-done.22, bf16[16,6400]{1,0:T(8,128)(2,1)} %copy-done.2, bf16[16,5376]{1,0:T(8,128)(2,1)} %shard_map.106.payload_ref, bf16[16,5376]{1,0:T(8,128)(2,1)} %copy-done.17, bf16[320,128]{1,0:T(8,128)(2,1)} %get-tuple-element.12.em_ref.refs_7_), custom_call_target="tpu_custom_call" | custom-call | flops 1000000 | bytes 400000 | tf_op jit(solution)/shard_map/pallas_call | solution.py:462
  87.1 2.8 %collective-permute-start.6 = (bf16[16,5376]{1,0:T(8,128)(2,1)}, bf16[16,5376]{1,0:T(8,128)(2,1)S(1)}, u32[]{:S(2)}, u32[]{:S(2)}) collective-permute-start(bf16[16,5376]{1,0:T(8,128)(2,1)} %shard_map.107), channel_id=1, source_target_pairs={{0,96},{1,97},{2,98},{3,99},{4,100},{5,101},{6,102},{7,103},{8,104... | collective-permute-start | bytes 516104 | tf_op jit(solution)/shard_map/ppermute | solution.py:665
  89.9 0.9 copy-done.27
  90.9 14.5 %shard_map.109.refs_15_ = f32[16,8192]{1,0:T(8,128)S(1)} custom-call(f32[3,8192]{1,0:T(4,128)S(1)} %copy-done.20, bf16[16,8192]{1,0:T(8,128)(2,1)S(1)} %copy-done.27, s32[12,128]{1,0:T(8,128)S(1)} %select_bitcast_fusion.rel_ref.refs_11_), custom_call_target="tpu_custom_call" | custom-call | flops 2000000000 | bytes 2000000 | tf_op jit(solution)/shard_map/pallas_call | solution.py:185
  105.4 19.4 %shard_map.110 = f32[16,8192]{1,0:T(8,128)} custom-call(s32[8]{0:T(128)S(1)} %copy-done.23, s32[2048]{0:T(1024)S(1)} %reshape.37.index_ref, bf16[16,6400]{1,0:T(8,128)(2,1)S(1)} %copy-done.3, bf16[16,6400]{1,0:T(8,128)(2,1)S(1)} %copy-done.8, bf16[16,5376]{1,0:T(8,128)(2,1)S(1)} %copy-done.10, bf16[16,5376]{1,0:T(8,128)(2,1)S(1)} %copy-done.12, ...), custom_call_target="tpu_custom_call" | custom-call | flops 3000000000 | bytes 16000000 | tf_op jit(solution)/shard_map/pallas_call | solution.py:602
  (51 shorter events, 0.1 us)
Async XLA Ops:
  0.0 18.1 %copy-start = (bf16[252,2,1024]{2,1,0:T(2,128)(2,1)S(1)}, bf16[252,2,1024]{2,1,0:T(2,128)(2,1)}, u32[]{:S(2)}) copy-start(bf16[252,2,1024]{2,1,0:T(2,128)(2,1)} %param.18) | copy-start | bytes 3096580
  0.0 61.1 %copy-start.28 = (s32[128,16]{0,1:T(8,128)S(1)}, s32[128,16]{0,1:T(8,128)}, u32[]{:S(2)}) copy-start(s32[128,16]{0,1:T(8,128)} %param.13) | copy-start | bytes 24580
  0.0 1.0 copy-start.19
  1.0 1.0 copy-start.24
  2.0 1.0 copy-start.25
  3.1 0.9 copy-start.26
  4.0 21.4 %copy-start.22 = (s32[8]{0:T(128)}, s32[8]{0:T(128)S(1)}, u32[]{:S(2)}) copy-start(s32[8]{0:T(128)S(1)} %compare_select_fusion.2.bits_ref) | copy-start | bytes 100
  12.9 1.4 %copy-start.6 = (bf16[17,256,256]{2,1,0:T(8,128)(2,1)}, bf16[17,256,256]{2,1,0:T(8,128)(2,1)S(1)}, u32[]{:S(2)}) copy-start(bf16[17,256,256]{2,1,0:T(8,128)(2,1)S(1)} %get-tuple-element.14.refs_9_) | copy-start | bytes 6684676
  14.3 11.2 %copy-start.2 = (bf16[16,6400]{1,0:T(8,128)(2,1)}, bf16[16,6400]{1,0:T(8,128)(2,1)S(1)}, u32[]{:S(2)}) copy-start(bf16[16,6400]{1,0:T(8,128)(2,1)S(1)} %get-tuple-element.11.first_ref.payload_ref) | copy-start | bytes 614404
  14.3 11.2 %collective-permute-start = (bf16[16,6400]{1,0:T(8,128)(2,1)S(1)}, bf16[16,6400]{1,0:T(8,128)(2,1)S(1)}, u32[]{:S(2)}, u32[]{:S(2)}) collective-permute-start(bf16[16,6400]{1,0:T(8,128)(2,1)S(1)} %get-tuple-element.11.first_ref.payload_ref), channel_id=1, source_target_pairs={{0,1},{1,0},{2,3},{3,2},{4,5},{5,4},{6,7},{7,6},{8,9},{9,8},{10,11... | collective-permute-start | bytes 614408 | tf_op jit(solution)/shard_map/ppermute | solution.py:665
  25.5 0.7 copy-start.7
  28.4 7.0 %collective-permute-start.1 = (bf16[16,5376]{1,0:T(8,128)(2,1)}, bf16[16,5376]{1,0:T(8,128)(2,1)S(1)}, u32[]{:S(2)}, u32[]{:S(2)}) collective-permute-start(bf16[16,5376]{1,0:T(8,128)(2,1)} %shard_map.102.payload_ref), channel_id=1, source_target_pairs={{0,2},{1,3},{2,0},{3,1},{4,6},{5,7},{6,4},{7,5},{8,10},{9,11},{10,... | collective-permute-start | bytes 516104 | tf_op jit(solution)/shard_map/ppermute | solution.py:665
  35.3 0.7 copy-start.9
  38.2 7.5 %collective-permute-start.2 = (bf16[16,5376]{1,0:T(8,128)(2,1)}, bf16[16,5376]{1,0:T(8,128)(2,1)S(1)}, u32[]{:S(2)}, u32[]{:S(2)}) collective-permute-start(bf16[16,5376]{1,0:T(8,128)(2,1)} %shard_map.103.payload_ref), channel_id=1, source_target_pairs={{0,6},{1,7},{2,4},{3,5},{4,2},{5,3},{6,0},{7,1},{8,14},{9,15},{10,... | collective-permute-start | bytes 516104 | tf_op jit(solution)/shard_map/ppermute | solution.py:665
  45.7 0.7 copy-start.11
  48.6 5.6 %collective-permute-start.3 = (bf16[16,5376]{1,0:T(8,128)(2,1)}, bf16[16,5376]{1,0:T(8,128)(2,1)S(1)}, u32[]{:S(2)}, u32[]{:S(2)}) collective-permute-start(bf16[16,5376]{1,0:T(8,128)(2,1)} %shard_map.104.payload_ref), channel_id=1, source_target_pairs={{0,8},{1,9},{2,10},{3,11},{4,12},{5,13},{6,14},{7,15},{8,0},{9,1},... | collective-permute-start | bytes 516104 | tf_op jit(solution)/shard_map/ppermute | solution.py:665
  54.2 0.7 copy-start.13
  57.0 18.8 %collective-permute-start.4 = (bf16[16,5376]{1,0:T(8,128)(2,1)}, bf16[16,5376]{1,0:T(8,128)(2,1)S(1)}, u32[]{:S(2)}, u32[]{:S(2)}) collective-permute-start(bf16[16,5376]{1,0:T(8,128)(2,1)} %shard_map.105.payload_ref), channel_id=1, source_target_pairs={{0,24},{1,25},{2,26},{3,27},{4,28},{5,29},{6,30},{7,31},{8,16},{9,... | collective-permute-start | bytes 516104 | tf_op jit(solution)/shard_map/ppermute | solution.py:665
  61.3 2.2 %copy-start.4 = (bf16[128,16,1024]{2,1,0:T(8,128)(2,1)S(1)}, bf16[128,16,1024]{2,1,0:T(8,128)(2,1)}, u32[]{:S(2)}) copy-start(bf16[128,16,1024]{2,1,0:T(8,128)(2,1)} %c_ref.1) | copy-start | bytes 12582916
  63.5 16.7 %copy-start.29 = (s32[128,12]{0,1:T(8,128)S(1)}, s32[128,12]{0,1:T(8,128)}, u32[]{:S(2)}) copy-start(s32[128,12]{0,1:T(8,128)} %param.15) | copy-start | bytes 18436
  63.5 26.4 %copy-start.20 = (f32[3,8192]{1,0:T(4,128)S(1)}, f32[3,8192]{1,0:T(4,128)}, u32[]{:S(2)}) copy-start(f32[3,8192]{1,0:T(4,128)} %refs_10_.1) | copy-start | bytes 294916
  73.8 2.0 %copy-start.1 = (bf16[16,256,512]{2,1,0:T(8,128)(2,1)}, bf16[16,256,512]{2,1,0:T(8,128)(2,1)S(1)}, u32[]{:S(2)}) copy-start(bf16[16,256,512]{2,1,0:T(8,128)(2,1)S(1)} %shard_map.108.refs_12_) | copy-start | bytes 12582916
  75.8 0.7 copy-start.15
  78.7 5.6 %collective-permute-start.5 = (bf16[16,5376]{1,0:T(8,128)(2,1)}, bf16[16,5376]{1,0:T(8,128)(2,1)S(1)}, u32[]{:S(2)}, u32[]{:S(2)}) collective-permute-start(bf16[16,5376]{1,0:T(8,128)(2,1)} %shard_map.106.payload_ref), channel_id=1, source_target_pairs={{0,32},{1,33},{2,34},{3,35},{4,36},{5,37},{6,38},{7,39},{8,40},{9,... | collective-permute-start | bytes 516104 | tf_op jit(solution)/shard_map/ppermute | solution.py:665
  84.3 0.7 copy-start.17
  87.0 18.3 %copy-start.3 = (bf16[16,6400]{1,0:T(8,128)(2,1)S(1)}, bf16[16,6400]{1,0:T(8,128)(2,1)}, u32[]{:S(2)}) copy-start(bf16[16,6400]{1,0:T(8,128)(2,1)} %copy-done.2) | copy-start | bytes 614404
  87.0 18.3 %copy-start.5 = (bf16[320,128]{1,0:T(8,128)(2,1)S(1)}, bf16[320,128]{1,0:T(8,128)(2,1)}, u32[]{:S(2)}) copy-start(bf16[320,128]{1,0:T(8,128)(2,1)} %get-tuple-element.12.em_ref.refs_7_) | copy-start | bytes 245764
  87.0 18.4 %copy-start.8 = (bf16[16,6400]{1,0:T(8,128)(2,1)S(1)}, bf16[16,6400]{1,0:T(8,128)(2,1)}, u32[]{:S(2)}) copy-start(bf16[16,6400]{1,0:T(8,128)(2,1)} %copy-done.7) | copy-start | bytes 614404
  87.0 18.4 %copy-start.10 = (bf16[16,5376]{1,0:T(8,128)(2,1)S(1)}, bf16[16,5376]{1,0:T(8,128)(2,1)}, u32[]{:S(2)}) copy-start(bf16[16,5376]{1,0:T(8,128)(2,1)} %copy-done.9) | copy-start | bytes 516100
  87.0 18.4 %copy-start.12 = (bf16[16,5376]{1,0:T(8,128)(2,1)S(1)}, bf16[16,5376]{1,0:T(8,128)(2,1)}, u32[]{:S(2)}) copy-start(bf16[16,5376]{1,0:T(8,128)(2,1)} %copy-done.11) | copy-start | bytes 516100
  87.0 18.4 %copy-start.14 = (bf16[16,5376]{1,0:T(8,128)(2,1)S(1)}, bf16[16,5376]{1,0:T(8,128)(2,1)}, u32[]{:S(2)}) copy-start(bf16[16,5376]{1,0:T(8,128)(2,1)} %copy-done.13) | copy-start | bytes 516100
  87.0 18.4 %copy-start.16 = (bf16[16,5376]{1,0:T(8,128)(2,1)S(1)}, bf16[16,5376]{1,0:T(8,128)(2,1)}, u32[]{:S(2)}) copy-start(bf16[16,5376]{1,0:T(8,128)(2,1)} %copy-done.15) | copy-start | bytes 516100
  87.0 18.4 %copy-start.18 = (bf16[16,5376]{1,0:T(8,128)(2,1)S(1)}, bf16[16,5376]{1,0:T(8,128)(2,1)}, u32[]{:S(2)}) copy-start(bf16[16,5376]{1,0:T(8,128)(2,1)} %copy-done.17) | copy-start | bytes 516100
  87.0 18.4 %copy-start.21 = (bf16[192,128]{1,0:T(8,128)(2,1)S(1)}, bf16[192,128]{1,0:T(8,128)(2,1)}, u32[]{:S(2)}) copy-start(bf16[192,128]{1,0:T(8,128)(2,1)} %get-tuple-element.13.refs_8_) | copy-start | bytes 147460
  87.1 18.4 %copy-start.23 = (s32[8]{0:T(128)S(1)}, s32[8]{0:T(128)}, u32[]{:S(2)}) copy-start(s32[8]{0:T(128)} %copy-done.22) | copy-start | bytes 100
  87.1 18.2 %collective-permute-start.6 = (bf16[16,5376]{1,0:T(8,128)(2,1)}, bf16[16,5376]{1,0:T(8,128)(2,1)S(1)}, u32[]{:S(2)}, u32[]{:S(2)}) collective-permute-start(bf16[16,5376]{1,0:T(8,128)(2,1)} %shard_map.107), channel_id=1, source_target_pairs={{0,96},{1,97},{2,98},{3,99},{4,100},{5,101},{6,102},{7,103},{8,104... | collective-permute-start | bytes 516104 | tf_op jit(solution)/shard_map/ppermute | solution.py:665
  89.9 1.0 copy-start.27

commit v4 on v3

--- a/solution.py
+++ b/solution.py
@@ -108,27 +108,25 @@
     return acc
 
 
-def near_kernel(blocks, coords_ref, points_ref, rel_ref, out_ref, left_ref, right_ref, weight_ref, acc_ref, x_ref, *kerns):
+def near_kernel(chunk, blocks, coords_ref, points_ref, rel_ref, after_ref, out_ref, token_ref, left_ref, right_ref, weight_ref, acc_ref, x_ref, *kerns):
+    del after_ref
     total = blocks + 2
+    begin = chunk * blocks
+    valid = min(total, LEAF_DEV // BL - begin)
+    token_ref[...] = jnp.zeros_like(token_ref)
     count = slot_counts(rel_ref)
-    for b in range(blocks):
-        weight_ref[b] = spread_counts(count, b)
-    for b in (blocks, blocks + 1):
-        weight_ref[b] = jnp.zeros((32, BLK), f32)
-    x_ref[:, : blocks * BLK] = points_ref[...]
-    x_ref[:, blocks * BLK :] = jnp.zeros((16, 2 * BLK), bf16)
-    left_ref[blocks * BLK :, :] = jnp.zeros((2 * BLK, FEAT), bf16)
-
-    @pl.loop(0, blocks // 2)
-    def _(b):
-        at = pl.multiple_of(2 * b * BLK, BLK)
-        left, right = features(split3(widened(scaled(coords_ref[:, pl.ds(at, 2 * BLK)]))))
-        left_ref[pl.ds(at, 2 * BLK), :] = jnp.transpose(left).astype(bf16)
-        right_ref[:, pl.ds(at, 2 * BLK)] = right.astype(bf16)
-
-    @pl.loop(0, total)
-    def _(b):
+    x_ref[:, : valid * BLK] = points_ref[:, begin * BLK : (begin + valid) * BLK]
+    if valid < total:
+        x_ref[:, valid * BLK :] = jnp.zeros((16, (total - valid) * BLK), bf16)
+        left_ref[valid * BLK :, :] = jnp.zeros(((total - valid) * BLK, FEAT), bf16)
+    for b in range(total):
         acc_ref[b] = jnp.zeros((16, BLK), f32)
+        weight_ref[b] = spread_counts(count, begin + b) if b < valid else jnp.zeros((32, BLK), f32)
+    for b in range(0, valid, 2):
+        at = b * BLK
+        left, right = features(split3(widened(scaled(coords_ref[:, begin * BLK + at : begin * BLK + at + 2 * BLK]))))
+        left_ref[at : at + 2 * BLK, :] = jnp.transpose(left).astype(bf16)
+        right_ref[:, at : at + 2 * BLK] = right.astype(bf16)
 
     rows = 128
     diagonal = [
@@ -159,7 +157,8 @@
             part = jnp.dot(x_i if step == 0 else block_x(j), kern, preferred_element_type=f32)
             if step:
                 mirror = lax.dot_general(x_i, kern, (((1,), (1,)), ((), ())), preferred_element_type=f32)
-            evaluate(n, step, next_ref)
+            if n is not None:
+                evaluate(n, step, next_ref)
             acc_i = weighed(acc_i, part, weight_i, BL * step)
             if step:
                 acc_ref[j] = weighed(acc_ref[j], mirror, weight_ref[j], -BL * step)
@@ -168,25 +167,32 @@
     for step in range(3):
         evaluate(0, step, kerns[0])
 
-    @pl.loop(0, blocks // 2)
+    @pl.loop(0, blocks // 2 - 1)
     def _(m):
         both(2 * m, kerns[0], 2 * m + 1, kerns[1])
-        both(2 * m + 1, kerns[1], jnp.minimum(2 * m + 2, blocks - 1), kerns[0])
-
-    @pl.loop(0, blocks)
-    def _(b):
-        out_ref[:, pl.ds(pl.multiple_of(b * BLK, BLK), BLK)] = acc_ref[b]
-
-
-def near_field(coords, points, near_rel):
-    blocks = LEAF_DEV // BL
+        both(2 * m + 1, kerns[1], 2 * m + 2, kerns[0])
+
+    both(blocks - 2, kerns[0], blocks - 1, kerns[1])
+    both(blocks - 1, kerns[1], None, None)
+    for b in range(total):
+        out_ref[:, b * BLK : b * BLK + BLK] = acc_ref[b]
+
+
+CHUNKS = 4
+
+
+def near_chunk(chunk, coords, points, near_rel, after):
+    blocks = LEAF_DEV // BL // CHUNKS
     total = blocks + 2
     vmem = pl.BlockSpec(memory_space=pltpu.VMEM)
     return pl.pallas_call(
-        functools.partial(near_kernel, blocks),
-        out_shape=jax.ShapeDtypeStruct((16, LEAF_DEV * LEAF), f32),
-        in_specs=[vmem] * 3,
-        out_specs=vmem,
+        functools.partial(near_kernel, chunk, blocks),
+        out_shape=(
+            jax.ShapeDtypeStruct((16, total * BLK), f32),
+            jax.ShapeDtypeStruct((8, 128), f32),
+        ),
+        in_specs=[vmem] * 3 + [pl.BlockSpec(memory_space=pl.ANY)],
+        out_specs=(vmem, vmem),
         scratch_shapes=[
             pltpu.VMEM((total * BLK, FEAT), bf16),
             pltpu.VMEM((FEAT, total * BLK), bf16),
@@ -196,9 +202,9 @@
             pltpu.VMEM((3, BLK, BLK), bf16),
             pltpu.VMEM((3, BLK, BLK), bf16),
         ],
-        compiler_params=pltpu.CompilerParams(vmem_limit_bytes=32 * 1024 * 1024),
-        cost_estimate=pl.CostEstimate(flops=2_000_000_000, bytes_accessed=2_000_000, transcendentals=13_000_000),
-    )(coords, points, near_rel)
+        compiler_params=pltpu.CompilerParams(vmem_limit_bytes=16 * 1024 * 1024),
+        cost_estimate=pl.CostEstimate(flops=1_000_000_000, bytes_accessed=1_000_000, transcendentals=4_000_000),
+    )(coords, points, near_rel, after)
 
 
 EDGES = ((0, -2, 0), (0, -1, 1), (1, -2, 1), (30, 2, 0), (31, 1, 0), (31, 2, 1))
@@ -365,34 +371,57 @@
     return jnp.concatenate([points_ref[:, start:end], rows.astype(bf16)], axis=1)
 
 
-def open_kernel(pair_ref, couple_ref, em_ref, sm_ref):
+def open_kernel(nodes_ref, transfer_ref, couple_ref, after_ref, em_ref, sm_ref, token_ref, rows_ref, sem):
+    del after_ref
+    token_ref[...] = jnp.zeros_like(token_ref)
+    copies = [
+        pltpu.make_async_copy(couple_ref.at[pl.ds(nodes_ref[k], 1)], rows_ref.at[pl.ds(k, 1)], sem.at[k])
+        for k in range(6)
+    ]
+    for copy in copies:
+        copy.start()
+    which = iota((16, 254), 0)
+    wanted = jnp.full((16, 254), -1, jnp.int32)
+    for k in range(5):
+        first = nodes_ref[k] - nodes_ref[8 + k]
+        wanted = jnp.where(which == 2 * k, first, wanted)
+        wanted = jnp.where(which == 2 * k + 1, first + 1, wanted)
+    pairs = dot(where_eq(wanted, iota((16, 254), 1)), transfer_ref[...])
     fold_row = iota((1024, 128), 0) % RANK
     fold_col = iota((1024, 128), 1)
     fold_first = where_eq(fold_row, fold_col)
     fold_second = where_eq(fold_row + RANK, fold_col)
     own = iota((RANK, 1024), 1) // RANK == iota((RANK, 1024), 0)
-    pairs = pair_ref[...].astype(f32)
-    couples = couple_ref[...].astype(f32)
 
     def opened(values, k):
         return jnp.where(own, values[k : k + 1, :], 0.0).astype(bf16)
 
+    for copy in copies:
+        copy.wait()
+    couples = [rows_ref[k].astype(f32) for k in range(6)]
     em_ref[...] = dot(jnp.concatenate([opened(pairs, k) for k in range(10)], axis=0), fold_first).astype(bf16)
     sm_ref[...] = (
-        dot(jnp.concatenate([opened(couples, 2 * k) for k in range(6)], axis=0), fold_first)
-        + dot(jnp.concatenate([opened(couples, 2 * k + 1) for k in range(6)], axis=0), fold_second)
+        dot(jnp.concatenate([opened(couples[k], 0) for k in range(6)], axis=0), fold_first)
+        + dot(jnp.concatenate([opened(couples[k], 1) for k in range(6)], axis=0), fold_second)
     ).astype(bf16)
 
 
-def opened_top(pairs, couples):
+def opened_top(nodes, top_transfer, top_coupling, after):
     vmem = pl.BlockSpec(memory_space=pltpu.VMEM)
+    anywhere = pl.BlockSpec(memory_space=pl.ANY)
     return pl.pallas_call(
         open_kernel,
-        out_shape=(jax.ShapeDtypeStruct((320, 128), bf16), jax.ShapeDtypeStruct((192, 128), bf16)),
-        in_specs=[vmem] * 2,
-        out_specs=(vmem, vmem),
-        cost_estimate=pl.CostEstimate(flops=1_000_000, bytes_accessed=400_000, transcendentals=0),
-    )(pairs, couples)
+        out_shape=(
+            jax.ShapeDtypeStruct((320, 128), bf16),
+            jax.ShapeDtypeStruct((192, 128), bf16),
+            jax.ShapeDtypeStruct((8, 128), f32),
+        ),
+        in_specs=[pl.BlockSpec(memory_space=pltpu.SMEM), vmem, anywhere, anywhere],
+        out_specs=(vmem, vmem, vmem),
+        scratch_shapes=[pltpu.VMEM((6, 2, 1024), bf16), pltpu.SemaphoreType.DMA((6,))],
+        compiler_params=pltpu.CompilerParams(vmem_limit_bytes=60 * 1024 * 1024),
+        cost_estimate=pl.CostEstimate(flops=100_000_000, bytes_accessed=800_000, transcendentals=0),
+    )(nodes, top_transfer, top_coupling, after)
 
 
 def fill_upper(y_ref, bdup_ref, target, tile, keep):
@@ -434,12 +463,13 @@
             pltpu.VMEM((128, 256), f32),
             pltpu.VMEM((8, 128, 1024), f32),
         ],
-        compiler_params=pltpu.CompilerParams(vmem_limit_bytes=48 * 1024 * 1024),
+        compiler_params=pltpu.CompilerParams(vmem_limit_bytes=60 * 1024 * 1024),
         cost_estimate=pl.CostEstimate(flops=1_000_000_000, bytes_accessed=10_000_000, transcendentals=0),
     )(bits, points, coords, basis, local_transfer)
 
 
-def step_kernel(height, bits_ref, first_ref, payload_ref, received_ref, em_ref, next_ref):
+def step_kernel(height, bits_ref, first_ref, payload_ref, received_ref, em_ref, after_ref, next_ref):
+    del after_ref
     forward = height % 2 == 1
     next_ref[:, :TABLE] = received_ref[:, :TABLE] if forward else first_ref[:, :TABLE]
     start = WIDTH if height == 0 else EDGE
@@ -457,28 +487,31 @@
     next_ref[:, TABLE:EDGE] = pack_state(parent, mine, sibling)
 
 
-def tree_step(height, bits, first, payload, received, em):
+def tree_step(height, bits, first, payload, received, em, after):
     vmem = pl.BlockSpec(memory_space=pltpu.VMEM)
     return pl.pallas_call(
         functools.partial(step_kernel, height),
         out_shape=jax.ShapeDtypeStruct((16, WIDTH), bf16),
-        in_specs=[pl.BlockSpec(memory_space=pltpu.SMEM)] + [vmem] * 4,
+        in_specs=[pl.BlockSpec(memory_space=pltpu.SMEM)] + [vmem] * 4 + [pl.BlockSpec(memory_space=pl.ANY)],
         out_specs=vmem,
+        compiler_params=pltpu.CompilerParams(vmem_limit_bytes=4 * 1024 * 1024),
         cost_estimate=pl.CostEstimate(flops=1_000_000, bytes_accessed=400_000, transcendentals=0),
-    )(bits, first, payload, received, em)
-
-
-def regroup_kernel(c_ref, out_ref, x_ref):
-    flat = c_ref[...].astype(f32).reshape(128, 1024)
-    for k in range(8):
-        x_ref[k] = flat[:, 128 * k : 128 * k + 128]
+    )(bits, first, payload, received, em, after)
+
+
+def regroup_kernel(c_ref, after_ref, out_ref, token_ref):
+    del after_ref
+    token_ref[...] = jnp.zeros_like(token_ref)
+    row = iota((128, 128), 0)
+    perm = where_eq((row % 8) * NF + row // 8, iota((128, 128), 1))
+    x = dot(perm, c_ref[...].reshape(128, 1024))
     lanes = iota((8, 128), 1)
     low_half = lanes < 64
     even = (lanes // RANK) % 2 == 0
     for s_high in range(4):
         for a_high in range(8):
             v = [
-                x_ref[a_high, pl.ds(4 * s_high + k, 8, stride=NF), :]
+                x[32 * s_high + 8 * k : 32 * s_high + 8 * k + 8, 128 * a_high : 128 * a_high + 128]
                 for k in range(4)
             ]
             u0 = jnp.where(low_half, v[0], pltpu.roll(v[2], 64, 1))
@@ -495,22 +528,31 @@
             out_ref[0, row + 16 : row + 32, lane : lane + 128] = jnp.concatenate(w[2:], axis=0).astype(bf16)
 
 
-def regroup(far_coupling):
+def regroup(half, far_coupling, after):
+    groups = GROUPS // 2
     return pl.pallas_call(
         regroup_kernel,
-        grid=(GROUPS,),
-        out_shape=jax.ShapeDtypeStruct((GROUPS, 256, 512), bf16),
-        in_specs=[pl.BlockSpec((8, NF, 1024), lambda i: (i, 0, 0))],
-        out_specs=pl.BlockSpec((1, 256, 512), lambda i: (i, 0, 0)),
-        scratch_shapes=[pltpu.VMEM((8, 128, 128), f32)],
-        compiler_params=pltpu.CompilerParams(vmem_limit_bytes=32 * 1024 * 1024),
-        cost_estimate=pl.CostEstimate(flops=30_000_000, bytes_accessed=8_400_000, transcendentals=0),
-    )(far_coupling)
+        grid=(groups,),
+        out_shape=(
+            jax.ShapeDtypeStruct((groups, 256, 512), bf16),
+            jax.ShapeDtypeStruct((8, 128), f32),
+        ),
+        in_specs=[
+            pl.BlockSpec((8, NF, 1024), lambda i: (i + half * groups, 0, 0)),
+            pl.BlockSpec(memory_space=pl.ANY),
+        ],
+        out_specs=(
+            pl.BlockSpec((1, 256, 512), lambda i: (i, 0, 0)),
+            pl.BlockSpec((8, 128), lambda i: (0, 0)),
+        ),
+        compiler_params=pltpu.CompilerParams(vmem_limit_bytes=60 * 1024 * 1024),
+        cost_estimate=pl.CostEstimate(flops=600_000_000, bytes_accessed=4_200_000, transcendentals=0),
+    )(far_coupling, after)
 
 
 def down_kernel(bits_ref, index_ref, payload_ref, *refs):
     received = refs[:7]
-    em_ref, sm_ref, bdup_ref, coords_ref, rel_ref, d_ref, ub_ref, bd_ref, near_ref, out_ref, table_ref, field_ref, far_ref, gather_ref, edge_ref = refs[7:]
+    em_ref, sm_ref, bdup_ref, coords_ref, rel_ref, d0_ref, d1_ref, ub_ref, bd_ref, near0_ref, near1_ref, near2_ref, near3_ref, out_ref, table_ref, field_ref, far_ref, gather_ref, edge_ref = refs[7:]
     step = pl.program_id(0)
 
     @pl.when(step == 0)
@@ -569,7 +611,8 @@
                 value = table_ref[pl.ds(pl.multiple_of(entry * 16, 16), 16), :]
                 merged = value if low == 0 else jnp.where(block == low, value, merged)
             gather_ref[16 * leaf : 16 * leaf + 16, 128 * s_high : 128 * s_high + 128] = merged
-    result = dot_nt(gather_ref[...], d_ref[0])
+    coupling = jnp.where(step < GROUPS // 2, d0_ref[0], d1_ref[0])
+    result = dot_nt(gather_ref[...], coupling)
     which = iota((16, 256), 1) % 8
     far = result[0:16]
     for leaf in range(1, 8):
@@ -586,8 +629,13 @@
         column = iota((512, 512), 1)
         perm = where_eq(iota((512, 512), 0), (column % LEAF) * 8 + column // LEAF)
         whole = joined(dot(far_ref[...], perm))
+        nears = (near0_ref, near1_ref, near2_ref, near3_ref)
         for g in range(GROUPS):
-            value = near_ref[:, 512 * g : 512 * g + 512] + whole[16 * g : 16 * g + 16, :]
+            per = GROUPS // CHUNKS
+            chunk, place = g // per, 512 * (g % per)
+            value = nears[chunk][:, place : place + 512] + whole[16 * g : 16 * g + 16, :]
+            if chunk and g % per == 0:
+                value = value + nears[chunk - 1][:, 512 * per : 512 * per + 512]
             if g == 0:
                 value = value + jnp.concatenate([edge_ref[0], edge_ref[1]], axis=1)
             if g == GROUPS - 1:
@@ -595,7 +643,7 @@
             out_ref[:, 512 * g : 512 * g + 512] = value
 
 
-def downward(bits, index, payload, received, em, sm, bdup, coords, near_rel, d, ub, bd, near):
+def downward(bits, index, payload, received, em, sm, bdup, coords, near_rel, d, ub, bd, nears):
     full = lambda *shape: pl.BlockSpec(shape, lambda i: (0,) * len(shape))
     smem = pl.BlockSpec(memory_space=pltpu.SMEM)
     each = lambda *shape: pl.BlockSpec((1,) + shape, lambda i: (i, 0, 0))
@@ -608,7 +656,12 @@
         + [full(16, WIDTH)] * 6
         + [full(320, 128), full(192, 128), full(UPPER, 256, 256)]
         + [full(3, LEAF_DEV * LEAF), full(NN, LEAF_DEV)]
-        + [each(256, 512), each(512, 256), each(256, 256), full(16, LEAF_DEV * LEAF)],
+        + [
+            pl.BlockSpec((1, 256, 512), lambda i: (jnp.minimum(i, GROUPS // 2 - 1), 0, 0)),
+            pl.BlockSpec((1, 256, 512), lambda i: (jnp.maximum(i - GROUPS // 2, 0), 0, 0)),
+        ]
+        + [each(512, 256), each(256, 256)]
+        + [full(16, (LEAF_DEV // BL // CHUNKS + 2) * BLK)] * CHUNKS,
         out_specs=full(16, LEAF_DEV * LEAF),
         scratch_shapes=[
             pltpu.VMEM((16400, 128), bf16),
@@ -617,9 +670,9 @@
             pltpu.VMEM((128, 512), bf16),
             pltpu.VMEM((4, 16, BLK), f32),
         ],
-        compiler_params=pltpu.CompilerParams(vmem_limit_bytes=48 * 1024 * 1024),
+        compiler_params=pltpu.CompilerParams(vmem_limit_bytes=24 * 1024 * 1024),
         cost_estimate=pl.CostEstimate(flops=3_000_000_000, bytes_accessed=16_000_000, transcendentals=0),
-    )(bits, index, payload, *received, em, sm, bdup, coords, near_rel, d, ub, bd, near)
+    )(bits, index, payload, *received, em, sm, bdup, coords, near_rel, *d, ub, bd, *nears)
 
 
 def top_start(height, number):
@@ -646,29 +699,34 @@
     bits = jnp.where(number == 7, jnp.maximum(level, 1), jnp.right_shift(device, number) & 1)
     starts = jnp.array([top_start(h, N_DEV) for h in range(6)], jnp.int32)
     heights = jnp.arange(6, dtype=jnp.int32)
-    nodes = starts + jnp.right_shift(device, heights)
-    pair_rows = (starts + (jnp.right_shift(device, heights) & -2))[:5]
-    pair_rows = (pair_rows[:, None] + jnp.arange(2, dtype=jnp.int32)[None, :]).reshape(10)
-    pairs = top_transfer[pair_rows]
-    couples = top_coupling[nodes].reshape(12, RANK * RANK)
+    parity = jnp.right_shift(device, heights) & 1
+    blank = jnp.zeros((2,), jnp.int32)
+    nodes = jnp.concatenate([starts + jnp.right_shift(device, heights), blank, parity, blank])
     owner = jnp.bitwise_xor(jnp.right_shift(far_list, 7), device)
     slot = sum((owner >> k > 0).astype(jnp.int32) for k in range(7))
     within = far_list & (LEAF_DEV - 1)
     entry = slot * LEAF_DEV + (within & 7) * GROUPS + (within >> 3)
     index = jnp.where(far_list >= 0, entry, 8 * LEAF_DEV).reshape(LEAF_DEV * NF)
     payload, ub, bd, bdup = upward(bits, points, coords, basis, local_transfer)
-    em, sm = opened_top(pairs, couples)
+    near_rel = jnp.transpose(jnp.where(near_list >= 0, near_list - device * LEAF_DEV, -1000))
     first = payload
     received = []
+    nears = []
+    halves_of = []
     for height, mask in enumerate(PARTNERS):
         route = [(i, i ^ mask) for i in range(N_DEV)]
         received.append(lax.ppermute(payload, "leaf", route))
+        if height == 0:
+            em, sm, token = opened_top(nodes, top_transfer, top_coupling, payload)
+        elif height in (4, 5):
+            part, token = regroup(height - 4, far_coupling, payload)
+            halves_of.append(part)
+        else:
+            part, token = near_chunk(len(nears), coords, points, near_rel, payload)
+            nears.append(part)
         if height < 6:
-            payload = tree_step(height, bits, first, payload, received[height], em)
-    near_rel = jnp.transpose(jnp.where(near_list >= 0, near_list - device * LEAF_DEV, -1000))
-    near_part = near_field(coords, points, near_rel)
-    d = regroup(far_coupling)
-    return downward(bits, index, first, received, em, sm, bdup, coords, near_rel, d, ub, bd, near_part)
+            payload = tree_step(height, bits, first, payload, received[height], em, token)
+    return downward(bits, index, first, received, em, sm, bdup, coords, near_rel, halves_of, ub, bd, nears)
 
 
 def solution(mesh):

time: 126 us -> 96.7 us (0.77)
  waiting for transfers between devices: 17.6 us -> 2.14 us
  Pallas kernels: 67.9 us -> 62.2 us
  local copies, waits for them, and re-layouts: 20.3 us -> 15.3 us
  other arithmetic: 3.75 us -> 1.25 us
    ppermute x7, waiting for transfers between devices: 17.6 us -> 2.14 us  [per_device(): received.append(lax.ppermute(payload, 'leaf', route))]
    pallas_call x6, Pallas kernels: 12.9 us -> 5.73 us  [tree_step(): pl.pallas_call(functools.partial(step_kernel, height), out_shape=jax.Shap...]
    pallas_call x1, Pallas kernels: 19.4 us -> 14.8 us  [downward(): pl.pallas_call(down_kernel, grid=(GROUPS,), out_shape=jax.ShapeDtypeStruc...]
    gather x2 -> x0, local copies, waits for them, and re-layouts: 3.49 us -> none  [the longest x1 2.3 us: per_device(): pairs = top_transfer[pair_rows]]
    pallas_call x2 -> x6, Pallas kernels: 24.8 us -> 27.5 us  [the longest x2 13.9 us: regroup(): pl.pallas_call(regroup_kernel, grid=(groups,), out_shape=(jax.ShapeDtypeS...]
    select_n x2 -> x0, other arithmetic: 2.41 us -> none  [the longest x1 1.22 us: per_device(): couples = top_coupling[nodes].reshape(12, RANK * RANK)]
    pallas_call x1, Pallas kernels: 8.84 us -> 11.2 us  [upward(): pl.pallas_call(up_kernel, grid=(GROUPS // 2,), out_shape=(jax.ShapeDtypeS...]
    reshape x1 -> x0, local copies, waits for them, and re-layouts: 1.35 us -> none  [per_device(): couples = top_coupling[nodes].reshape(12, RANK * RANK)]
  transfers between devices with their start and end apart: 7 -> 7, of which waited for: 4 -> 3; matrix products, arithmetic and copies ran while one was open for 8% -> 1% of each run, Pallas kernels for 21% -> 32%
where the time goes in v4:
time: 96.7 us; the launch traced here: 95.5 us
  Pallas kernels  62.2 us (64%)
  local copies, waits for them, and re-layouts  15.3 us (16%)
  starting transfers between devices  14.4 us (15%)
  waiting for transfers between devices  2.14 us (2%)
  other arithmetic  1.25 us (1%)
    unnamed x64, local copies, waits for them, and re-layouts  15.1 us
    pallas_call x1, Pallas kernels, downward(): pl.pallas_call(down_kernel, grid=(GROUPS,), out_shape=jax.ShapeDtypeStruc...  14.8 us
    ppermute x7, starting transfers between devices, per_device(): received.append(lax.ppermute(payload, 'leaf', route))  14.4 us
    pallas_call x2, Pallas kernels, regroup(): pl.pallas_call(regroup_kernel, grid=(groups,), out_shape=(jax.ShapeDtypeS...  13.9 us
    pallas_call x4, Pallas kernels, near_chunk(): pl.pallas_call(functools.partial(near_kernel, chunk, blocks), out_shape=(...  13.6 us
    pallas_call x1, Pallas kernels, upward(): pl.pallas_call(up_kernel, grid=(GROUPS // 2,), out_shape=(jax.ShapeDtypeS...  11.2 us
    pallas_call x6, Pallas kernels, tree_step(): pl.pallas_call(functools.partial(step_kernel, height), out_shape=jax.Shap...  5.73 us
    pallas_call x1, Pallas kernels, opened_top(): pl.pallas_call(open_kernel, out_shape=(jax.ShapeDtypeStruct((320, 128), b...  3.03 us
  transfers between devices with their start and end apart: 7, of which 3 were waited for; matrix products, arithmetic and copies ran while one was open for 1% of the time, Pallas kernels for 32%

profile of v4, /device:TPU:0, one launch (start us, length us, event | category | flops | bytes accessed | tf_op | source)
XLA Modules:
  0.0 95.5 jit_solution(15670737615391724621)
XLA Ops:
  0.0 0.6 compare_select_fusion.bits_ref
  0.6 11.2 %shard_map.100 = (bf16[16,6400]{1,0:T(8,128)(2,1)}, bf16[16,512,256]{2,1,0:T(8,128)(2,1)}, bf16[16,256,256]{2,1,0:T(8,128)(2,1)}, bf16[17,256,256]{2,1,0:T(8,128)(2,1)}) custom-call(s32[8]{0:T(128)} %compare_select_fusion.bits_ref, bf16[16,8192]{1,0:T(8,128)(2,1)} %points_ref.9, f32[3,8192]{1,0:T(4,128)} %refs_10_.1, bf16[128,2048]{1,0:T(8,128)(2,1)} %basis_ref.1, ...), custom_call_target="tpu_custom_call" | custom-call | flops 1000000000 | bytes 10000000 | tf_op jit(solution)/shard_map/pallas_call | solution.py:438
  11.8 0.0 copy-start.29
  11.8 0.0 copy-start.19
  11.8 0.0 copy-start.27
  11.8 0.1 collective-permute-start
  11.9 0.6 pad_add_fusion.nodes_ref
  12.6 3.0 %shard_map.101 = (bf16[320,128]{1,0:T(8,128)(2,1)}, bf16[192,128]{1,0:T(8,128)(2,1)}, f32[8,128]{1,0:T(8,128)}) custom-call(s32[16]{0:T(128)} %pad_add_fusion.nodes_ref, bf16[254,1024]{1,0:T(8,128)(2,1)} %transfer_ref.1, bf16[252,2,1024]{2,1,0:T(2,128)(2,1)} %couple_ref.1, bf16[16,6400]{1,0:T(8,128)(2,1)} %get-tuple-element.23.after_ref.first_ref.payload_ref), custom_call_target="tpu_custom_call" | custom-call | flops 100000000 | bytes 800000 | tf_op jit(solution)/shard_map/pallas_call | solution.py:412
  15.6 0.9 copy-done
  16.5 0.9 copy-done.3
  17.4 0.7 copy-done.24
  18.1 0.9 shard_map.102.after_ref.payload_ref
  19.0 1.7 %collective-permute-start.1 = (bf16[16,5376]{1,0:T(8,128)(2,1)S(1)}, bf16[16,5376]{1,0:T(8,128)(2,1)S(1)}, u32[]{:S(2)}, u32[]{:S(2)}) collective-permute-start(bf16[16,5376]{1,0:T(8,128)(2,1)S(1)} %shard_map.102.after_ref.payload_ref), channel_id=1, source_target_pairs={{0,2},{1,3},{2,0},{3,1},{4,6},{5,7},{6,4},{7,5},{8,10},{9,11},{10,... | collective-permute-start | bytes 516104 | tf_op jit(solution)/shard_map/ppermute | solution.py:718
  20.7 3.4 %shard_map.103 = (f32[16,2560]{1,0:T(8,128)S(1)}, f32[8,128]{1,0:T(8,128)S(1)}) custom-call(f32[3,8192]{1,0:T(4,128)S(1)} %copy-done.19, bf16[16,8192]{1,0:T(8,128)(2,1)S(1)} %copy-done.27, s32[12,128]{1,0:T(8,128)S(1)} %select_bitcast_fusion.rel_ref.refs_11_, bf16[16,5376]{1,0:T(8,128)(2,1)S(1)} %shard_map.102.after_ref.payload_ref), custom_call_target="tpu_custom_call" | custom-call | flops 1000000000 | bytes 1000000 | tf_op jit(solution)/shard_map/pallas_call | solution.py:188
  24.1 1.6 %collective-permute-done.1.received_ref.refs_1_ = bf16[16,5376]{1,0:T(8,128)(2,1)S(1)} collective-permute-done((bf16[16,5376]{1,0:T(8,128)(2,1)S(1)}, bf16[16,5376]{1,0:T(8,128)(2,1)S(1)}, u32[]{:S(2)}, u32[]{:S(2)}) %collective-permute-start.1) | collective-permute-done | bytes 172064 | tf_op jit(solution)/shard_map/ppermute | solution.py:718
  25.8 0.9 shard_map.104.after_ref.payload_ref
  26.6 3.1 %collective-permute-start.2 = (bf16[16,5376]{1,0:T(8,128)(2,1)S(1)}, bf16[16,5376]{1,0:T(8,128)(2,1)S(1)}, u32[]{:S(2)}, u32[]{:S(2)}) collective-permute-start(bf16[16,5376]{1,0:T(8,128)(2,1)S(1)} %shard_map.104.after_ref.payload_ref), channel_id=1, source_target_pairs={{0,6},{1,7},{2,4},{3,5},{4,2},{5,3},{6,0},{7,1},{8,14},{9,15},{10,... | collective-permute-start | bytes 516104 | tf_op jit(solution)/shard_map/ppermute | solution.py:718
  29.7 3.4 %shard_map.105 = (f32[16,2560]{1,0:T(8,128)S(1)}, f32[8,128]{1,0:T(8,128)S(1)}) custom-call(f32[3,8192]{1,0:T(4,128)S(1)} %copy-done.19, bf16[16,8192]{1,0:T(8,128)(2,1)S(1)} %copy-done.27, s32[12,128]{1,0:T(8,128)S(1)} %select_bitcast_fusion.rel_ref.refs_11_, bf16[16,5376]{1,0:T(8,128)(2,1)S(1)} %shard_map.104.after_ref.payload_ref), custom_call_target="tpu_custom_call" | custom-call | flops 1000000000 | bytes 1000000 | tf_op jit(solution)/shard_map/pallas_call | solution.py:188
  33.2 0.6 copy-done.15
  33.8 0.1 collective-permute-done.2.received_ref.refs_2_
  34.0 0.9 shard_map.106.after_ref.payload_ref
  34.8 1.9 %collective-permute-start.3 = (bf16[16,5376]{1,0:T(8,128)(2,1)S(1)}, bf16[16,5376]{1,0:T(8,128)(2,1)S(1)}, u32[]{:S(2)}, u32[]{:S(2)}) collective-permute-start(bf16[16,5376]{1,0:T(8,128)(2,1)S(1)} %shard_map.106.after_ref.payload_ref), channel_id=1, source_target_pairs={{0,8},{1,9},{2,10},{3,11},{4,12},{5,13},{6,14},{7,15},{8,0},{9,1},... | collective-permute-start | bytes 516104 | tf_op jit(solution)/shard_map/ppermute | solution.py:718
  36.8 3.4 %shard_map.107 = (f32[16,2560]{1,0:T(8,128)S(1)}, f32[8,128]{1,0:T(8,128)S(1)}) custom-call(f32[3,8192]{1,0:T(4,128)S(1)} %copy-done.19, bf16[16,8192]{1,0:T(8,128)(2,1)S(1)} %copy-done.27, s32[12,128]{1,0:T(8,128)S(1)} %select_bitcast_fusion.rel_ref.refs_11_, bf16[16,5376]{1,0:T(8,128)(2,1)S(1)} %shard_map.106.after_ref.payload_ref), custom_call_target="tpu_custom_call" | custom-call | flops 1000000000 | bytes 1000000 | tf_op jit(solution)/shard_map/pallas_call | solution.py:188
  40.2 0.4 collective-permute-done.3.received_ref.refs_3_
  40.6 0.9 shard_map.108.after_ref.payload_ref
  41.5 4.0 %collective-permute-start.4 = (bf16[16,5376]{1,0:T(8,128)(2,1)S(1)}, bf16[16,5376]{1,0:T(8,128)(2,1)S(1)}, u32[]{:S(2)}, u32[]{:S(2)}) collective-permute-start(bf16[16,5376]{1,0:T(8,128)(2,1)S(1)} %shard_map.108.after_ref.payload_ref), channel_id=1, source_target_pairs={{0,24},{1,25},{2,26},{3,27},{4,28},{5,29},{6,30},{7,31},{8,16},{9,... | collective-permute-start | bytes 516104 | tf_op jit(solution)/shard_map/ppermute | solution.py:718
  45.4 6.9 %shard_map.109 = (bf16[8,256,512]{2,1,0:T(8,128)(2,1)}, f32[8,128]{1,0:T(8,128)}) custom-call(bf16[128,16,1024]{2,1,0:T(8,128)(2,1)} %c_ref.3, bf16[16,5376]{1,0:T(8,128)(2,1)} %copy-done.9), custom_call_target="tpu_custom_call" | custom-call | flops 600000000 | bytes 4200000 | tf_op jit(solution)/shard_map/pallas_call | solution.py:533
  52.4 0.9 copy-done.10
  53.3 0.7 copy-done.25
  54.0 0.9 shard_map.110.after_ref.payload_ref
  54.9 1.5 %collective-permute-start.5 = (bf16[16,5376]{1,0:T(8,128)(2,1)S(1)}, bf16[16,5376]{1,0:T(8,128)(2,1)S(1)}, u32[]{:S(2)}, u32[]{:S(2)}) collective-permute-start(bf16[16,5376]{1,0:T(8,128)(2,1)S(1)} %shard_map.110.after_ref.payload_ref), channel_id=1, source_target_pairs={{0,32},{1,33},{2,34},{3,35},{4,36},{5,37},{6,38},{7,39},{8,40},{9,... | collective-permute-start | bytes 516104 | tf_op jit(solution)/shard_map/ppermute | solution.py:718
  56.4 7.0 %shard_map.111 = (bf16[8,256,512]{2,1,0:T(8,128)(2,1)}, f32[8,128]{1,0:T(8,128)}) custom-call(bf16[128,16,1024]{2,1,0:T(8,128)(2,1)} %c_ref.3, bf16[16,5376]{1,0:T(8,128)(2,1)} %copy-done.11), custom_call_target="tpu_custom_call" | custom-call | flops 600000000 | bytes 4200000 | tf_op jit(solution)/shard_map/pallas_call | solution.py:533
  63.3 0.9 copy-done.12
  64.3 0.7 copy-done.26
  64.9 1.4 %shard_map.112.after_ref = bf16[16,5376]{1,0:T(8,128)(2,1)} custom-call(s32[8]{0:T(128)S(1)} %copy-done.23, bf16[16,6400]{1,0:T(8,128)(2,1)S(1)} %copy-done.1, bf16[16,5376]{1,0:T(8,128)(2,1)S(1)} %copy-done.12, bf16[16,5376]{1,0:T(8,128)(2,1)S(1)} %collective-permute-done.5.received_ref.refs_5_, bf16[320,128]{1,0:T(8,128)(2,1)S(1)} %copy-done.4, ...), custom_call_target="tpu_custom_call" | custom-call | flops 1000000 | bytes 400000 | tf_op jit(solution)/shard_map/pallas_call | solution.py:492
  66.3 2.1 %collective-permute-start.6 = (bf16[16,5376]{1,0:T(8,128)(2,1)}, bf16[16,5376]{1,0:T(8,128)(2,1)}, u32[]{:S(2)}, u32[]{:S(2)}) collective-permute-start(bf16[16,5376]{1,0:T(8,128)(2,1)} %shard_map.112.after_ref), channel_id=1, source_target_pairs={{0,96},{1,97},{2,98},{3,99},{4,100},{5,101},{6,102},{7,103},{8,104... | collective-permute-start | bytes 516104 | tf_op jit(solution)/shard_map/ppermute | solution.py:718
  68.4 0.1 copy.11
  68.5 0.1 reshape.3.index_ref
  68.6 0.9 copy-done.20
  69.5 0.9 copy-done.28
  70.5 3.4 %shard_map.113 = (f32[16,2560]{1,0:T(8,128)S(1)}, f32[8,128]{1,0:T(8,128)}) custom-call(f32[3,8192]{1,0:T(4,128)S(1)} %copy-done.20, bf16[16,8192]{1,0:T(8,128)(2,1)S(1)} %copy-done.28, s32[12,128]{1,0:T(8,128)S(1)} %select_bitcast_fusion.rel_ref.refs_11_, bf16[16,5376]{1,0:T(8,128)(2,1)} %shard_map.112.after_ref), custom_call_target="tpu_custom_call" | custom-call | flops 1000000000 | bytes 1000000 | tf_op jit(solution)/shard_map/pallas_call | solution.py:188
  73.9 1.6 %copy-done.7 = bf16[8,256,512]{2,1,0:T(8,128)(2,1)S(1)} copy-done((bf16[8,256,512]{2,1,0:T(8,128)(2,1)S(1)}, bf16[8,256,512]{2,1,0:T(8,128)(2,1)}, u32[]{:S(2)}) %copy-start.7) | copy-done | bytes 2097176
  75.5 1.6 %copy-done.8 = bf16[8,256,512]{2,1,0:T(8,128)(2,1)S(1)} copy-done((bf16[8,256,512]{2,1,0:T(8,128)(2,1)S(1)}, bf16[8,256,512]{2,1,0:T(8,128)(2,1)}, u32[]{:S(2)}) %copy-start.8) | copy-done | bytes 2097176
  77.1 0.9 copy-done.14
  78.0 0.9 copy-done.16
  78.9 0.9 copy-done.18
  79.8 0.9 copy-done.21
  80.7 14.8 %shard_map.114 = f32[16,8192]{1,0:T(8,128)} custom-call(s32[8]{0:T(128)S(1)} %copy-done.23, s32[2048]{0:T(1024)S(1)} %reshape.3.index_ref, bf16[16,6400]{1,0:T(8,128)(2,1)S(1)} %copy-done.1, bf16[16,6400]{1,0:T(8,128)(2,1)S(1)} %collective-permute-done.received_ref.refs_0_, bf16[16,5376]{1,0:T(8,128)(2,1)S(1)} %collective-permute-done.1.received_ref.refs_1_, ...), custom_call_target="tpu_custom_call" | custom-call | flops 3000000000 | bytes 16000000 | tf_op jit(solution)/shard_map/pallas_call | solution.py:650
  (53 shorter events, 0.1 us)
Async XLA Ops:
  0.0 11.9 %copy-start.31 = (s32[6]{0:T(128)S(1)}, s32[6]{0:T(128)}, u32[]{:S(2)}) copy-start(s32[6]{0:T(128)} %constant.6.clone) | copy-start | bytes 76
  0.6 15.0 %copy-start.23 = (s32[8]{0:T(128)S(1)}, s32[8]{0:T(128)}, u32[]{:S(2)}) copy-start(s32[8]{0:T(128)} %compare_select_fusion.bits_ref) | copy-start | bytes 100
  11.8 8.9 %copy-start.29 = (s32[128,12]{0,1:T(8,128)S(1)}, s32[128,12]{0,1:T(8,128)}, u32[]{:S(2)}) copy-start(s32[128,12]{0,1:T(8,128)} %param.15) | copy-start | bytes 18436
  11.8 8.9 %copy-start.19 = (f32[3,8192]{1,0:T(4,128)S(1)}, f32[3,8192]{1,0:T(4,128)}, u32[]{:S(2)}) copy-start(f32[3,8192]{1,0:T(4,128)} %refs_10_.1) | copy-start | bytes 294916
  11.8 8.9 %copy-start.27 = (bf16[16,8192]{1,0:T(8,128)(2,1)S(1)}, bf16[16,8192]{1,0:T(8,128)(2,1)}, u32[]{:S(2)}) copy-start(bf16[16,8192]{1,0:T(8,128)(2,1)} %points_ref.9) | copy-start | bytes 786436
  11.8 3.8 %collective-permute-start = (bf16[16,6400]{1,0:T(8,128)(2,1)}, bf16[16,6400]{1,0:T(8,128)(2,1)S(1)}, u32[]{:S(2)}, u32[]{:S(2)}) collective-permute-start(bf16[16,6400]{1,0:T(8,128)(2,1)} %get-tuple-element.23.after_ref.first_ref.payload_ref), channel_id=1, source_target_pairs={{0,1},{1,0},{2,3},{3,2},{4,5},{5,4},{6,7},{7,6},{8,9},{9,8},{10,11... | collective-permute-start | bytes 614408 | tf_op jit(solution)/shard_map/ppermute | solution.py:718
  15.6 0.9 copy-start
  16.5 0.9 copy-start.3
  17.4 0.7 copy-start.24
  19.0 6.8 %collective-permute-start.1 = (bf16[16,5376]{1,0:T(8,128)(2,1)S(1)}, bf16[16,5376]{1,0:T(8,128)(2,1)S(1)}, u32[]{:S(2)}, u32[]{:S(2)}) collective-permute-start(bf16[16,5376]{1,0:T(8,128)(2,1)S(1)} %shard_map.102.after_ref.payload_ref), channel_id=1, source_target_pairs={{0,2},{1,3},{2,0},{3,1},{4,6},{5,7},{6,4},{7,5},{8,10},{9,11},{10,... | collective-permute-start | bytes 516104 | tf_op jit(solution)/shard_map/ppermute | solution.py:718
  20.7 5.1 %copy-start.1 = (bf16[16,6400]{1,0:T(8,128)(2,1)S(1)}, bf16[16,6400]{1,0:T(8,128)(2,1)}, u32[]{:S(2)}) copy-start(bf16[16,6400]{1,0:T(8,128)(2,1)} %get-tuple-element.23.after_ref.first_ref.payload_ref) | copy-start | bytes 614404
  20.7 5.0 %copy-start.4 = (bf16[320,128]{1,0:T(8,128)(2,1)S(1)}, bf16[320,128]{1,0:T(8,128)(2,1)}, u32[]{:S(2)}) copy-start(bf16[320,128]{1,0:T(8,128)(2,1)} %get-tuple-element.24.em_ref.refs_7_) | copy-start | bytes 245764
  24.1 2.5 %copy-start.13 = (f32[16,2560]{1,0:T(8,128)}, f32[16,2560]{1,0:T(8,128)S(1)}, u32[]{:S(2)}) copy-start(f32[16,2560]{1,0:T(8,128)S(1)} %get-tuple-element.37.refs_16_) | copy-start | bytes 491524
  26.6 7.3 %collective-permute-start.2 = (bf16[16,5376]{1,0:T(8,128)(2,1)S(1)}, bf16[16,5376]{1,0:T(8,128)(2,1)S(1)}, u32[]{:S(2)}, u32[]{:S(2)}) collective-permute-start(bf16[16,5376]{1,0:T(8,128)(2,1)S(1)} %shard_map.104.after_ref.payload_ref), channel_id=1, source_target_pairs={{0,6},{1,7},{2,4},{3,5},{4,2},{5,3},{6,0},{7,1},{8,14},{9,15},{10,... | collective-permute-start | bytes 516104 | tf_op jit(solution)/shard_map/ppermute | solution.py:718
  33.2 0.7 copy-start.15
  34.8 5.7 %collective-permute-start.3 = (bf16[16,5376]{1,0:T(8,128)(2,1)S(1)}, bf16[16,5376]{1,0:T(8,128)(2,1)S(1)}, u32[]{:S(2)}, u32[]{:S(2)}) collective-permute-start(bf16[16,5376]{1,0:T(8,128)(2,1)S(1)} %shard_map.106.after_ref.payload_ref), channel_id=1, source_target_pairs={{0,8},{1,9},{2,10},{3,11},{4,12},{5,13},{6,14},{7,15},{8,0},{9,1},... | collective-permute-start | bytes 516104 | tf_op jit(solution)/shard_map/ppermute | solution.py:718
  40.2 1.3 %copy-start.17 = (f32[16,2560]{1,0:T(8,128)}, f32[16,2560]{1,0:T(8,128)S(1)}, u32[]{:S(2)}) copy-start(f32[16,2560]{1,0:T(8,128)S(1)} %get-tuple-element.39.refs_18_) | copy-start | bytes 491524
  41.5 4.0 %copy-start.9 = (bf16[16,5376]{1,0:T(8,128)(2,1)}, bf16[16,5376]{1,0:T(8,128)(2,1)S(1)}, u32[]{:S(2)}) copy-start(bf16[16,5376]{1,0:T(8,128)(2,1)S(1)} %shard_map.108.after_ref.payload_ref) | copy-start | bytes 516100
  41.5 10.9 %collective-permute-start.4 = (bf16[16,5376]{1,0:T(8,128)(2,1)S(1)}, bf16[16,5376]{1,0:T(8,128)(2,1)S(1)}, u32[]{:S(2)}, u32[]{:S(2)}) collective-permute-start(bf16[16,5376]{1,0:T(8,128)(2,1)S(1)} %shard_map.108.after_ref.payload_ref), channel_id=1, source_target_pairs={{0,24},{1,25},{2,26},{3,27},{4,28},{5,29},{6,30},{7,31},{8,16},{9,... | collective-permute-start | bytes 516104 | tf_op jit(solution)/shard_map/ppermute | solution.py:718
  52.4 0.9 copy-start.10
  53.3 0.7 copy-start.25
  54.9 1.5 %copy-start.11 = (bf16[16,5376]{1,0:T(8,128)(2,1)}, bf16[16,5376]{1,0:T(8,128)(2,1)S(1)}, u32[]{:S(2)}) copy-start(bf16[16,5376]{1,0:T(8,128)(2,1)S(1)} %shard_map.110.after_ref.payload_ref) | copy-start | bytes 516100
  54.9 13.5 %copy-start.30 = (s32[128,16]{0,1:T(8,128)S(1)}, s32[128,16]{0,1:T(8,128)}, u32[]{:S(2)}) copy-start(s32[128,16]{0,1:T(8,128)} %param.13) | copy-start | bytes 24580
  54.9 8.5 %collective-permute-start.5 = (bf16[16,5376]{1,0:T(8,128)(2,1)S(1)}, bf16[16,5376]{1,0:T(8,128)(2,1)S(1)}, u32[]{:S(2)}, u32[]{:S(2)}) collective-permute-start(bf16[16,5376]{1,0:T(8,128)(2,1)S(1)} %shard_map.110.after_ref.payload_ref), channel_id=1, source_target_pairs={{0,32},{1,33},{2,34},{3,35},{4,36},{5,37},{6,38},{7,39},{8,40},{9,... | collective-permute-start | bytes 516104 | tf_op jit(solution)/shard_map/ppermute | solution.py:718
  63.3 0.9 copy-start.12
  64.3 0.7 copy-start.26
  64.9 8.9 %copy-start.6 = (bf16[16,256,256]{2,1,0:T(8,128)(2,1)S(1)}, bf16[16,256,256]{2,1,0:T(8,128)(2,1)}, u32[]{:S(2)}) copy-start(bf16[16,256,256]{2,1,0:T(8,128)(2,1)} %get-tuple-element.36.refs_15_) | copy-start | bytes 6291460
  66.3 7.6 %collective-permute-start.6 = (bf16[16,5376]{1,0:T(8,128)(2,1)}, bf16[16,5376]{1,0:T(8,128)(2,1)}, u32[]{:S(2)}, u32[]{:S(2)}) collective-permute-start(bf16[16,5376]{1,0:T(8,128)(2,1)} %shard_map.112.after_ref), channel_id=1, source_target_pairs={{0,96},{1,97},{2,98},{3,99},{4,100},{5,101},{6,102},{7,103},{8,104... | collective-permute-start | bytes 516104 | tf_op jit(solution)/shard_map/ppermute | solution.py:718
  68.6 0.9 copy-start.20
  69.5 0.9 copy-start.28
  70.4 3.4 %copy-start.2 = (bf16[16,512,256]{2,1,0:T(8,128)(2,1)S(1)}, bf16[16,512,256]{2,1,0:T(8,128)(2,1)}, u32[]{:S(2)}) copy-start(bf16[16,512,256]{2,1,0:T(8,128)(2,1)} %get-tuple-element.35.refs_14_) | copy-start | bytes 12582916
  70.5 3.4 %copy-start.5 = (bf16[17,256,256]{2,1,0:T(8,128)(2,1)S(1)}, bf16[17,256,256]{2,1,0:T(8,128)(2,1)}, u32[]{:S(2)}) copy-start(bf16[17,256,256]{2,1,0:T(8,128)(2,1)} %get-tuple-element.32.refs_9_) | copy-start | bytes 6684676
  70.5 3.4 %copy-start.22 = (bf16[192,128]{1,0:T(8,128)(2,1)S(1)}, bf16[192,128]{1,0:T(8,128)(2,1)}, u32[]{:S(2)}) copy-start(bf16[192,128]{1,0:T(8,128)(2,1)} %get-tuple-element.31.refs_8_) | copy-start | bytes 147460
  73.9 1.6 %copy-start.7 = (bf16[8,256,512]{2,1,0:T(8,128)(2,1)S(1)}, bf16[8,256,512]{2,1,0:T(8,128)(2,1)}, u32[]{:S(2)}) copy-start(bf16[8,256,512]{2,1,0:T(8,128)(2,1)} %get-tuple-element.33.refs_12_) | copy-start | bytes 6291460
  75.5 1.6 %copy-start.8 = (bf16[8,256,512]{2,1,0:T(8,128)(2,1)S(1)}, bf16[8,256,512]{2,1,0:T(8,128)(2,1)}, u32[]{:S(2)}) copy-start(bf16[8,256,512]{2,1,0:T(8,128)(2,1)} %get-tuple-element.34.refs_13_) | copy-start | bytes 6291460
  77.1 0.9 copy-start.14
  78.0 0.9 copy-start.16
  78.9 0.9 copy-start.18
  79.8 0.9 copy-start.21

commit v5 on v4

--- a/solution.py
+++ b/solution.py
@@ -294,19 +294,8 @@
     )
 
 
-def up_kernel(bits_ref, points_ref, coords_ref, basis_ref, local_ref, payload_ref, ub_ref, bd_ref, bdup_ref, rep_ref, x_ref, c_ref, y_ref):
-    step = pl.program_id(0)
-    lanes = iota((8, 256), 1) % 8
-    rows = iota((8, 256), 0)
-
-    @pl.when(step == 0)
-    def _():
-        rep_ref[...] = where_eq(iota((128, 1024), 0), iota((128, 1024), 1) // 8)
-        column = iota((512, 512), 1)
-        perm = where_eq(iota((512, 512), 0), (column % 8) * LEAF + column // 8)
-        stacked = jnp.concatenate([points_ref[:, 512 * g : 512 * g + 512] for g in range(GROUPS)], axis=0)
-        x_ref[...] = dot(stacked, perm).astype(bf16)
-    basis = basis_ref[...]
+def up_step(step, lanes, rows, basis_ref, local_ref, payload_ref, ub_ref, bd_ref, rep_ref, x_ref, c_ref):
+    basis = basis_ref[16 * step : 16 * step + 16, :]
     wide = dot(jnp.concatenate([basis[:, 128 * k : 128 * k + 128] for k in range(16)], axis=0), rep_ref[...])
     keep = lanes == rows
     for e in range(2):
@@ -315,8 +304,8 @@
             for q in (p, p + 1):
                 k, low = q // 4, q % 4
                 both.append(jnp.where(keep, wide[16 * k + 8 * e : 16 * k + 8 * e + 8, 256 * low : 256 * low + 256], 0.0))
-            ub_ref[e, 8 * p : 8 * p + 16, :] = jnp.concatenate(both, axis=0).astype(bf16)
-    local = local_ref[pl.ds(pl.multiple_of(16 * step, 16), 16), :]
+            ub_ref[2 * step + e, 8 * p : 8 * p + 16, :] = jnp.concatenate(both, axis=0).astype(bf16)
+    local = local_ref[16 * step : 16 * step + 16, :]
     wide = dot(jnp.concatenate([local[:, 128 * k : 128 * k + 128] for k in range(8)], axis=0), rep_ref[...])
     total = jnp.zeros((16, 256), f32)
     for e in range(2):
@@ -326,42 +315,71 @@
             for q in (a, a + 1):
                 k, low = q // 4, q % 4
                 both.append(jnp.where(keep, wide[16 * k + 8 * e : 16 * k + 8 * e + 8, 256 * low : 256 * low + 256], 0.0))
-            bd_ref[e, 8 * a : 8 * a + 16, :] = jnp.concatenate(both, axis=0).astype(bf16)
-        own = x_ref[pl.ds(pl.multiple_of(32 * step + 16 * e, 16), 16), :]
-        coeff = dot(own, ub_ref[e]).astype(bf16)
-        payload_ref[:, pl.ds(pl.multiple_of(512 * step + 256 * e, 256), 256)] = coeff
-        total = total + dot(coeff, bd_ref[e])
-    c_ref[pl.ds(pl.multiple_of(16 * step, 16), 16), :] = total
-
-    @pl.when(step == GROUPS // 2 - 1)
-    def _():
-        for k in range(8):
-            y_ref[k, 0:126, :] = dot(local_ref[128:254, 128 * k : 128 * k + 128], rep_ref[...])
-        tile = 0
-        for level_tiles in (8, 4, 2, 1):
-            for q in range(level_tiles):
-                fill_upper(y_ref, bdup_ref, tile, tile, lanes == rows // 2 + 4 * (q % 2))
-                tile += 1
-        fill_upper(y_ref, bdup_ref, 15, 15, (lanes == rows // 2 + 4) & (rows < 4))
-        fill_upper(y_ref, bdup_ref, 16, 15, (lanes == 0) & (rows >= 4) & (rows < 6))
-        current = [c_ref[16 * q : 16 * q + 16, :] for q in range(8)]
-        tile = 0
-        for level_tiles in (8, 4, 2, 1, 1, 1):
-            parts = [joined(dot(halves(current[q]), bdup_ref[tile + q])) for q in range(level_tiles)]
-            tile += level_tiles
-            if level_tiles > 1:
-                current = [parts[2 * q] + parts[2 * q + 1] for q in range(level_tiles // 2)]
-            else:
-                current = parts
-        squeeze = where_eq(iota((256, 128), 0), iota((256, 128), 1) * 8)
-        mine = joined(dot(halves(current[0]), squeeze))
-        zero = jnp.zeros_like(mine)
-        payload_ref[:, TABLE:EDGE] = pack_state(mine, zero, zero)
-        head = side(points_ref, coords_ref, 0)
-        tail = side(points_ref, coords_ref, (LEAF_DEV - SPAN) * LEAF)
-        even = bits_ref[0] == 0
-        payload_ref[:, EDGE:WIDTH] = jnp.where(even, tail, head)
-        payload_ref[:, WIDTH:] = jnp.where(even, head, tail)
+            bd_ref[2 * step + e, 8 * a : 8 * a + 16, :] = jnp.concatenate(both, axis=0).astype(bf16)
+        own = x_ref[32 * step + 16 * e : 32 * step + 16 * e + 16, :]
+        coeff = dot(own, ub_ref[2 * step + e]).astype(bf16)
+        payload_ref[:, 512 * step + 256 * e : 512 * step + 256 * e + 256] = coeff
+        total = total + dot(coeff, bd_ref[2 * step + e])
+    c_ref[16 * step : 16 * step + 16, :] = total
+
+
+def up_kernel(bits_ref, points_in, coords_in, basis_in, local_in, payload_ref, ub_out, bd_out, bdup_out, rep_ref, x_ref, c_ref, y_ref, points_ref, coords_ref, basis_ref, local_ref, ub_ref, bd_ref, bdup_ref, in_sem, out_sem):
+    arrivals = [
+        pltpu.make_async_copy(source, target, in_sem.at[k])
+        for k, (source, target) in enumerate(
+            ((points_in, points_ref), (basis_in, basis_ref), (local_in, local_ref), (coords_in, coords_ref))
+        )
+    ]
+    for copy in arrivals:
+        copy.start()
+    lanes = iota((8, 256), 1) % 8
+    rows = iota((8, 256), 0)
+    rep_ref[...] = where_eq(iota((128, 1024), 0), iota((128, 1024), 1) // 8)
+    column = iota((512, 512), 1)
+    perm = where_eq(iota((512, 512), 0), (column % 8) * LEAF + column // 8)
+    for copy in arrivals:
+        copy.wait()
+    stacked = jnp.concatenate([points_ref[:, 512 * g : 512 * g + 512] for g in range(GROUPS)], axis=0)
+    x_ref[...] = dot(stacked, perm).astype(bf16)
+    departures = []
+    for step in range(GROUPS // 2):
+        up_step(step, lanes, rows, basis_ref, local_ref, payload_ref, ub_ref, bd_ref, rep_ref, x_ref, c_ref)
+        part = pl.ds(2 * step, 2)
+        departures.append(pltpu.make_async_copy(ub_ref.at[part], ub_out.at[part], out_sem.at[step]))
+        departures[-1].start()
+    departures.append(pltpu.make_async_copy(bd_ref, bd_out, out_sem.at[8]))
+    departures[-1].start()
+    for k in range(8):
+        y_ref[k, 0:126, :] = dot(local_ref[128:254, 128 * k : 128 * k + 128], rep_ref[...])
+    tile = 0
+    for level_tiles in (8, 4, 2, 1):
+        for q in range(level_tiles):
+            fill_upper(y_ref, bdup_ref, tile, tile, lanes == rows // 2 + 4 * (q % 2))
+            tile += 1
+    fill_upper(y_ref, bdup_ref, 15, 15, (lanes == rows // 2 + 4) & (rows < 4))
+    fill_upper(y_ref, bdup_ref, 16, 15, (lanes == 0) & (rows >= 4) & (rows < 6))
+    departures.append(pltpu.make_async_copy(bdup_ref, bdup_out, out_sem.at[9]))
+    departures[-1].start()
+    current = [c_ref[16 * q : 16 * q + 16, :] for q in range(8)]
+    tile = 0
+    for level_tiles in (8, 4, 2, 1, 1, 1):
+        parts = [joined(dot(halves(current[q]), bdup_ref[tile + q])) for q in range(level_tiles)]
+        tile += level_tiles
+        if level_tiles > 1:
+            current = [parts[2 * q] + parts[2 * q + 1] for q in range(level_tiles // 2)]
+        else:
+            current = parts
+    squeeze = where_eq(iota((256, 128), 0), iota((256, 128), 1) * 8)
+    mine = joined(dot(halves(current[0]), squeeze))
+    zero = jnp.zeros_like(mine)
+    payload_ref[:, TABLE:EDGE] = pack_state(mine, zero, zero)
+    head = side(points_ref, coords_ref, 0)
+    tail = side(points_ref, coords_ref, (LEAF_DEV - SPAN) * LEAF)
+    even = bits_ref[0] == 0
+    payload_ref[:, EDGE:WIDTH] = jnp.where(even, tail, head)
+    payload_ref[:, WIDTH:] = jnp.where(even, head, tail)
+    for copy in departures:
+        copy.wait()
 
 
 def side(points_ref, coords_ref, start):
@@ -419,7 +437,7 @@
         in_specs=[pl.BlockSpec(memory_space=pltpu.SMEM), vmem, anywhere, anywhere],
         out_specs=(vmem, vmem, vmem),
         scratch_shapes=[pltpu.VMEM((6, 2, 1024), bf16), pltpu.SemaphoreType.DMA((6,))],
-        compiler_params=pltpu.CompilerParams(vmem_limit_bytes=60 * 1024 * 1024),
+        compiler_params=pltpu.CompilerParams(vmem_limit_bytes=8 * 1024 * 1024),
         cost_estimate=pl.CostEstimate(flops=100_000_000, bytes_accessed=800_000, transcendentals=0),
     )(nodes, top_transfer, top_coupling, after)
 
@@ -434,42 +452,40 @@
 
 
 def upward(bits, points, coords, basis, local_transfer):
-    full = lambda *shape: pl.BlockSpec(shape, lambda i: (0,) * len(shape))
+    vmem = pl.BlockSpec(memory_space=pltpu.VMEM)
+    hbm = pl.BlockSpec(memory_space=pltpu.HBM)
     return pl.pallas_call(
         up_kernel,
-        grid=(GROUPS // 2,),
         out_shape=(
             jax.ShapeDtypeStruct((16, FIRST), bf16),
             jax.ShapeDtypeStruct((GROUPS, 512, 256), bf16),
             jax.ShapeDtypeStruct((GROUPS, 256, 256), bf16),
             jax.ShapeDtypeStruct((UPPER, 256, 256), bf16),
         ),
-        in_specs=[
-            pl.BlockSpec(memory_space=pltpu.SMEM),
-            full(16, LEAF_DEV * LEAF),
-            full(3, LEAF_DEV * LEAF),
-            pl.BlockSpec((16, LEAF * RANK), lambda i: (i, 0)),
-            full(254, 1024),
-        ],
-        out_specs=(
-            full(16, FIRST),
-            pl.BlockSpec((2, 512, 256), lambda i: (i, 0, 0)),
-            pl.BlockSpec((2, 256, 256), lambda i: (i, 0, 0)),
-            full(UPPER, 256, 256),
-        ),
+        in_specs=[pl.BlockSpec(memory_space=pltpu.SMEM)] + [hbm] * 4,
+        out_specs=(vmem,) + (hbm,) * 3,
         scratch_shapes=[
             pltpu.VMEM((128, 1024), bf16),
             pltpu.VMEM((256, 512), bf16),
             pltpu.VMEM((128, 256), f32),
             pltpu.VMEM((8, 128, 1024), f32),
+            pltpu.VMEM((16, LEAF_DEV * LEAF), bf16),
+            pltpu.VMEM((3, LEAF_DEV * LEAF), f32),
+            pltpu.VMEM((LEAF_DEV, LEAF * RANK), bf16),
+            pltpu.VMEM((254, 1024), bf16),
+            pltpu.VMEM((GROUPS, 512, 256), bf16),
+            pltpu.VMEM((GROUPS, 256, 256), bf16),
+            pltpu.VMEM((UPPER, 256, 256), bf16),
+            pltpu.SemaphoreType.DMA((4,)),
+            pltpu.SemaphoreType.DMA((10,)),
         ],
         compiler_params=pltpu.CompilerParams(vmem_limit_bytes=60 * 1024 * 1024),
         cost_estimate=pl.CostEstimate(flops=1_000_000_000, bytes_accessed=10_000_000, transcendentals=0),
     )(bits, points, coords, basis, local_transfer)
 
 
-def step_kernel(height, bits_ref, first_ref, payload_ref, received_ref, em_ref, after_ref, next_ref):
-    del after_ref
+def step_kernel(height, bits_ref, first_ref, payload_ref, received_ref, em_ref, *rest):
+    next_ref = rest[-1]
     forward = height % 2 == 1
     next_ref[:, :TABLE] = received_ref[:, :TABLE] if forward else first_ref[:, :TABLE]
     start = WIDTH if height == 0 else EDGE
@@ -487,16 +503,16 @@
     next_ref[:, TABLE:EDGE] = pack_state(parent, mine, sibling)
 
 
-def tree_step(height, bits, first, payload, received, em, after):
+def tree_step(height, bits, first, payload, received, em, *after):
     vmem = pl.BlockSpec(memory_space=pltpu.VMEM)
     return pl.pallas_call(
         functools.partial(step_kernel, height),
         out_shape=jax.ShapeDtypeStruct((16, WIDTH), bf16),
-        in_specs=[pl.BlockSpec(memory_space=pltpu.SMEM)] + [vmem] * 4 + [pl.BlockSpec(memory_space=pl.ANY)],
+        in_specs=[pl.BlockSpec(memory_space=pltpu.SMEM)] + [vmem] * 4 + [pl.BlockSpec(memory_space=pl.ANY)] * len(after),
         out_specs=vmem,
         compiler_params=pltpu.CompilerParams(vmem_limit_bytes=4 * 1024 * 1024),
         cost_estimate=pl.CostEstimate(flops=1_000_000, bytes_accessed=400_000, transcendentals=0),
-    )(bits, first, payload, received, em, after)
+    )(bits, first, payload, received, em, *after)
 
 
 def regroup_kernel(c_ref, after_ref, out_ref, token_ref):
@@ -545,134 +561,139 @@
             pl.BlockSpec((1, 256, 512), lambda i: (i, 0, 0)),
             pl.BlockSpec((8, 128), lambda i: (0, 0)),
         ),
-        compiler_params=pltpu.CompilerParams(vmem_limit_bytes=60 * 1024 * 1024),
+        compiler_params=pltpu.CompilerParams(vmem_limit_bytes=12 * 1024 * 1024),
         cost_estimate=pl.CostEstimate(flops=600_000_000, bytes_accessed=4_200_000, transcendentals=0),
     )(far_coupling, after)
 
 
 def down_kernel(bits_ref, index_ref, payload_ref, *refs):
     received = refs[:7]
-    em_ref, sm_ref, bdup_ref, coords_ref, rel_ref, d0_ref, d1_ref, ub_ref, bd_ref, near0_ref, near1_ref, near2_ref, near3_ref, out_ref, table_ref, field_ref, far_ref, gather_ref, edge_ref = refs[7:]
-    step = pl.program_id(0)
-
-    @pl.when(step == 0)
-    def _():
-        column = iota((256, 1024), 1)
-        repeat = where_eq(iota((256, 1024), 0), (column % RANK) * 8 + column // 128)
-        for k, ref in enumerate((payload_ref,) + received):
-            stacked = jnp.concatenate([ref[:, 256 * g : 256 * g + 256] for g in range(GROUPS)], axis=0)
-            wide = dot(stacked, repeat).astype(bf16)
-            for m in range(8):
-                table_ref[2048 * k + 256 * m : 2048 * k + 256 * m + 256, :] = wide[:, 128 * m : 128 * m + 128]
-        table_ref[16384:16400, :] = jnp.zeros((16, 128), bf16)
-        terms = []
-        for height in range(1, 7):
-            _, before_mine, before_sibling = unpack_state(received[height][:, TABLE:EDGE])
-            plain = (bits_ref[height - 1] == 0) == (height % 2 == 1)
-            left = jnp.where(plain, before_mine, before_sibling)
-            right = jnp.where(plain, before_sibling, before_mine)
-            both = left + pltpu.roll(right, 32, 1)
-            terms.append(joined(dot_nt(halves(both), sm_ref[32 * height - 32 : 32 * height, :])))
-        field = terms[5]
-        for height in range(5, 0, -1):
-            row = pl.multiple_of(64 * (height - 1) + 32 * bits_ref[height - 1], 32)
-            matrix = em_ref[pl.ds(row, 32), 0:RANK]
-            field = terms[height - 1] + joined(dot_nt(halves(field), matrix))
-        stretch = where_eq(iota((RANK, 256), 0) * 8, iota((RANK, 256), 1))
-        fields = [joined(dot(halves(field), stretch))]
-        tile = UPPER
-        for level_tiles in (1, 1, 1, 2, 4, 8):
-            tile -= level_tiles
-            fields = [
-                joined(dot_nt(halves(fields[q // 2 if level_tiles > 1 else 0]), bdup_ref[tile + q]))
-                for q in range(level_tiles)
-            ]
-        near_side = received[0][:, EDGE:WIDTH]
-        far_side = received[1][:, EDGE:WIDTH]
-        for height in range(2, 7):
-            far_side = jnp.where(bits_ref[7] == height, received[height][:, EDGE:WIDTH], far_side)
-        even = bits_ref[0] == 0
-        left_halo = jnp.where(even, far_side, near_side)
-        right_halo = jnp.where(even, near_side, far_side)
-
-        def add(own, acc):
-            edge_ref[own % 4] = acc
-
-        edge_products(left_halo, right_halo, coords_ref, rel_ref, add)
-        for q in range(8):
-            field_ref[32 * q : 32 * q + 32, :] = halves(fields[q])
-
+    em_ref, sm_ref, coords_ref, rel_ref, bdup_in, d0_ref, d1_ref, bd_in, ub_in, near0_ref, near1_ref, near2_ref, near3_ref, out_ref, table_ref, field_ref, far_ref, gather_ref, edge_ref, d_ref, bdup_ref, bd_ref, ub_ref, sem = refs[7:]
+    half = GROUPS // 2
+    copies = [
+        pltpu.make_async_copy(source, target, sem.at[k])
+        for k, (source, target) in enumerate(
+            (
+                (bdup_in, bdup_ref),
+                (d0_ref, d_ref.at[pl.ds(0, half)]),
+                (bd_in, bd_ref),
+                (ub_in, ub_ref),
+                (d1_ref, d_ref.at[pl.ds(half, half)]),
+            )
+        )
+    ]
+    for copy in copies:
+        copy.start()
+
+    column = iota((256, 1024), 1)
+    repeat = where_eq(iota((256, 1024), 0), (column % RANK) * 8 + column // 128)
+    for k, ref in enumerate((payload_ref,) + received):
+        stacked = jnp.concatenate([ref[:, 256 * g : 256 * g + 256] for g in range(GROUPS)], axis=0)
+        wide = dot(stacked, repeat).astype(bf16)
+        for m in range(8):
+            table_ref[2048 * k + 256 * m : 2048 * k + 256 * m + 256, :] = wide[:, 128 * m : 128 * m + 128]
+    table_ref[16384:16400, :] = jnp.zeros((16, 128), bf16)
+    terms = []
+    for height in range(1, 7):
+        _, before_mine, before_sibling = unpack_state(received[height][:, TABLE:EDGE])
+        plain = (bits_ref[height - 1] == 0) == (height % 2 == 1)
+        left = jnp.where(plain, before_mine, before_sibling)
+        right = jnp.where(plain, before_sibling, before_mine)
+        both = left + pltpu.roll(right, 32, 1)
+        terms.append(joined(dot_nt(halves(both), sm_ref[32 * height - 32 : 32 * height, :])))
+    field = terms[5]
+    for height in range(5, 0, -1):
+        row = pl.multiple_of(64 * (height - 1) + 32 * bits_ref[height - 1], 32)
+        matrix = em_ref[pl.ds(row, 32), 0:RANK]
+        field = terms[height - 1] + joined(dot_nt(halves(field), matrix))
+    stretch = where_eq(iota((RANK, 256), 0) * 8, iota((RANK, 256), 1))
+    fields = [joined(dot(halves(field), stretch))]
+    copies[0].wait()
+    tile = UPPER
+    for level_tiles in (1, 1, 1, 2, 4, 8):
+        tile -= level_tiles
+        fields = [
+            joined(dot_nt(halves(fields[q // 2 if level_tiles > 1 else 0]), bdup_ref[tile + q]))
+            for q in range(level_tiles)
+        ]
+    near_side = received[0][:, EDGE:WIDTH]
+    far_side = received[1][:, EDGE:WIDTH]
+    for height in range(2, 7):
+        far_side = jnp.where(bits_ref[7] == height, received[height][:, EDGE:WIDTH], far_side)
+    even = bits_ref[0] == 0
+    left_halo = jnp.where(even, far_side, near_side)
+    right_halo = jnp.where(even, near_side, far_side)
+
+    def add(own, acc):
+        edge_ref[own % 4] = acc
+
+    edge_products(left_halo, right_halo, coords_ref, rel_ref, add)
+    for q in range(8):
+        field_ref[32 * q : 32 * q + 32, :] = halves(fields[q])
+    for copy in copies[1:]:
+        copy.wait()
     block = iota((16, 128), 1) // RANK
-    for leaf in range(8):
-        for s_high in range(4):
-            merged = None
-            for low in range(4):
-                entry = index_ref[(8 * step + leaf) * NF + 4 * s_high + low]
-                value = table_ref[pl.ds(pl.multiple_of(entry * 16, 16), 16), :]
-                merged = value if low == 0 else jnp.where(block == low, value, merged)
-            gather_ref[16 * leaf : 16 * leaf + 16, 128 * s_high : 128 * s_high + 128] = merged
-    coupling = jnp.where(step < GROUPS // 2, d0_ref[0], d1_ref[0])
-    result = dot_nt(gather_ref[...], coupling)
     which = iota((16, 256), 1) % 8
-    far = result[0:16]
-    for leaf in range(1, 8):
-        far = jnp.where(which == leaf, result[16 * leaf : 16 * leaf + 16], far)
-    parent = field_ref[pl.ds(pl.multiple_of(32 * (step // 2), 32), 32), :]
-    leaf_field = (far + joined(dot_nt(parent, bd_ref[0]))).astype(bf16)
-    part = dot_nt(leaf_field, ub_ref[0])
-    high = part.astype(bf16)
-    far_ref[pl.ds(pl.multiple_of(16 * step, 16), 16), :] = high
-    far_ref[pl.ds(pl.multiple_of(256 + 16 * step, 16), 16), :] = (part - high.astype(f32)).astype(bf16)
-
-    @pl.when(step == GROUPS - 1)
-    def _():
-        column = iota((512, 512), 1)
-        perm = where_eq(iota((512, 512), 0), (column % LEAF) * 8 + column // LEAF)
-        whole = joined(dot(far_ref[...], perm))
-        nears = (near0_ref, near1_ref, near2_ref, near3_ref)
-        for g in range(GROUPS):
-            per = GROUPS // CHUNKS
-            chunk, place = g // per, 512 * (g % per)
-            value = nears[chunk][:, place : place + 512] + whole[16 * g : 16 * g + 16, :]
-            if chunk and g % per == 0:
-                value = value + nears[chunk - 1][:, 512 * per : 512 * per + 512]
-            if g == 0:
-                value = value + jnp.concatenate([edge_ref[0], edge_ref[1]], axis=1)
-            if g == GROUPS - 1:
-                value = value + jnp.concatenate([edge_ref[2], edge_ref[3]], axis=1)
-            out_ref[:, 512 * g : 512 * g + 512] = value
+    for step in range(GROUPS):
+        for leaf in range(8):
+            for s_high in range(4):
+                merged = None
+                for low in range(4):
+                    entry = index_ref[(8 * step + leaf) * NF + 4 * s_high + low]
+                    value = table_ref[pl.ds(pl.multiple_of(entry, 16), 16), :]
+                    merged = value if low == 0 else jnp.where(block == low, value, merged)
+                gather_ref[step % 2, 16 * leaf : 16 * leaf + 16, 128 * s_high : 128 * s_high + 128] = merged
+        result = dot_nt(gather_ref[step % 2], d_ref[step])
+        far = result[0:16]
+        for leaf in range(1, 8):
+            far = jnp.where(which == leaf, result[16 * leaf : 16 * leaf + 16], far)
+        parent = field_ref[32 * (step // 2) : 32 * (step // 2) + 32, :]
+        leaf_field = (far + joined(dot_nt(parent, bd_ref[step]))).astype(bf16)
+        part = dot_nt(leaf_field, ub_ref[step])
+        high = part.astype(bf16)
+        far_ref[16 * step : 16 * step + 16, :] = high
+        far_ref[256 + 16 * step : 272 + 16 * step, :] = (part - high.astype(f32)).astype(bf16)
+    column = iota((512, 512), 1)
+    perm = where_eq(iota((512, 512), 0), (column % LEAF) * 8 + column // LEAF)
+    whole = joined(dot(far_ref[...], perm))
+    nears = (near0_ref, near1_ref, near2_ref, near3_ref)
+    for g in range(GROUPS):
+        per = GROUPS // CHUNKS
+        chunk, place = g // per, 512 * (g % per)
+        value = nears[chunk][:, place : place + 512] + whole[16 * g : 16 * g + 16, :]
+        if chunk and g % per == 0:
+            value = value + nears[chunk - 1][:, 512 * per : 512 * per + 512]
+        if g == 0:
+            value = value + jnp.concatenate([edge_ref[0], edge_ref[1]], axis=1)
+        if g == GROUPS - 1:
+            value = value + jnp.concatenate([edge_ref[2], edge_ref[3]], axis=1)
+        out_ref[:, 512 * g : 512 * g + 512] = value
 
 
 def downward(bits, index, payload, received, em, sm, bdup, coords, near_rel, d, ub, bd, nears):
-    full = lambda *shape: pl.BlockSpec(shape, lambda i: (0,) * len(shape))
     smem = pl.BlockSpec(memory_space=pltpu.SMEM)
-    each = lambda *shape: pl.BlockSpec((1,) + shape, lambda i: (i, 0, 0))
+    vmem = pl.BlockSpec(memory_space=pltpu.VMEM)
+    hbm = pl.BlockSpec(memory_space=pltpu.HBM)
     return pl.pallas_call(
         down_kernel,
-        grid=(GROUPS,),
         out_shape=jax.ShapeDtypeStruct((16, LEAF_DEV * LEAF), f32),
-        in_specs=[smem, smem]
-        + [full(16, FIRST)] * 2
-        + [full(16, WIDTH)] * 6
-        + [full(320, 128), full(192, 128), full(UPPER, 256, 256)]
-        + [full(3, LEAF_DEV * LEAF), full(NN, LEAF_DEV)]
-        + [
-            pl.BlockSpec((1, 256, 512), lambda i: (jnp.minimum(i, GROUPS // 2 - 1), 0, 0)),
-            pl.BlockSpec((1, 256, 512), lambda i: (jnp.maximum(i - GROUPS // 2, 0), 0, 0)),
-        ]
-        + [each(512, 256), each(256, 256)]
-        + [full(16, (LEAF_DEV // BL // CHUNKS + 2) * BLK)] * CHUNKS,
-        out_specs=full(16, LEAF_DEV * LEAF),
+        in_specs=[smem, smem] + [vmem] * 12 + [hbm] * 5 + [vmem] * CHUNKS,
+        out_specs=vmem,
         scratch_shapes=[
             pltpu.VMEM((16400, 128), bf16),
             pltpu.VMEM((256, 256), bf16),
             pltpu.VMEM((512, 512), bf16),
-            pltpu.VMEM((128, 512), bf16),
+            pltpu.VMEM((2, 128, 512), bf16),
             pltpu.VMEM((4, 16, BLK), f32),
+            pltpu.VMEM((GROUPS, 256, 512), bf16),
+            pltpu.VMEM((UPPER, 256, 256), bf16),
+            pltpu.VMEM((GROUPS, 256, 256), bf16),
+            pltpu.VMEM((GROUPS, 512, 256), bf16),
+            pltpu.SemaphoreType.DMA((5,)),
         ],
-        compiler_params=pltpu.CompilerParams(vmem_limit_bytes=24 * 1024 * 1024),
+        compiler_params=pltpu.CompilerParams(vmem_limit_bytes=40 * 1024 * 1024),
         cost_estimate=pl.CostEstimate(flops=3_000_000_000, bytes_accessed=16_000_000, transcendentals=0),
-    )(bits, index, payload, *received, em, sm, bdup, coords, near_rel, *d, ub, bd, *nears)
+    )(bits, index, payload, *received, em, sm, coords, near_rel, bdup, *d, bd, ub, *nears)
 
 
 def top_start(height, number):
@@ -706,7 +727,7 @@
     slot = sum((owner >> k > 0).astype(jnp.int32) for k in range(7))
     within = far_list & (LEAF_DEV - 1)
     entry = slot * LEAF_DEV + (within & 7) * GROUPS + (within >> 3)
-    index = jnp.where(far_list >= 0, entry, 8 * LEAF_DEV).reshape(LEAF_DEV * NF)
+    index = 16 * jnp.where(far_list >= 0, entry, 8 * LEAF_DEV).reshape(LEAF_DEV * NF)
     payload, ub, bd, bdup = upward(bits, points, coords, basis, local_transfer)
     near_rel = jnp.transpose(jnp.where(near_list >= 0, near_list - device * LEAF_DEV, -1000))
     first = payload
@@ -725,7 +746,8 @@
             part, token = near_chunk(len(nears), coords, points, near_rel, payload)
             nears.append(part)
         if height < 6:
-            payload = tree_step(height, bits, first, payload, received[height], em, token)
+            extra = (token, index) if height == 1 else (token,)
+            payload = tree_step(height, bits, first, payload, received[height], em, *extra)
     return downward(bits, index, first, received, em, sm, bdup, coords, near_rel, halves_of, ub, bd, nears)
 
 

time: 96.7 us -> 69.7 us (0.72); the launches traced: 95.5 us -> 69.5 us
  Pallas kernels: 62.2 us -> 46.8 us
  local copies, waits for them, and re-layouts: 15.3 us -> 2.14 us
  waiting for transfers between devices: 2.14 us -> 4.14 us
  starting transfers between devices: 14.4 us -> 15.4 us
    unnamed x64 -> x28, local copies, waits for them, and re-layouts: 15.1 us -> 1.95 us
    pallas_call x2, Pallas kernels: 13.9 us -> 5.95 us  [regroup(): pl.pallas_call(regroup_kernel, grid=(groups,), out_shape=(jax.ShapeDtypeS...]
    pallas_call x2, Pallas kernels: 25.9 us -> 20.8 us  [the longest x1 12.2 us: downward(): pl.pallas_call(down_kernel, out_shape=jax.ShapeDtypeStruct((16, LEAF_DEV...]
    ppermute x7, waiting for transfers between devices: 2.14 us -> 4.14 us  [per_device(): received.append(lax.ppermute(payload, 'leaf', route))]
    pallas_call x1, Pallas kernels: 3.03 us -> 1.46 us  [opened_top(): pl.pallas_call(open_kernel, out_shape=(jax.ShapeDtypeStruct((320, 128), b...]
    ppermute x7, starting transfers between devices: 14.4 us -> 15.4 us  [per_device(): received.append(lax.ppermute(payload, 'leaf', route))]
  transfers between devices with their start and end apart: 7 -> 7, of which waited for: 3 -> 6; matrix products, arithmetic and copies ran while one was open for 1% -> 0% of each run, Pallas kernels for 32% -> 30%
where the time goes in v5:
time: 69.7 us; the launch traced here: 69.5 us
  Pallas kernels  46.8 us (67%)
  starting transfers between devices  15.4 us (22%)
  waiting for transfers between devices  4.14 us (6%)
  local copies, waits for them, and re-layouts  2.14 us (3%)
    ppermute x7, starting transfers between devices, per_device(): received.append(lax.ppermute(payload, 'leaf', route))  15.4 us
    pallas_call x4, Pallas kernels, near_chunk(): pl.pallas_call(functools.partial(near_kernel, chunk, blocks), out_shape=(...  13.6 us
    pallas_call x1, Pallas kernels, downward(): pl.pallas_call(down_kernel, out_shape=jax.ShapeDtypeStruct((16, LEAF_DEV...  12.2 us
    pallas_call x1, Pallas kernels, upward(): pl.pallas_call(up_kernel, out_shape=(jax.ShapeDtypeStruct((16, FIRST), bf...  8.55 us
    pallas_call x2, Pallas kernels, regroup(): pl.pallas_call(regroup_kernel, grid=(groups,), out_shape=(jax.ShapeDtypeS...  5.95 us
    pallas_call x6, Pallas kernels, tree_step(): pl.pallas_call(functools.partial(step_kernel, height), out_shape=jax.Shap...  5 us
    ppermute x7, waiting for transfers between devices, per_device(): received.append(lax.ppermute(payload, 'leaf', route))  4.14 us
    unnamed x28, local copies, waits for them, and re-layouts  1.95 us
  transfers between devices with their start and end apart: 7, of which 6 were waited for; matrix products, arithmetic and copies ran while one was open for 0% of the time, Pallas kernels for 30%

profile of v5, /device:TPU:0, one launch (start us, length us, event | category | flops | bytes accessed | tf_op | source)
XLA Modules:
  0.0 69.5 jit_solution(14938602499618126944)
XLA Ops:
  0.0 0.5 compare_select_fusion.bits_ref
  0.5 8.6 %shard_map.100 = (bf16[16,6400]{1,0:T(8,128)(2,1)}, bf16[16,512,256]{2,1,0:T(8,128)(2,1)}, bf16[16,256,256]{2,1,0:T(8,128)(2,1)}, bf16[17,256,256]{2,1,0:T(8,128)(2,1)}) custom-call(s32[8]{0:T(128)} %compare_select_fusion.bits_ref, bf16[16,8192]{1,0:T(8,128)(2,1)} %points_ref.7, f32[3,8192]{1,0:T(4,128)} %refs_9_.1, bf16[128,2048]{1,0:T(8,128)(2,1)} %basis_in.1, ...), custom_call_target="tpu_custom_call" | custom-call | flops 1000000000 | bytes 10000000 | tf_op jit(solution)/shard_map/pallas_call | solution.py:457
  9.1 0.0 copy-start.12
  9.1 0.1 collective-permute-start
  9.2 0.0 copy-done.13
  9.2 0.1 pad_add_fusion.nodes_ref
  9.3 0.0 copy-done.6
  9.3 0.0 copy-done.7
  9.3 0.9 %copy-done.1 = bf16[16,6400]{1,0:T(8,128)(2,1)S(1)} copy-done((bf16[16,6400]{1,0:T(8,128)(2,1)S(1)}, bf16[16,6400]{1,0:T(8,128)(2,1)}, u32[]{:S(2)}) %copy-start.1) | copy-done | bytes 204824
  10.2 1.5 %shard_map.101 = (bf16[320,128]{1,0:T(8,128)(2,1)S(1)}, bf16[192,128]{1,0:T(8,128)(2,1)S(1)}, f32[8,128]{1,0:T(8,128)S(1)}) custom-call(s32[16]{0:T(128)S(1)} %pad_add_fusion.nodes_ref, bf16[254,1024]{1,0:T(8,128)(2,1)S(1)} %copy-done.7, bf16[252,2,1024]{2,1,0:T(2,128)(2,1)S(1)} %copy-done.6, bf16[16,6400]{1,0:T(8,128)(2,1)S(1)} %copy-done.1), custom_call_target="tpu_custom_call" | custom-call | flops 100000000 | bytes 800000 | tf_op jit(solution)/shard_map/pallas_call | solution.py:430
  11.7 0.0 copy-done.11
  11.8 0.0 collective-permute-done.received_ref.refs_0_
  11.8 0.0 copy-done.9
  11.8 0.0 copy-start.2
  11.8 0.9 %copy-done.2 = bf16[16,6400]{1,0:T(8,128)(2,1)S(1)} copy-done((bf16[16,6400]{1,0:T(8,128)(2,1)S(1)}, bf16[16,6400]{1,0:T(8,128)(2,1)}, u32[]{:S(2)}) %copy-start.2) | copy-done | bytes 204824
  12.7 0.9 %shard_map.102.after_ref.payload_ref = bf16[16,5376]{1,0:T(8,128)(2,1)S(1)} custom-call(s32[8]{0:T(128)S(1)} %copy-done.9, bf16[16,6400]{1,0:T(8,128)(2,1)S(1)} %copy-done.2, bf16[16,6400]{1,0:T(8,128)(2,1)S(1)} %copy-done.2, bf16[16,6400]{1,0:T(8,128)(2,1)S(1)} %collective-permute-done.received_ref.refs_0_, ...), custom_call_target="tpu_custom_call" | custom-call | flops 1000000 | bytes 400000 | tf_op jit(solution)/shard_map/pallas_call | solution.py:508
  13.6 1.7 %collective-permute-start.1 = (bf16[16,5376]{1,0:T(8,128)(2,1)S(1)}, bf16[16,5376]{1,0:T(8,128)(2,1)S(1)}, u32[]{:S(2)}, u32[]{:S(2)}) collective-permute-start(bf16[16,5376]{1,0:T(8,128)(2,1)S(1)} %shard_map.102.after_ref.payload_ref), channel_id=1, source_target_pairs={{0,2},{1,3},{2,0},{3,1},{4,6},{5,7},{6,4},{7,5},{8,10},{9,11},{10,... | collective-permute-start | bytes 516104 | tf_op jit(solution)/shard_map/ppermute | solution.py:739
  15.3 0.0 copy-done.12
  15.3 0.1 copy.11
  15.4 0.1 mul.30.rest_1_.index_ref
  15.5 0.0 copy-done.8
  15.5 0.0 copy-done.10
  15.5 0.0 copy-start.3
  15.5 3.4 %shard_map.103 = (f32[16,2560]{1,0:T(8,128)S(1)}, f32[8,128]{1,0:T(8,128)S(1)}) custom-call(f32[3,8192]{1,0:T(4,128)S(1)} %copy-done.8, bf16[16,8192]{1,0:T(8,128)(2,1)S(1)} %copy-done.10, s32[12,128]{1,0:T(8,128)S(1)} %select_bitcast_fusion.rel_ref.refs_10_, bf16[16,5376]{1,0:T(8,128)(2,1)S(1)} %shard_map.102.after_ref.payload_ref), custom_call_target="tpu_custom_call" | custom-call | flops 1000000000 | bytes 1000000 | tf_op jit(solution)/shard_map/pallas_call | solution.py:188
  18.9 1.5 %collective-permute-done.1.received_ref.refs_1_ = bf16[16,5376]{1,0:T(8,128)(2,1)S(1)} collective-permute-done((bf16[16,5376]{1,0:T(8,128)(2,1)S(1)}, bf16[16,5376]{1,0:T(8,128)(2,1)S(1)}, u32[]{:S(2)}, u32[]{:S(2)}) %collective-permute-start.1) | collective-permute-done | bytes 172064 | tf_op jit(solution)/shard_map/ppermute | solution.py:739
  20.3 0.0 copy-done.3
  20.4 0.9 %shard_map.104.after_ref.payload_ref = bf16[16,5376]{1,0:T(8,128)(2,1)S(1)} custom-call(s32[8]{0:T(128)S(1)} %copy-done.9, bf16[16,6400]{1,0:T(8,128)(2,1)S(1)} %copy-done.3, bf16[16,5376]{1,0:T(8,128)(2,1)S(1)} %shard_map.102.after_ref.payload_ref, bf16[16,5376]{1,0:T(8,128)(2,1)S(1)} %collective-permute-done.1.received_ref.refs_1_, ...), custom_call_target="tpu_custom_call" | custom-call | flops 1000000 | bytes 400000 | tf_op jit(solution)/shard_map/pallas_call | solution.py:508
  21.2 3.1 %collective-permute-start.2 = (bf16[16,5376]{1,0:T(8,128)(2,1)S(1)}, bf16[16,5376]{1,0:T(8,128)(2,1)S(1)}, u32[]{:S(2)}, u32[]{:S(2)}) collective-permute-start(bf16[16,5376]{1,0:T(8,128)(2,1)S(1)} %shard_map.104.after_ref.payload_ref), channel_id=1, source_target_pairs={{0,6},{1,7},{2,4},{3,5},{4,2},{5,3},{6,0},{7,1},{8,14},{9,15},{10,... | collective-permute-start | bytes 516104 | tf_op jit(solution)/shard_map/ppermute | solution.py:739
  24.4 3.4 %shard_map.105 = (f32[16,2560]{1,0:T(8,128)S(1)}, f32[8,128]{1,0:T(8,128)S(1)}) custom-call(f32[3,8192]{1,0:T(4,128)S(1)} %copy-done.8, bf16[16,8192]{1,0:T(8,128)(2,1)S(1)} %copy-done.10, s32[12,128]{1,0:T(8,128)S(1)} %select_bitcast_fusion.rel_ref.refs_10_, bf16[16,5376]{1,0:T(8,128)(2,1)S(1)} %shard_map.104.after_ref.payload_ref), custom_call_target="tpu_custom_call" | custom-call | flops 1000000000 | bytes 1000000 | tf_op jit(solution)/shard_map/pallas_call | solution.py:188
  27.8 0.8 %collective-permute-done.2.received_ref.refs_2_ = bf16[16,5376]{1,0:T(8,128)(2,1)S(1)} collective-permute-done((bf16[16,5376]{1,0:T(8,128)(2,1)S(1)}, bf16[16,5376]{1,0:T(8,128)(2,1)S(1)}, u32[]{:S(2)}, u32[]{:S(2)}) %collective-permute-start.2) | collective-permute-done | bytes 172064 | tf_op jit(solution)/shard_map/ppermute | solution.py:739
  28.6 0.9 %shard_map.106.after_ref.payload_ref = bf16[16,5376]{1,0:T(8,128)(2,1)S(1)} custom-call(s32[8]{0:T(128)S(1)} %copy-done.9, bf16[16,6400]{1,0:T(8,128)(2,1)S(1)} %copy-done.3, bf16[16,5376]{1,0:T(8,128)(2,1)S(1)} %shard_map.104.after_ref.payload_ref, bf16[16,5376]{1,0:T(8,128)(2,1)S(1)} %collective-permute-done.2.received_ref.refs_2_, ...), custom_call_target="tpu_custom_call" | custom-call | flops 1000000 | bytes 400000 | tf_op jit(solution)/shard_map/pallas_call | solution.py:508
  29.5 1.9 %collective-permute-start.3 = (bf16[16,5376]{1,0:T(8,128)(2,1)S(1)}, bf16[16,5376]{1,0:T(8,128)(2,1)S(1)}, u32[]{:S(2)}, u32[]{:S(2)}) collective-permute-start(bf16[16,5376]{1,0:T(8,128)(2,1)S(1)} %shard_map.106.after_ref.payload_ref), channel_id=1, source_target_pairs={{0,8},{1,9},{2,10},{3,11},{4,12},{5,13},{6,14},{7,15},{8,0},{9,1},... | collective-permute-start | bytes 516104 | tf_op jit(solution)/shard_map/ppermute | solution.py:739
  31.4 3.4 %shard_map.107 = (f32[16,2560]{1,0:T(8,128)S(1)}, f32[8,128]{1,0:T(8,128)S(1)}) custom-call(f32[3,8192]{1,0:T(4,128)S(1)} %copy-done.8, bf16[16,8192]{1,0:T(8,128)(2,1)S(1)} %copy-done.10, s32[12,128]{1,0:T(8,128)S(1)} %select_bitcast_fusion.rel_ref.refs_10_, bf16[16,5376]{1,0:T(8,128)(2,1)S(1)} %shard_map.106.after_ref.payload_ref), custom_call_target="tpu_custom_call" | custom-call | flops 1000000000 | bytes 1000000 | tf_op jit(solution)/shard_map/pallas_call | solution.py:188
  34.8 0.1 collective-permute-done.3.received_ref.refs_3_
  34.9 0.9 %shard_map.108.after_ref.payload_ref = bf16[16,5376]{1,0:T(8,128)(2,1)S(1)} custom-call(s32[8]{0:T(128)S(1)} %copy-done.9, bf16[16,6400]{1,0:T(8,128)(2,1)S(1)} %copy-done.3, bf16[16,5376]{1,0:T(8,128)(2,1)S(1)} %shard_map.106.after_ref.payload_ref, bf16[16,5376]{1,0:T(8,128)(2,1)S(1)} %collective-permute-done.3.received_ref.refs_3_, ...), custom_call_target="tpu_custom_call" | custom-call | flops 1000000 | bytes 400000 | tf_op jit(solution)/shard_map/pallas_call | solution.py:508
  35.8 4.2 %collective-permute-start.4 = (bf16[16,5376]{1,0:T(8,128)(2,1)S(1)}, bf16[16,5376]{1,0:T(8,128)(2,1)S(1)}, u32[]{:S(2)}, u32[]{:S(2)}) collective-permute-start(bf16[16,5376]{1,0:T(8,128)(2,1)S(1)} %shard_map.108.after_ref.payload_ref), channel_id=1, source_target_pairs={{0,24},{1,25},{2,26},{3,27},{4,28},{5,29},{6,30},{7,31},{8,16},{9,... | collective-permute-start | bytes 516104 | tf_op jit(solution)/shard_map/ppermute | solution.py:739
  40.0 3.0 %shard_map.109 = (bf16[8,256,512]{2,1,0:T(8,128)(2,1)S(1)}, f32[8,128]{1,0:T(8,128)S(1)}) custom-call(bf16[128,16,1024]{2,1,0:T(8,128)(2,1)S(1)} %copy-done, bf16[16,5376]{1,0:T(8,128)(2,1)S(1)} %shard_map.108.after_ref.payload_ref), custom_call_target="tpu_custom_call" | custom-call | flops 600000000 | bytes 4200000 | tf_op jit(solution)/shard_map/pallas_call | solution.py:549
  43.0 0.4 collective-permute-done.4.received_ref.refs_4_
  43.4 0.9 %shard_map.110.after_ref.payload_ref = bf16[16,5376]{1,0:T(8,128)(2,1)S(1)} custom-call(s32[8]{0:T(128)S(1)} %copy-done.9, bf16[16,6400]{1,0:T(8,128)(2,1)S(1)} %copy-done.3, bf16[16,5376]{1,0:T(8,128)(2,1)S(1)} %shard_map.108.after_ref.payload_ref, bf16[16,5376]{1,0:T(8,128)(2,1)S(1)} %collective-permute-done.4.received_ref.refs_4_, ...), custom_call_target="tpu_custom_call" | custom-call | flops 1000000 | bytes 400000 | tf_op jit(solution)/shard_map/pallas_call | solution.py:508
  44.3 1.5 %collective-permute-start.5 = (bf16[16,5376]{1,0:T(8,128)(2,1)S(1)}, bf16[16,5376]{1,0:T(8,128)(2,1)S(1)}, u32[]{:S(2)}, u32[]{:S(2)}) collective-permute-start(bf16[16,5376]{1,0:T(8,128)(2,1)S(1)} %shard_map.110.after_ref.payload_ref), channel_id=1, source_target_pairs={{0,32},{1,33},{2,34},{3,35},{4,36},{5,37},{6,38},{7,39},{8,40},{9,... | collective-permute-start | bytes 516104 | tf_op jit(solution)/shard_map/ppermute | solution.py:739
  45.8 3.0 %shard_map.111 = (bf16[8,256,512]{2,1,0:T(8,128)(2,1)S(1)}, f32[8,128]{1,0:T(8,128)S(1)}) custom-call(bf16[128,16,1024]{2,1,0:T(8,128)(2,1)S(1)} %copy-done, bf16[16,5376]{1,0:T(8,128)(2,1)S(1)} %shard_map.110.after_ref.payload_ref), custom_call_target="tpu_custom_call" | custom-call | flops 600000000 | bytes 4200000 | tf_op jit(solution)/shard_map/pallas_call | solution.py:549
  48.7 0.9 %collective-permute-done.5.received_ref.refs_5_ = bf16[16,5376]{1,0:T(8,128)(2,1)S(1)} collective-permute-done((bf16[16,5376]{1,0:T(8,128)(2,1)S(1)}, bf16[16,5376]{1,0:T(8,128)(2,1)S(1)}, u32[]{:S(2)}, u32[]{:S(2)}) %collective-permute-start.5) | collective-permute-done | bytes 172064 | tf_op jit(solution)/shard_map/ppermute | solution.py:739
  49.7 0.6 shard_map.112.after_ref
  50.3 0.1 copy-start.5
  50.4 2.8 %collective-permute-start.6 = (bf16[16,5376]{1,0:T(8,128)(2,1)S(1)}, bf16[16,5376]{1,0:T(8,128)(2,1)S(1)}, u32[]{:S(2)}, u32[]{:S(2)}) collective-permute-start(bf16[16,5376]{1,0:T(8,128)(2,1)S(1)} %shard_map.112.after_ref), channel_id=1, source_target_pairs={{0,96},{1,97},{2,98},{3,99},{4,100},{5,101},{6,102},{7,103},{8,104... | collective-permute-start | bytes 516104 | tf_op jit(solution)/shard_map/ppermute | solution.py:739
  53.2 3.4 %shard_map.113 = (f32[16,2560]{1,0:T(8,128)S(1)}, f32[8,128]{1,0:T(8,128)}) custom-call(f32[3,8192]{1,0:T(4,128)S(1)} %copy-done.8, bf16[16,8192]{1,0:T(8,128)(2,1)S(1)} %copy-done.10, s32[12,128]{1,0:T(8,128)S(1)} %select_bitcast_fusion.rel_ref.refs_10_, bf16[16,5376]{1,0:T(8,128)(2,1)S(1)} %shard_map.112.after_ref), custom_call_target="tpu_custom_call" | custom-call | flops 1000000000 | bytes 1000000 | tf_op jit(solution)/shard_map/pallas_call | solution.py:188
  56.6 0.5 collective-permute-done.6.refs_6_
  57.1 12.2 %shard_map.114 = f32[16,8192]{1,0:T(8,128)} custom-call(s32[8]{0:T(128)S(1)} %copy-done.9, s32[2048]{0:T(1024)S(1)} %mul.30.rest_1_.index_ref, bf16[16,6400]{1,0:T(8,128)(2,1)S(1)} %copy-done.3, bf16[16,6400]{1,0:T(8,128)(2,1)S(1)} %collective-permute-done.received_ref.refs_0_, bf16[16,5376]{1,0:T(8,128)(2,1)S(1)} %collective-permute-done.1.received_ref.refs_1_, ...), custom_call_target="tpu_custom_call" | custom-call | flops 3000000000 | bytes 16000000 | tf_op jit(solution)/shard_map/pallas_call | solution.py:677
  (17 shorter events, 0.1 us)
Async XLA Ops:
  0.0 9.2 %copy-start.13 = (s32[6]{0:T(128)S(1)}, s32[6]{0:T(128)}, u32[]{:S(2)}) copy-start(s32[6]{0:T(128)} %constant.5.clone) | copy-start | bytes 76
  0.0 9.3 %copy-start.6 = (bf16[252,2,1024]{2,1,0:T(2,128)(2,1)S(1)}, bf16[252,2,1024]{2,1,0:T(2,128)(2,1)}, u32[]{:S(2)}) copy-start(bf16[252,2,1024]{2,1,0:T(2,128)(2,1)} %couple_ref.1) | copy-start | bytes 3096580
  0.0 9.3 %copy-start.7 = (bf16[254,1024]{1,0:T(8,128)(2,1)S(1)}, bf16[254,1024]{1,0:T(8,128)(2,1)}, u32[]{:S(2)}) copy-start(bf16[254,1024]{1,0:T(8,128)(2,1)} %transfer_ref.1) | copy-start | bytes 1560580
  0.5 11.2 %copy-start.11 = (s32[128,16]{0,1:T(8,128)S(1)}, s32[128,16]{0,1:T(8,128)}, u32[]{:S(2)}) copy-start(s32[128,16]{0,1:T(8,128)} %param.13) | copy-start | bytes 24580
  0.5 11.2 %copy-start.9 = (s32[8]{0:T(128)S(1)}, s32[8]{0:T(128)}, u32[]{:S(2)}) copy-start(s32[8]{0:T(128)} %compare_select_fusion.bits_ref) | copy-start | bytes 100
  0.5 15.0 %copy-start.8 = (f32[3,8192]{1,0:T(4,128)S(1)}, f32[3,8192]{1,0:T(4,128)}, u32[]{:S(2)}) copy-start(f32[3,8192]{1,0:T(4,128)} %refs_9_.1) | copy-start | bytes 294916
  0.5 15.0 %copy-start.10 = (bf16[16,8192]{1,0:T(8,128)(2,1)S(1)}, bf16[16,8192]{1,0:T(8,128)(2,1)}, u32[]{:S(2)}) copy-start(bf16[16,8192]{1,0:T(8,128)(2,1)} %points_ref.7) | copy-start | bytes 786436
  9.1 6.2 %copy-start.12 = (s32[128,12]{0,1:T(8,128)S(1)}, s32[128,12]{0,1:T(8,128)}, u32[]{:S(2)}) copy-start(s32[128,12]{0,1:T(8,128)} %param.15) | copy-start | bytes 18436
  9.1 2.7 %collective-permute-start = (bf16[16,6400]{1,0:T(8,128)(2,1)}, bf16[16,6400]{1,0:T(8,128)(2,1)S(1)}, u32[]{:S(2)}, u32[]{:S(2)}) collective-permute-start(bf16[16,6400]{1,0:T(8,128)(2,1)} %get-tuple-element.23.after_ref.first_ref.payload_ref), channel_id=1, source_target_pairs={{0,1},{1,0},{2,3},{3,2},{4,5},{5,4},{6,7},{7,6},{8,9},{9,8},{10,11... | collective-permute-start | bytes 614408 | tf_op jit(solution)/shard_map/ppermute | solution.py:739
  9.3 0.9 %copy-start.1 = (bf16[16,6400]{1,0:T(8,128)(2,1)S(1)}, bf16[16,6400]{1,0:T(8,128)(2,1)}, u32[]{:S(2)}) copy-start(bf16[16,6400]{1,0:T(8,128)(2,1)} %get-tuple-element.23.after_ref.first_ref.payload_ref) | copy-start | bytes 614404
  11.8 0.9 %copy-start.2 = (bf16[16,6400]{1,0:T(8,128)(2,1)S(1)}, bf16[16,6400]{1,0:T(8,128)(2,1)}, u32[]{:S(2)}) copy-start(bf16[16,6400]{1,0:T(8,128)(2,1)} %get-tuple-element.23.after_ref.first_ref.payload_ref) | copy-start | bytes 614404
  13.6 6.8 %collective-permute-start.1 = (bf16[16,5376]{1,0:T(8,128)(2,1)S(1)}, bf16[16,5376]{1,0:T(8,128)(2,1)S(1)}, u32[]{:S(2)}, u32[]{:S(2)}) collective-permute-start(bf16[16,5376]{1,0:T(8,128)(2,1)S(1)} %shard_map.102.after_ref.payload_ref), channel_id=1, source_target_pairs={{0,2},{1,3},{2,0},{3,1},{4,6},{5,7},{6,4},{7,5},{8,10},{9,11},{10,... | collective-permute-start | bytes 516104 | tf_op jit(solution)/shard_map/ppermute | solution.py:739
  15.5 4.9 %copy-start.3 = (bf16[16,6400]{1,0:T(8,128)(2,1)S(1)}, bf16[16,6400]{1,0:T(8,128)(2,1)}, u32[]{:S(2)}) copy-start(bf16[16,6400]{1,0:T(8,128)(2,1)} %get-tuple-element.23.after_ref.first_ref.payload_ref) | copy-start | bytes 614404
  21.2 7.4 %collective-permute-start.2 = (bf16[16,5376]{1,0:T(8,128)(2,1)S(1)}, bf16[16,5376]{1,0:T(8,128)(2,1)S(1)}, u32[]{:S(2)}, u32[]{:S(2)}) collective-permute-start(bf16[16,5376]{1,0:T(8,128)(2,1)S(1)} %shard_map.104.after_ref.payload_ref), channel_id=1, source_target_pairs={{0,6},{1,7},{2,4},{3,5},{4,2},{5,3},{6,0},{7,1},{8,14},{9,15},{10,... | collective-permute-start | bytes 516104 | tf_op jit(solution)/shard_map/ppermute | solution.py:739
  29.5 5.4 %collective-permute-start.3 = (bf16[16,5376]{1,0:T(8,128)(2,1)S(1)}, bf16[16,5376]{1,0:T(8,128)(2,1)S(1)}, u32[]{:S(2)}, u32[]{:S(2)}) collective-permute-start(bf16[16,5376]{1,0:T(8,128)(2,1)S(1)} %shard_map.106.after_ref.payload_ref), channel_id=1, source_target_pairs={{0,8},{1,9},{2,10},{3,11},{4,12},{5,13},{6,14},{7,15},{8,0},{9,1},... | collective-permute-start | bytes 516104 | tf_op jit(solution)/shard_map/ppermute | solution.py:739
  31.4 8.6 %copy-start = (bf16[128,16,1024]{2,1,0:T(8,128)(2,1)S(1)}, bf16[128,16,1024]{2,1,0:T(8,128)(2,1)}, u32[]{:S(2)}) copy-start(bf16[128,16,1024]{2,1,0:T(8,128)(2,1)} %c_ref.3) | copy-start | bytes 12582916
  35.8 7.6 %collective-permute-start.4 = (bf16[16,5376]{1,0:T(8,128)(2,1)S(1)}, bf16[16,5376]{1,0:T(8,128)(2,1)S(1)}, u32[]{:S(2)}, u32[]{:S(2)}) collective-permute-start(bf16[16,5376]{1,0:T(8,128)(2,1)S(1)} %shard_map.108.after_ref.payload_ref), channel_id=1, source_target_pairs={{0,24},{1,25},{2,26},{3,27},{4,28},{5,29},{6,30},{7,31},{8,16},{9,... | collective-permute-start | bytes 516104 | tf_op jit(solution)/shard_map/ppermute | solution.py:739
  44.3 5.4 %collective-permute-start.5 = (bf16[16,5376]{1,0:T(8,128)(2,1)S(1)}, bf16[16,5376]{1,0:T(8,128)(2,1)S(1)}, u32[]{:S(2)}, u32[]{:S(2)}) collective-permute-start(bf16[16,5376]{1,0:T(8,128)(2,1)S(1)} %shard_map.110.after_ref.payload_ref), channel_id=1, source_target_pairs={{0,32},{1,33},{2,34},{3,35},{4,36},{5,37},{6,38},{7,39},{8,40},{9,... | collective-permute-start | bytes 516104 | tf_op jit(solution)/shard_map/ppermute | solution.py:739
  50.3 6.8 %copy-start.4 = (bf16[17,256,256]{2,1,0:T(8,128)(2,1)S(1)}, bf16[17,256,256]{2,1,0:T(8,128)(2,1)}, u32[]{:S(2)}) copy-start(bf16[17,256,256]{2,1,0:T(8,128)(2,1)} %get-tuple-element.32.refs_11_) | copy-start | bytes 6684676
  50.3 6.8 %copy-start.5 = (bf16[16,256,256]{2,1,0:T(8,128)(2,1)S(1)}, bf16[16,256,256]{2,1,0:T(8,128)(2,1)}, u32[]{:S(2)}) copy-start(bf16[16,256,256]{2,1,0:T(8,128)(2,1)} %get-tuple-element.35.refs_14_) | copy-start | bytes 6291460
  50.4 6.7 %collective-permute-start.6 = (bf16[16,5376]{1,0:T(8,128)(2,1)S(1)}, bf16[16,5376]{1,0:T(8,128)(2,1)S(1)}, u32[]{:S(2)}, u32[]{:S(2)}) collective-permute-start(bf16[16,5376]{1,0:T(8,128)(2,1)S(1)} %shard_map.112.after_ref), channel_id=1, source_target_pairs={{0,96},{1,97},{2,98},{3,99},{4,100},{5,101},{6,102},{7,103},{8,104... | collective-permute-start | bytes 516104 | tf_op jit(solution)/shard_map/ppermute | solution.py:739

commit v6 on v5

--- a/solution.py
+++ b/solution.py
@@ -294,7 +294,7 @@
     )
 
 
-def up_step(step, lanes, rows, basis_ref, local_ref, payload_ref, ub_ref, bd_ref, rep_ref, x_ref, c_ref):
+def up_step(step, lanes, rows, basis_ref, local_ref, ub_ref, bd_ref, rep_ref):
     basis = basis_ref[16 * step : 16 * step + 16, :]
     wide = dot(jnp.concatenate([basis[:, 128 * k : 128 * k + 128] for k in range(16)], axis=0), rep_ref[...])
     keep = lanes == rows
@@ -307,7 +307,6 @@
             ub_ref[2 * step + e, 8 * p : 8 * p + 16, :] = jnp.concatenate(both, axis=0).astype(bf16)
     local = local_ref[16 * step : 16 * step + 16, :]
     wide = dot(jnp.concatenate([local[:, 128 * k : 128 * k + 128] for k in range(8)], axis=0), rep_ref[...])
-    total = jnp.zeros((16, 256), f32)
     for e in range(2):
         keep = lanes == rows // 2 + 4 * e
         for a in range(0, RANK, 2):
@@ -316,14 +315,9 @@
                 k, low = q // 4, q % 4
                 both.append(jnp.where(keep, wide[16 * k + 8 * e : 16 * k + 8 * e + 8, 256 * low : 256 * low + 256], 0.0))
             bd_ref[2 * step + e, 8 * a : 8 * a + 16, :] = jnp.concatenate(both, axis=0).astype(bf16)
-        own = x_ref[32 * step + 16 * e : 32 * step + 16 * e + 16, :]
-        coeff = dot(own, ub_ref[2 * step + e]).astype(bf16)
-        payload_ref[:, 512 * step + 256 * e : 512 * step + 256 * e + 256] = coeff
-        total = total + dot(coeff, bd_ref[2 * step + e])
-    c_ref[16 * step : 16 * step + 16, :] = total
-
-
-def up_kernel(bits_ref, points_in, coords_in, basis_in, local_in, payload_ref, ub_out, bd_out, bdup_out, rep_ref, x_ref, c_ref, y_ref, points_ref, coords_ref, basis_ref, local_ref, ub_ref, bd_ref, bdup_ref, in_sem, out_sem):
+
+
+def up_kernel(bits_ref, points_in, coords_in, basis_in, local_in, payload_ref, ub_out, bd_out, bdup_out, rep_ref, x_ref, y_ref, points_ref, coords_ref, basis_ref, local_ref, ub_ref, bd_ref, bdup_ref, in_sem, out_sem):
     arrivals = [
         pltpu.make_async_copy(source, target, in_sem.at[k])
         for k, (source, target) in enumerate(
@@ -343,10 +337,14 @@
     x_ref[...] = dot(stacked, perm).astype(bf16)
     departures = []
     for step in range(GROUPS // 2):
-        up_step(step, lanes, rows, basis_ref, local_ref, payload_ref, ub_ref, bd_ref, rep_ref, x_ref, c_ref)
+        up_step(step, lanes, rows, basis_ref, local_ref, ub_ref, bd_ref, rep_ref)
         part = pl.ds(2 * step, 2)
         departures.append(pltpu.make_async_copy(ub_ref.at[part], ub_out.at[part], out_sem.at[step]))
         departures[-1].start()
+    coeffs = []
+    for g in range(GROUPS):
+        coeffs.append(dot(x_ref[16 * g : 16 * g + 16, :], ub_ref[g]).astype(bf16))
+        payload_ref[:, 256 * g : 256 * g + 256] = coeffs[g]
     departures.append(pltpu.make_async_copy(bd_ref, bd_out, out_sem.at[8]))
     departures[-1].start()
     for k in range(8):
@@ -360,7 +358,7 @@
     fill_upper(y_ref, bdup_ref, 16, 15, (lanes == 0) & (rows >= 4) & (rows < 6))
     departures.append(pltpu.make_async_copy(bdup_ref, bdup_out, out_sem.at[9]))
     departures[-1].start()
-    current = [c_ref[16 * q : 16 * q + 16, :] for q in range(8)]
+    current = [dot(coeffs[2 * q], bd_ref[2 * q]) + dot(coeffs[2 * q + 1], bd_ref[2 * q + 1]) for q in range(8)]
     tile = 0
     for level_tiles in (8, 4, 2, 1, 1, 1):
         parts = [joined(dot(halves(current[q]), bdup_ref[tile + q])) for q in range(level_tiles)]
@@ -467,7 +465,6 @@
         scratch_shapes=[
             pltpu.VMEM((128, 1024), bf16),
             pltpu.VMEM((256, 512), bf16),
-            pltpu.VMEM((128, 256), f32),
             pltpu.VMEM((8, 128, 1024), f32),
             pltpu.VMEM((16, LEAF_DEV * LEAF), bf16),
             pltpu.VMEM((3, LEAF_DEV * LEAF), f32),
@@ -566,6 +563,36 @@
     )(far_coupling, after)
 
 
+def field_chain(bits_ref, received, em_ref, sm_ref, bdup_ref, field_ref):
+    terms = []
+    for height in range(1, 7):
+        _, before_mine, before_sibling = unpack_state(received[height][:, TABLE:EDGE])
+        plain = (bits_ref[height - 1] == 0) == (height % 2 == 1)
+        left = jnp.where(plain, before_mine, before_sibling)
+        right = jnp.where(plain, before_sibling, before_mine)
+        both = left + pltpu.roll(right, 32, 1)
+        yield
+        terms.append(joined(dot_nt(halves(both), sm_ref[32 * height - 32 : 32 * height, :])))
+    field = terms[5]
+    for height in range(5, 0, -1):
+        row = pl.multiple_of(64 * (height - 1) + 32 * bits_ref[height - 1], 32)
+        matrix = em_ref[pl.ds(row, 32), 0:RANK]
+        yield
+        field = terms[height - 1] + joined(dot_nt(halves(field), matrix))
+    stretch = where_eq(iota((RANK, 256), 0) * 8, iota((RANK, 256), 1))
+    fields = [joined(dot(halves(field), stretch))]
+    tile = UPPER
+    for level_tiles in (1, 1, 1, 2, 4, 8):
+        yield
+        tile -= level_tiles
+        fields = [
+            joined(dot_nt(halves(fields[q // 2 if level_tiles > 1 else 0]), bdup_ref[tile + q]))
+            for q in range(level_tiles)
+        ]
+    for q in range(8):
+        field_ref[32 * q : 32 * q + 32, :] = halves(fields[q])
+
+
 def down_kernel(bits_ref, index_ref, payload_ref, *refs):
     received = refs[:7]
     em_ref, sm_ref, coords_ref, rel_ref, bdup_in, d0_ref, d1_ref, bd_in, ub_in, near0_ref, near1_ref, near2_ref, near3_ref, out_ref, table_ref, field_ref, far_ref, gather_ref, edge_ref, d_ref, bdup_ref, bd_ref, ub_ref, sem = refs[7:]
@@ -593,29 +620,6 @@
         for m in range(8):
             table_ref[2048 * k + 256 * m : 2048 * k + 256 * m + 256, :] = wide[:, 128 * m : 128 * m + 128]
     table_ref[16384:16400, :] = jnp.zeros((16, 128), bf16)
-    terms = []
-    for height in range(1, 7):
-        _, before_mine, before_sibling = unpack_state(received[height][:, TABLE:EDGE])
-        plain = (bits_ref[height - 1] == 0) == (height % 2 == 1)
-        left = jnp.where(plain, before_mine, before_sibling)
-        right = jnp.where(plain, before_sibling, before_mine)
-        both = left + pltpu.roll(right, 32, 1)
-        terms.append(joined(dot_nt(halves(both), sm_ref[32 * height - 32 : 32 * height, :])))
-    field = terms[5]
-    for height in range(5, 0, -1):
-        row = pl.multiple_of(64 * (height - 1) + 32 * bits_ref[height - 1], 32)
-        matrix = em_ref[pl.ds(row, 32), 0:RANK]
-        field = terms[height - 1] + joined(dot_nt(halves(field), matrix))
-    stretch = where_eq(iota((RANK, 256), 0) * 8, iota((RANK, 256), 1))
-    fields = [joined(dot(halves(field), stretch))]
-    copies[0].wait()
-    tile = UPPER
-    for level_tiles in (1, 1, 1, 2, 4, 8):
-        tile -= level_tiles
-        fields = [
-            joined(dot_nt(halves(fields[q // 2 if level_tiles > 1 else 0]), bdup_ref[tile + q]))
-            for q in range(level_tiles)
-        ]
     near_side = received[0][:, EDGE:WIDTH]
     far_side = received[1][:, EDGE:WIDTH]
     for height in range(2, 7):
@@ -628,12 +632,12 @@
         edge_ref[own % 4] = acc
 
     edge_products(left_halo, right_halo, coords_ref, rel_ref, add)
-    for q in range(8):
-        field_ref[32 * q : 32 * q + 32, :] = halves(fields[q])
-    for copy in copies[1:]:
+    for copy in copies:
         copy.wait()
     block = iota((16, 128), 1) // RANK
     which = iota((16, 256), 1) % 8
+    chain = field_chain(bits_ref, received, em_ref, sm_ref, bdup_ref, field_ref)
+    fars = []
     for step in range(GROUPS):
         for leaf in range(8):
             for s_high in range(4):
@@ -642,14 +646,21 @@
                     entry = index_ref[(8 * step + leaf) * NF + 4 * s_high + low]
                     value = table_ref[pl.ds(pl.multiple_of(entry, 16), 16), :]
                     merged = value if low == 0 else jnp.where(block == low, value, merged)
-                gather_ref[step % 2, 16 * leaf : 16 * leaf + 16, 128 * s_high : 128 * s_high + 128] = merged
-        result = dot_nt(gather_ref[step % 2], d_ref[step])
+                gather_ref[step, 16 * leaf : 16 * leaf + 16, 128 * s_high : 128 * s_high + 128] = merged
+        result = dot_nt(gather_ref[step], d_ref[step])
+        next(chain, None)
         far = result[0:16]
         for leaf in range(1, 8):
             far = jnp.where(which == leaf, result[16 * leaf : 16 * leaf + 16], far)
+        fars.append(far)
+    for _ in chain:
+        pass
+    leaf_fields = []
+    for step in range(GROUPS):
         parent = field_ref[32 * (step // 2) : 32 * (step // 2) + 32, :]
-        leaf_field = (far + joined(dot_nt(parent, bd_ref[step]))).astype(bf16)
-        part = dot_nt(leaf_field, ub_ref[step])
+        leaf_fields.append((fars[step] + joined(dot_nt(parent, bd_ref[step]))).astype(bf16))
+    for step in range(GROUPS):
+        part = dot_nt(leaf_fields[step], ub_ref[step])
         high = part.astype(bf16)
         far_ref[16 * step : 16 * step + 16, :] = high
         far_ref[256 + 16 * step : 272 + 16 * step, :] = (part - high.astype(f32)).astype(bf16)
@@ -683,7 +694,7 @@
             pltpu.VMEM((16400, 128), bf16),
             pltpu.VMEM((256, 256), bf16),
             pltpu.VMEM((512, 512), bf16),
-            pltpu.VMEM((2, 128, 512), bf16),
+            pltpu.VMEM((GROUPS, 128, 512), bf16),
             pltpu.VMEM((4, 16, BLK), f32),
             pltpu.VMEM((GROUPS, 256, 512), bf16),
             pltpu.VMEM((UPPER, 256, 256), bf16),

time: 69.7 us -> 66.4 us (0.953)
  Pallas kernels: 46.8 us -> 43.6 us
    pallas_call x1, Pallas kernels: 12.2 us -> 10.2 us  [downward(): pl.pallas_call(down_kernel, out_shape=jax.ShapeDtypeStruct((16, LEAF_DEV...]
    pallas_call x1, Pallas kernels: 8.55 us -> 7.42 us  [upward(): pl.pallas_call(up_kernel, out_shape=(jax.ShapeDtypeStruct((16, FIRST), bf...]
  transfers between devices with their start and end apart: 7 -> 7, of which waited for: 6 -> 5; matrix products, arithmetic and copies ran while one was open for 0% -> 0% of each run, Pallas kernels for 30% -> 32%
where the time goes in v6:
time: 66.4 us; the launch traced here: 66.3 us
  Pallas kernels  43.6 us (66%)
  starting transfers between devices  15.4 us (23%)
  waiting for transfers between devices  4.1 us (6%)
  local copies, waits for them, and re-layouts  2.14 us (3%)
    ppermute x7, starting transfers between devices, per_device(): received.append(lax.ppermute(payload, 'leaf', route))  15.4 us
    pallas_call x4, Pallas kernels, near_chunk(): pl.pallas_call(functools.partial(near_kernel, chunk, blocks), out_shape=(...  13.6 us
    pallas_call x1, Pallas kernels, downward(): pl.pallas_call(down_kernel, out_shape=jax.ShapeDtypeStruct((16, LEAF_DEV...  10.2 us
    pallas_call x1, Pallas kernels, upward(): pl.pallas_call(up_kernel, out_shape=(jax.ShapeDtypeStruct((16, FIRST), bf...  7.42 us
    pallas_call x2, Pallas kernels, regroup(): pl.pallas_call(regroup_kernel, grid=(groups,), out_shape=(jax.ShapeDtypeS...  5.94 us
    pallas_call x6, Pallas kernels, tree_step(): pl.pallas_call(functools.partial(step_kernel, height), out_shape=jax.Shap...  5 us
    ppermute x7, waiting for transfers between devices, per_device(): received.append(lax.ppermute(payload, 'leaf', route))  4.1 us
    unnamed x28, local copies, waits for them, and re-layouts  1.95 us
  transfers between devices with their start and end apart: 7, of which 5 were waited for; matrix products, arithmetic and copies ran while one was open for 0% of the time, Pallas kernels for 32%

profile of v6, /device:TPU:0, one launch (start us, length us, event | category | flops | bytes accessed | tf_op | source)
XLA Modules:
  0.0 66.3 jit_solution(5483269047367357072)
XLA Ops:
  0.0 0.5 compare_select_fusion.bits_ref
  0.5 7.4 %shard_map.100 = (bf16[16,6400]{1,0:T(8,128)(2,1)}, bf16[16,512,256]{2,1,0:T(8,128)(2,1)}, bf16[16,256,256]{2,1,0:T(8,128)(2,1)}, bf16[17,256,256]{2,1,0:T(8,128)(2,1)}) custom-call(s32[8]{0:T(128)} %compare_select_fusion.bits_ref, bf16[16,8192]{1,0:T(8,128)(2,1)} %points_ref.7, f32[3,8192]{1,0:T(4,128)} %refs_9_.1, bf16[128,2048]{1,0:T(8,128)(2,1)} %basis_in.1, ...), custom_call_target="tpu_custom_call" | custom-call | flops 1000000000 | bytes 10000000 | tf_op jit(solution)/shard_map/pallas_call | solution.py:455
  8.0 0.0 copy-start.12
  8.0 0.1 collective-permute-start
  8.1 0.0 copy-done.13
  8.1 0.1 pad_add_fusion.nodes_ref
  8.2 0.0 copy-done.6
  8.2 0.0 copy-done.7
  8.2 0.9 %copy-done.1 = bf16[16,6400]{1,0:T(8,128)(2,1)S(1)} copy-done((bf16[16,6400]{1,0:T(8,128)(2,1)S(1)}, bf16[16,6400]{1,0:T(8,128)(2,1)}, u32[]{:S(2)}) %copy-start.1) | copy-done | bytes 204824
  9.1 1.5 %shard_map.101 = (bf16[320,128]{1,0:T(8,128)(2,1)S(1)}, bf16[192,128]{1,0:T(8,128)(2,1)S(1)}, f32[8,128]{1,0:T(8,128)S(1)}) custom-call(s32[16]{0:T(128)S(1)} %pad_add_fusion.nodes_ref, bf16[254,1024]{1,0:T(8,128)(2,1)S(1)} %copy-done.7, bf16[252,2,1024]{2,1,0:T(2,128)(2,1)S(1)} %copy-done.6, bf16[16,6400]{1,0:T(8,128)(2,1)S(1)} %copy-done.1), custom_call_target="tpu_custom_call" | custom-call | flops 100000000 | bytes 800000 | tf_op jit(solution)/shard_map/pallas_call | solution.py:428
  10.6 0.0 copy-done.11
  10.6 0.0 collective-permute-done.received_ref.refs_0_
  10.6 0.0 copy-done.9
  10.6 0.0 copy-start.2
  10.7 0.9 %copy-done.2 = bf16[16,6400]{1,0:T(8,128)(2,1)S(1)} copy-done((bf16[16,6400]{1,0:T(8,128)(2,1)S(1)}, bf16[16,6400]{1,0:T(8,128)(2,1)}, u32[]{:S(2)}) %copy-start.2) | copy-done | bytes 204824
  11.6 0.9 %shard_map.102.after_ref.payload_ref = bf16[16,5376]{1,0:T(8,128)(2,1)S(1)} custom-call(s32[8]{0:T(128)S(1)} %copy-done.9, bf16[16,6400]{1,0:T(8,128)(2,1)S(1)} %copy-done.2, bf16[16,6400]{1,0:T(8,128)(2,1)S(1)} %copy-done.2, bf16[16,6400]{1,0:T(8,128)(2,1)S(1)} %collective-permute-done.received_ref.refs_0_, ...), custom_call_target="tpu_custom_call" | custom-call | flops 1000000 | bytes 400000 | tf_op jit(solution)/shard_map/pallas_call | solution.py:505
  12.5 1.7 %collective-permute-start.1 = (bf16[16,5376]{1,0:T(8,128)(2,1)S(1)}, bf16[16,5376]{1,0:T(8,128)(2,1)S(1)}, u32[]{:S(2)}, u32[]{:S(2)}) collective-permute-start(bf16[16,5376]{1,0:T(8,128)(2,1)S(1)} %shard_map.102.after_ref.payload_ref), channel_id=1, source_target_pairs={{0,2},{1,3},{2,0},{3,1},{4,6},{5,7},{6,4},{7,5},{8,10},{9,11},{10,... | collective-permute-start | bytes 516104 | tf_op jit(solution)/shard_map/ppermute | solution.py:750
  14.2 0.0 copy-done.12
  14.2 0.1 copy.11
  14.3 0.1 mul.30.rest_1_.index_ref
  14.3 0.0 copy-done.8
  14.3 0.0 copy-done.10
  14.4 0.0 copy-start.3
  14.4 3.4 %shard_map.103 = (f32[16,2560]{1,0:T(8,128)S(1)}, f32[8,128]{1,0:T(8,128)S(1)}) custom-call(f32[3,8192]{1,0:T(4,128)S(1)} %copy-done.8, bf16[16,8192]{1,0:T(8,128)(2,1)S(1)} %copy-done.10, s32[12,128]{1,0:T(8,128)S(1)} %select_bitcast_fusion.rel_ref.refs_10_, bf16[16,5376]{1,0:T(8,128)(2,1)S(1)} %shard_map.102.after_ref.payload_ref), custom_call_target="tpu_custom_call" | custom-call | flops 1000000000 | bytes 1000000 | tf_op jit(solution)/shard_map/pallas_call | solution.py:188
  17.8 1.4 %collective-permute-done.1.received_ref.refs_1_ = bf16[16,5376]{1,0:T(8,128)(2,1)S(1)} collective-permute-done((bf16[16,5376]{1,0:T(8,128)(2,1)S(1)}, bf16[16,5376]{1,0:T(8,128)(2,1)S(1)}, u32[]{:S(2)}, u32[]{:S(2)}) %collective-permute-start.1) | collective-permute-done | bytes 172064 | tf_op jit(solution)/shard_map/ppermute | solution.py:750
  19.2 0.0 copy-done.3
  19.2 0.9 %shard_map.104.after_ref.payload_ref = bf16[16,5376]{1,0:T(8,128)(2,1)S(1)} custom-call(s32[8]{0:T(128)S(1)} %copy-done.9, bf16[16,6400]{1,0:T(8,128)(2,1)S(1)} %copy-done.3, bf16[16,5376]{1,0:T(8,128)(2,1)S(1)} %shard_map.102.after_ref.payload_ref, bf16[16,5376]{1,0:T(8,128)(2,1)S(1)} %collective-permute-done.1.received_ref.refs_1_, ...), custom_call_target="tpu_custom_call" | custom-call | flops 1000000 | bytes 400000 | tf_op jit(solution)/shard_map/pallas_call | solution.py:505
  20.1 3.1 %collective-permute-start.2 = (bf16[16,5376]{1,0:T(8,128)(2,1)S(1)}, bf16[16,5376]{1,0:T(8,128)(2,1)S(1)}, u32[]{:S(2)}, u32[]{:S(2)}) collective-permute-start(bf16[16,5376]{1,0:T(8,128)(2,1)S(1)} %shard_map.104.after_ref.payload_ref), channel_id=1, source_target_pairs={{0,6},{1,7},{2,4},{3,5},{4,2},{5,3},{6,0},{7,1},{8,14},{9,15},{10,... | collective-permute-start | bytes 516104 | tf_op jit(solution)/shard_map/ppermute | solution.py:750
  23.2 3.4 %shard_map.105 = (f32[16,2560]{1,0:T(8,128)S(1)}, f32[8,128]{1,0:T(8,128)S(1)}) custom-call(f32[3,8192]{1,0:T(4,128)S(1)} %copy-done.8, bf16[16,8192]{1,0:T(8,128)(2,1)S(1)} %copy-done.10, s32[12,128]{1,0:T(8,128)S(1)} %select_bitcast_fusion.rel_ref.refs_10_, bf16[16,5376]{1,0:T(8,128)(2,1)S(1)} %shard_map.104.after_ref.payload_ref), custom_call_target="tpu_custom_call" | custom-call | flops 1000000000 | bytes 1000000 | tf_op jit(solution)/shard_map/pallas_call | solution.py:188
  26.7 0.8 %collective-permute-done.2.received_ref.refs_2_ = bf16[16,5376]{1,0:T(8,128)(2,1)S(1)} collective-permute-done((bf16[16,5376]{1,0:T(8,128)(2,1)S(1)}, bf16[16,5376]{1,0:T(8,128)(2,1)S(1)}, u32[]{:S(2)}, u32[]{:S(2)}) %collective-permute-start.2) | collective-permute-done | bytes 172064 | tf_op jit(solution)/shard_map/ppermute | solution.py:750
  27.5 0.9 %shard_map.106.after_ref.payload_ref = bf16[16,5376]{1,0:T(8,128)(2,1)S(1)} custom-call(s32[8]{0:T(128)S(1)} %copy-done.9, bf16[16,6400]{1,0:T(8,128)(2,1)S(1)} %copy-done.3, bf16[16,5376]{1,0:T(8,128)(2,1)S(1)} %shard_map.104.after_ref.payload_ref, bf16[16,5376]{1,0:T(8,128)(2,1)S(1)} %collective-permute-done.2.received_ref.refs_2_, ...), custom_call_target="tpu_custom_call" | custom-call | flops 1000000 | bytes 400000 | tf_op jit(solution)/shard_map/pallas_call | solution.py:505
  28.3 1.9 %collective-permute-start.3 = (bf16[16,5376]{1,0:T(8,128)(2,1)S(1)}, bf16[16,5376]{1,0:T(8,128)(2,1)S(1)}, u32[]{:S(2)}, u32[]{:S(2)}) collective-permute-start(bf16[16,5376]{1,0:T(8,128)(2,1)S(1)} %shard_map.106.after_ref.payload_ref), channel_id=1, source_target_pairs={{0,8},{1,9},{2,10},{3,11},{4,12},{5,13},{6,14},{7,15},{8,0},{9,1},... | collective-permute-start | bytes 516104 | tf_op jit(solution)/shard_map/ppermute | solution.py:750
  30.3 3.4 %shard_map.107 = (f32[16,2560]{1,0:T(8,128)S(1)}, f32[8,128]{1,0:T(8,128)S(1)}) custom-call(f32[3,8192]{1,0:T(4,128)S(1)} %copy-done.8, bf16[16,8192]{1,0:T(8,128)(2,1)S(1)} %copy-done.10, s32[12,128]{1,0:T(8,128)S(1)} %select_bitcast_fusion.rel_ref.refs_10_, bf16[16,5376]{1,0:T(8,128)(2,1)S(1)} %shard_map.106.after_ref.payload_ref), custom_call_target="tpu_custom_call" | custom-call | flops 1000000000 | bytes 1000000 | tf_op jit(solution)/shard_map/pallas_call | solution.py:188
  33.7 0.0 collective-permute-done.3.received_ref.refs_3_
  33.8 0.9 %shard_map.108.after_ref.payload_ref = bf16[16,5376]{1,0:T(8,128)(2,1)S(1)} custom-call(s32[8]{0:T(128)S(1)} %copy-done.9, bf16[16,6400]{1,0:T(8,128)(2,1)S(1)} %copy-done.3, bf16[16,5376]{1,0:T(8,128)(2,1)S(1)} %shard_map.106.after_ref.payload_ref, bf16[16,5376]{1,0:T(8,128)(2,1)S(1)} %collective-permute-done.3.received_ref.refs_3_, ...), custom_call_target="tpu_custom_call" | custom-call | flops 1000000 | bytes 400000 | tf_op jit(solution)/shard_map/pallas_call | solution.py:505
  34.6 4.2 %collective-permute-start.4 = (bf16[16,5376]{1,0:T(8,128)(2,1)S(1)}, bf16[16,5376]{1,0:T(8,128)(2,1)S(1)}, u32[]{:S(2)}, u32[]{:S(2)}) collective-permute-start(bf16[16,5376]{1,0:T(8,128)(2,1)S(1)} %shard_map.108.after_ref.payload_ref), channel_id=1, source_target_pairs={{0,24},{1,25},{2,26},{3,27},{4,28},{5,29},{6,30},{7,31},{8,16},{9,... | collective-permute-start | bytes 516104 | tf_op jit(solution)/shard_map/ppermute | solution.py:750
  38.9 3.0 %shard_map.109 = (bf16[8,256,512]{2,1,0:T(8,128)(2,1)S(1)}, f32[8,128]{1,0:T(8,128)S(1)}) custom-call(bf16[128,16,1024]{2,1,0:T(8,128)(2,1)S(1)} %copy-done, bf16[16,5376]{1,0:T(8,128)(2,1)S(1)} %shard_map.108.after_ref.payload_ref), custom_call_target="tpu_custom_call" | custom-call | flops 600000000 | bytes 4200000 | tf_op jit(solution)/shard_map/pallas_call | solution.py:546
  41.8 0.4 collective-permute-done.4.received_ref.refs_4_
  42.2 0.9 %shard_map.110.after_ref.payload_ref = bf16[16,5376]{1,0:T(8,128)(2,1)S(1)} custom-call(s32[8]{0:T(128)S(1)} %copy-done.9, bf16[16,6400]{1,0:T(8,128)(2,1)S(1)} %copy-done.3, bf16[16,5376]{1,0:T(8,128)(2,1)S(1)} %shard_map.108.after_ref.payload_ref, bf16[16,5376]{1,0:T(8,128)(2,1)S(1)} %collective-permute-done.4.received_ref.refs_4_, ...), custom_call_target="tpu_custom_call" | custom-call | flops 1000000 | bytes 400000 | tf_op jit(solution)/shard_map/pallas_call | solution.py:505
  43.1 1.5 %collective-permute-start.5 = (bf16[16,5376]{1,0:T(8,128)(2,1)S(1)}, bf16[16,5376]{1,0:T(8,128)(2,1)S(1)}, u32[]{:S(2)}, u32[]{:S(2)}) collective-permute-start(bf16[16,5376]{1,0:T(8,128)(2,1)S(1)} %shard_map.110.after_ref.payload_ref), channel_id=1, source_target_pairs={{0,32},{1,33},{2,34},{3,35},{4,36},{5,37},{6,38},{7,39},{8,40},{9,... | collective-permute-start | bytes 516104 | tf_op jit(solution)/shard_map/ppermute | solution.py:750
  44.6 3.0 %shard_map.111 = (bf16[8,256,512]{2,1,0:T(8,128)(2,1)S(1)}, f32[8,128]{1,0:T(8,128)S(1)}) custom-call(bf16[128,16,1024]{2,1,0:T(8,128)(2,1)S(1)} %copy-done, bf16[16,5376]{1,0:T(8,128)(2,1)S(1)} %shard_map.110.after_ref.payload_ref), custom_call_target="tpu_custom_call" | custom-call | flops 600000000 | bytes 4200000 | tf_op jit(solution)/shard_map/pallas_call | solution.py:546
  47.6 0.9 %collective-permute-done.5.received_ref.refs_5_ = bf16[16,5376]{1,0:T(8,128)(2,1)S(1)} collective-permute-done((bf16[16,5376]{1,0:T(8,128)(2,1)S(1)}, bf16[16,5376]{1,0:T(8,128)(2,1)S(1)}, u32[]{:S(2)}, u32[]{:S(2)}) %collective-permute-start.5) | collective-permute-done | bytes 172064 | tf_op jit(solution)/shard_map/ppermute | solution.py:750
  48.5 0.6 shard_map.112.after_ref
  49.2 0.1 copy-start.5
  49.2 2.8 %collective-permute-start.6 = (bf16[16,5376]{1,0:T(8,128)(2,1)S(1)}, bf16[16,5376]{1,0:T(8,128)(2,1)S(1)}, u32[]{:S(2)}, u32[]{:S(2)}) collective-permute-start(bf16[16,5376]{1,0:T(8,128)(2,1)S(1)} %shard_map.112.after_ref), channel_id=1, source_target_pairs={{0,96},{1,97},{2,98},{3,99},{4,100},{5,101},{6,102},{7,103},{8,104... | collective-permute-start | bytes 516104 | tf_op jit(solution)/shard_map/ppermute | solution.py:750
  52.1 3.4 %shard_map.113 = (f32[16,2560]{1,0:T(8,128)S(1)}, f32[8,128]{1,0:T(8,128)}) custom-call(f32[3,8192]{1,0:T(4,128)S(1)} %copy-done.8, bf16[16,8192]{1,0:T(8,128)(2,1)S(1)} %copy-done.10, s32[12,128]{1,0:T(8,128)S(1)} %select_bitcast_fusion.rel_ref.refs_10_, bf16[16,5376]{1,0:T(8,128)(2,1)S(1)} %shard_map.112.after_ref), custom_call_target="tpu_custom_call" | custom-call | flops 1000000000 | bytes 1000000 | tf_op jit(solution)/shard_map/pallas_call | solution.py:188
  55.5 0.5 collective-permute-done.6.refs_6_
  55.9 10.2 %shard_map.114 = f32[16,8192]{1,0:T(8,128)} custom-call(s32[8]{0:T(128)S(1)} %copy-done.9, s32[2048]{0:T(1024)S(1)} %mul.30.rest_1_.index_ref, bf16[16,6400]{1,0:T(8,128)(2,1)S(1)} %copy-done.3, bf16[16,6400]{1,0:T(8,128)(2,1)S(1)} %collective-permute-done.received_ref.refs_0_, bf16[16,5376]{1,0:T(8,128)(2,1)S(1)} %collective-permute-done.1.received_ref.refs_1_, ...), custom_call_target="tpu_custom_call" | custom-call | flops 3000000000 | bytes 16000000 | tf_op jit(solution)/shard_map/pallas_call | solution.py:688
  (17 shorter events, 0.1 us)
Async XLA Ops:
  0.0 8.1 %copy-start.13 = (s32[6]{0:T(128)S(1)}, s32[6]{0:T(128)}, u32[]{:S(2)}) copy-start(s32[6]{0:T(128)} %constant.5.clone) | copy-start | bytes 76
  0.0 8.2 %copy-start.6 = (bf16[252,2,1024]{2,1,0:T(2,128)(2,1)S(1)}, bf16[252,2,1024]{2,1,0:T(2,128)(2,1)}, u32[]{:S(2)}) copy-start(bf16[252,2,1024]{2,1,0:T(2,128)(2,1)} %couple_ref.1) | copy-start | bytes 3096580
  0.0 8.2 %copy-start.7 = (bf16[254,1024]{1,0:T(8,128)(2,1)S(1)}, bf16[254,1024]{1,0:T(8,128)(2,1)}, u32[]{:S(2)}) copy-start(bf16[254,1024]{1,0:T(8,128)(2,1)} %transfer_ref.1) | copy-start | bytes 1560580
  0.5 10.1 %copy-start.11 = (s32[128,16]{0,1:T(8,128)S(1)}, s32[128,16]{0,1:T(8,128)}, u32[]{:S(2)}) copy-start(s32[128,16]{0,1:T(8,128)} %param.13) | copy-start | bytes 24580
  0.5 10.1 %copy-start.9 = (s32[8]{0:T(128)S(1)}, s32[8]{0:T(128)}, u32[]{:S(2)}) copy-start(s32[8]{0:T(128)} %compare_select_fusion.bits_ref) | copy-start | bytes 100
  0.5 13.8 %copy-start.8 = (f32[3,8192]{1,0:T(4,128)S(1)}, f32[3,8192]{1,0:T(4,128)}, u32[]{:S(2)}) copy-start(f32[3,8192]{1,0:T(4,128)} %refs_9_.1) | copy-start | bytes 294916
  0.5 13.8 %copy-start.10 = (bf16[16,8192]{1,0:T(8,128)(2,1)S(1)}, bf16[16,8192]{1,0:T(8,128)(2,1)}, u32[]{:S(2)}) copy-start(bf16[16,8192]{1,0:T(8,128)(2,1)} %points_ref.7) | copy-start | bytes 786436
  8.0 6.2 %copy-start.12 = (s32[128,12]{0,1:T(8,128)S(1)}, s32[128,12]{0,1:T(8,128)}, u32[]{:S(2)}) copy-start(s32[128,12]{0,1:T(8,128)} %param.15) | copy-start | bytes 18436
  8.0 2.7 %collective-permute-start = (bf16[16,6400]{1,0:T(8,128)(2,1)}, bf16[16,6400]{1,0:T(8,128)(2,1)S(1)}, u32[]{:S(2)}, u32[]{:S(2)}) collective-permute-start(bf16[16,6400]{1,0:T(8,128)(2,1)} %get-tuple-element.23.after_ref.first_ref.payload_ref), channel_id=1, source_target_pairs={{0,1},{1,0},{2,3},{3,2},{4,5},{5,4},{6,7},{7,6},{8,9},{9,8},{10,11... | collective-permute-start | bytes 614408 | tf_op jit(solution)/shard_map/ppermute | solution.py:750
  8.2 0.9 %copy-start.1 = (bf16[16,6400]{1,0:T(8,128)(2,1)S(1)}, bf16[16,6400]{1,0:T(8,128)(2,1)}, u32[]{:S(2)}) copy-start(bf16[16,6400]{1,0:T(8,128)(2,1)} %get-tuple-element.23.after_ref.first_ref.payload_ref) | copy-start | bytes 614404
  10.6 0.9 %copy-start.2 = (bf16[16,6400]{1,0:T(8,128)(2,1)S(1)}, bf16[16,6400]{1,0:T(8,128)(2,1)}, u32[]{:S(2)}) copy-start(bf16[16,6400]{1,0:T(8,128)(2,1)} %get-tuple-element.23.after_ref.first_ref.payload_ref) | copy-start | bytes 614404
  12.5 6.8 %collective-permute-start.1 = (bf16[16,5376]{1,0:T(8,128)(2,1)S(1)}, bf16[16,5376]{1,0:T(8,128)(2,1)S(1)}, u32[]{:S(2)}, u32[]{:S(2)}) collective-permute-start(bf16[16,5376]{1,0:T(8,128)(2,1)S(1)} %shard_map.102.after_ref.payload_ref), channel_id=1, source_target_pairs={{0,2},{1,3},{2,0},{3,1},{4,6},{5,7},{6,4},{7,5},{8,10},{9,11},{10,... | collective-permute-start | bytes 516104 | tf_op jit(solution)/shard_map/ppermute | solution.py:750
  14.4 4.9 %copy-start.3 = (bf16[16,6400]{1,0:T(8,128)(2,1)S(1)}, bf16[16,6400]{1,0:T(8,128)(2,1)}, u32[]{:S(2)}) copy-start(bf16[16,6400]{1,0:T(8,128)(2,1)} %get-tuple-element.23.after_ref.first_ref.payload_ref) | copy-start | bytes 614404
  20.1 7.4 %collective-permute-start.2 = (bf16[16,5376]{1,0:T(8,128)(2,1)S(1)}, bf16[16,5376]{1,0:T(8,128)(2,1)S(1)}, u32[]{:S(2)}, u32[]{:S(2)}) collective-permute-start(bf16[16,5376]{1,0:T(8,128)(2,1)S(1)} %shard_map.104.after_ref.payload_ref), channel_id=1, source_target_pairs={{0,6},{1,7},{2,4},{3,5},{4,2},{5,3},{6,0},{7,1},{8,14},{9,15},{10,... | collective-permute-start | bytes 516104 | tf_op jit(solution)/shard_map/ppermute | solution.py:750
  28.3 5.4 %collective-permute-start.3 = (bf16[16,5376]{1,0:T(8,128)(2,1)S(1)}, bf16[16,5376]{1,0:T(8,128)(2,1)S(1)}, u32[]{:S(2)}, u32[]{:S(2)}) collective-permute-start(bf16[16,5376]{1,0:T(8,128)(2,1)S(1)} %shard_map.106.after_ref.payload_ref), channel_id=1, source_target_pairs={{0,8},{1,9},{2,10},{3,11},{4,12},{5,13},{6,14},{7,15},{8,0},{9,1},... | collective-permute-start | bytes 516104 | tf_op jit(solution)/shard_map/ppermute | solution.py:750
  30.3 8.6 %copy-start = (bf16[128,16,1024]{2,1,0:T(8,128)(2,1)S(1)}, bf16[128,16,1024]{2,1,0:T(8,128)(2,1)}, u32[]{:S(2)}) copy-start(bf16[128,16,1024]{2,1,0:T(8,128)(2,1)} %c_ref.3) | copy-start | bytes 12582916
  34.6 7.6 %collective-permute-start.4 = (bf16[16,5376]{1,0:T(8,128)(2,1)S(1)}, bf16[16,5376]{1,0:T(8,128)(2,1)S(1)}, u32[]{:S(2)}, u32[]{:S(2)}) collective-permute-start(bf16[16,5376]{1,0:T(8,128)(2,1)S(1)} %shard_map.108.after_ref.payload_ref), channel_id=1, source_target_pairs={{0,24},{1,25},{2,26},{3,27},{4,28},{5,29},{6,30},{7,31},{8,16},{9,... | collective-permute-start | bytes 516104 | tf_op jit(solution)/shard_map/ppermute | solution.py:750
  43.1 5.4 %collective-permute-start.5 = (bf16[16,5376]{1,0:T(8,128)(2,1)S(1)}, bf16[16,5376]{1,0:T(8,128)(2,1)S(1)}, u32[]{:S(2)}, u32[]{:S(2)}) collective-permute-start(bf16[16,5376]{1,0:T(8,128)(2,1)S(1)} %shard_map.110.after_ref.payload_ref), channel_id=1, source_target_pairs={{0,32},{1,33},{2,34},{3,35},{4,36},{5,37},{6,38},{7,39},{8,40},{9,... | collective-permute-start | bytes 516104 | tf_op jit(solution)/shard_map/ppermute | solution.py:750
  49.2 6.8 %copy-start.4 = (bf16[17,256,256]{2,1,0:T(8,128)(2,1)S(1)}, bf16[17,256,256]{2,1,0:T(8,128)(2,1)}, u32[]{:S(2)}) copy-start(bf16[17,256,256]{2,1,0:T(8,128)(2,1)} %get-tuple-element.32.refs_11_) | copy-start | bytes 6684676
  49.2 6.8 %copy-start.5 = (bf16[16,256,256]{2,1,0:T(8,128)(2,1)S(1)}, bf16[16,256,256]{2,1,0:T(8,128)(2,1)}, u32[]{:S(2)}) copy-start(bf16[16,256,256]{2,1,0:T(8,128)(2,1)} %get-tuple-element.35.refs_14_) | copy-start | bytes 6291460
  49.2 6.7 %collective-permute-start.6 = (bf16[16,5376]{1,0:T(8,128)(2,1)S(1)}, bf16[16,5376]{1,0:T(8,128)(2,1)S(1)}, u32[]{:S(2)}, u32[]{:S(2)}) collective-permute-start(bf16[16,5376]{1,0:T(8,128)(2,1)S(1)} %shard_map.112.after_ref), channel_id=1, source_target_pairs={{0,96},{1,97},{2,98},{3,99},{4,100},{5,101},{6,102},{7,103},{8,104... | collective-permute-start | bytes 516104 | tf_op jit(solution)/shard_map/ppermute | solution.py:750

commit v7 on v6

--- a/solution.py
+++ b/solution.py
@@ -601,11 +601,11 @@
         pltpu.make_async_copy(source, target, sem.at[k])
         for k, (source, target) in enumerate(
             (
+                (d0_ref, d_ref.at[pl.ds(0, half)]),
+                (d1_ref, d_ref.at[pl.ds(half, half)]),
                 (bdup_in, bdup_ref),
-                (d0_ref, d_ref.at[pl.ds(0, half)]),
                 (bd_in, bd_ref),
                 (ub_in, ub_ref),
-                (d1_ref, d_ref.at[pl.ds(half, half)]),
             )
         )
     ]
@@ -632,7 +632,7 @@
         edge_ref[own % 4] = acc
 
     edge_products(left_halo, right_halo, coords_ref, rel_ref, add)
-    for copy in copies:
+    for copy in copies[:2]:
         copy.wait()
     block = iota((16, 128), 1) // RANK
     which = iota((16, 256), 1) % 8
@@ -648,6 +648,8 @@
                     merged = value if low == 0 else jnp.where(block == low, value, merged)
                 gather_ref[step, 16 * leaf : 16 * leaf + 16, 128 * s_high : 128 * s_high + 128] = merged
         result = dot_nt(gather_ref[step], d_ref[step])
+        if step == 8:
+            copies[2].wait()
         next(chain, None)
         far = result[0:16]
         for leaf in range(1, 8):
@@ -655,6 +657,8 @@
         fars.append(far)
     for _ in chain:
         pass
+    for copy in copies[3:]:
+        copy.wait()
     leaf_fields = []
     for step in range(GROUPS):
         parent = field_ref[32 * (step // 2) : 32 * (step // 2) + 32, :]

time: 66.4 us -> 66.8 us (level)
  no operation moved by 1% of the time
where the time goes in v7:
time: 66.8 us; the launch traced here: 66.6 us
  Pallas kernels  44 us (66%)
  starting transfers between devices  15.4 us (23%)
  waiting for transfers between devices  4.1 us (6%)
  local copies, waits for them, and re-layouts  2.14 us (3%)
    ppermute x7, starting transfers between devices, per_device(): received.append(lax.ppermute(payload, 'leaf', route))  15.4 us
    pallas_call x4, Pallas kernels, near_chunk(): pl.pallas_call(functools.partial(near_kernel, chunk, blocks), out_shape=(...  13.6 us
    pallas_call x1, Pallas kernels, downward(): pl.pallas_call(down_kernel, out_shape=jax.ShapeDtypeStruct((16, LEAF_DEV...  10.5 us
    pallas_call x1, Pallas kernels, upward(): pl.pallas_call(up_kernel, out_shape=(jax.ShapeDtypeStruct((16, FIRST), bf...  7.42 us
    pallas_call x2, Pallas kernels, regroup(): pl.pallas_call(regroup_kernel, grid=(groups,), out_shape=(jax.ShapeDtypeS...  5.94 us
    pallas_call x6, Pallas kernels, tree_step(): pl.pallas_call(functools.partial(step_kernel, height), out_shape=jax.Shap...  5 us
    ppermute x7, waiting for transfers between devices, per_device(): received.append(lax.ppermute(payload, 'leaf', route))  4.1 us
    unnamed x28, local copies, waits for them, and re-layouts  1.95 us
  transfers between devices with their start and end apart: 7, of which 5 were waited for; matrix products, arithmetic and copies ran while one was open for 0% of the time, Pallas kernels for 32%

profile of v7, /device:TPU:0, one launch (start us, length us, event | category | flops | bytes accessed | tf_op | source)
XLA Modules:
  0.0 66.6 jit_solution(5954214877546988488)
XLA Ops:
  0.0 0.5 compare_select_fusion.bits_ref
  0.5 7.4 %shard_map.100 = (bf16[16,6400]{1,0:T(8,128)(2,1)}, bf16[16,512,256]{2,1,0:T(8,128)(2,1)}, bf16[16,256,256]{2,1,0:T(8,128)(2,1)}, bf16[17,256,256]{2,1,0:T(8,128)(2,1)}) custom-call(s32[8]{0:T(128)} %compare_select_fusion.bits_ref, bf16[16,8192]{1,0:T(8,128)(2,1)} %points_ref.7, f32[3,8192]{1,0:T(4,128)} %refs_9_.1, bf16[128,2048]{1,0:T(8,128)(2,1)} %basis_in.1, ...), custom_call_target="tpu_custom_call" | custom-call | flops 1000000000 | bytes 10000000 | tf_op jit(solution)/shard_map/pallas_call | solution.py:455
  8.0 0.0 copy-start.12
  8.0 0.1 collective-permute-start
  8.1 0.0 copy-done.13
  8.1 0.1 pad_add_fusion.nodes_ref
  8.2 0.0 copy-done.6
  8.2 0.0 copy-done.7
  8.2 0.9 %copy-done.1 = bf16[16,6400]{1,0:T(8,128)(2,1)S(1)} copy-done((bf16[16,6400]{1,0:T(8,128)(2,1)S(1)}, bf16[16,6400]{1,0:T(8,128)(2,1)}, u32[]{:S(2)}) %copy-start.1) | copy-done | bytes 204824
  9.1 1.5 %shard_map.101 = (bf16[320,128]{1,0:T(8,128)(2,1)S(1)}, bf16[192,128]{1,0:T(8,128)(2,1)S(1)}, f32[8,128]{1,0:T(8,128)S(1)}) custom-call(s32[16]{0:T(128)S(1)} %pad_add_fusion.nodes_ref, bf16[254,1024]{1,0:T(8,128)(2,1)S(1)} %copy-done.7, bf16[252,2,1024]{2,1,0:T(2,128)(2,1)S(1)} %copy-done.6, bf16[16,6400]{1,0:T(8,128)(2,1)S(1)} %copy-done.1), custom_call_target="tpu_custom_call" | custom-call | flops 100000000 | bytes 800000 | tf_op jit(solution)/shard_map/pallas_call | solution.py:428
  10.6 0.0 copy-done.11
  10.6 0.0 collective-permute-done.received_ref.refs_0_
  10.6 0.0 copy-done.9
  10.6 0.0 copy-start.2
  10.7 0.9 %copy-done.2 = bf16[16,6400]{1,0:T(8,128)(2,1)S(1)} copy-done((bf16[16,6400]{1,0:T(8,128)(2,1)S(1)}, bf16[16,6400]{1,0:T(8,128)(2,1)}, u32[]{:S(2)}) %copy-start.2) | copy-done | bytes 204824
  11.6 0.9 %shard_map.102.after_ref.payload_ref = bf16[16,5376]{1,0:T(8,128)(2,1)S(1)} custom-call(s32[8]{0:T(128)S(1)} %copy-done.9, bf16[16,6400]{1,0:T(8,128)(2,1)S(1)} %copy-done.2, bf16[16,6400]{1,0:T(8,128)(2,1)S(1)} %copy-done.2, bf16[16,6400]{1,0:T(8,128)(2,1)S(1)} %collective-permute-done.received_ref.refs_0_, ...), custom_call_target="tpu_custom_call" | custom-call | flops 1000000 | bytes 400000 | tf_op jit(solution)/shard_map/pallas_call | solution.py:505
  12.5 1.7 %collective-permute-start.1 = (bf16[16,5376]{1,0:T(8,128)(2,1)S(1)}, bf16[16,5376]{1,0:T(8,128)(2,1)S(1)}, u32[]{:S(2)}, u32[]{:S(2)}) collective-permute-start(bf16[16,5376]{1,0:T(8,128)(2,1)S(1)} %shard_map.102.after_ref.payload_ref), channel_id=1, source_target_pairs={{0,2},{1,3},{2,0},{3,1},{4,6},{5,7},{6,4},{7,5},{8,10},{9,11},{10,... | collective-permute-start | bytes 516104 | tf_op jit(solution)/shard_map/ppermute | solution.py:754
  14.2 0.0 copy-done.12
  14.2 0.1 copy.11
  14.3 0.1 mul.30.rest_1_.index_ref
  14.3 0.0 copy-done.8
  14.3 0.0 copy-done.10
  14.4 0.0 copy-start.3
  14.4 3.4 %shard_map.103 = (f32[16,2560]{1,0:T(8,128)S(1)}, f32[8,128]{1,0:T(8,128)S(1)}) custom-call(f32[3,8192]{1,0:T(4,128)S(1)} %copy-done.8, bf16[16,8192]{1,0:T(8,128)(2,1)S(1)} %copy-done.10, s32[12,128]{1,0:T(8,128)S(1)} %select_bitcast_fusion.rel_ref.refs_10_, bf16[16,5376]{1,0:T(8,128)(2,1)S(1)} %shard_map.102.after_ref.payload_ref), custom_call_target="tpu_custom_call" | custom-call | flops 1000000000 | bytes 1000000 | tf_op jit(solution)/shard_map/pallas_call | solution.py:188
  17.8 1.4 %collective-permute-done.1.received_ref.refs_1_ = bf16[16,5376]{1,0:T(8,128)(2,1)S(1)} collective-permute-done((bf16[16,5376]{1,0:T(8,128)(2,1)S(1)}, bf16[16,5376]{1,0:T(8,128)(2,1)S(1)}, u32[]{:S(2)}, u32[]{:S(2)}) %collective-permute-start.1) | collective-permute-done | bytes 172064 | tf_op jit(solution)/shard_map/ppermute | solution.py:754
  19.2 0.9 %shard_map.104.after_ref.payload_ref = bf16[16,5376]{1,0:T(8,128)(2,1)S(1)} custom-call(s32[8]{0:T(128)S(1)} %copy-done.9, bf16[16,6400]{1,0:T(8,128)(2,1)S(1)} %copy-done.3, bf16[16,5376]{1,0:T(8,128)(2,1)S(1)} %shard_map.102.after_ref.payload_ref, bf16[16,5376]{1,0:T(8,128)(2,1)S(1)} %collective-permute-done.1.received_ref.refs_1_, ...), custom_call_target="tpu_custom_call" | custom-call | flops 1000000 | bytes 400000 | tf_op jit(solution)/shard_map/pallas_call | solution.py:505
  20.1 3.1 %collective-permute-start.2 = (bf16[16,5376]{1,0:T(8,128)(2,1)S(1)}, bf16[16,5376]{1,0:T(8,128)(2,1)S(1)}, u32[]{:S(2)}, u32[]{:S(2)}) collective-permute-start(bf16[16,5376]{1,0:T(8,128)(2,1)S(1)} %shard_map.104.after_ref.payload_ref), channel_id=1, source_target_pairs={{0,6},{1,7},{2,4},{3,5},{4,2},{5,3},{6,0},{7,1},{8,14},{9,15},{10,... | collective-permute-start | bytes 516104 | tf_op jit(solution)/shard_map/ppermute | solution.py:754
  23.2 3.4 %shard_map.105 = (f32[16,2560]{1,0:T(8,128)S(1)}, f32[8,128]{1,0:T(8,128)S(1)}) custom-call(f32[3,8192]{1,0:T(4,128)S(1)} %copy-done.8, bf16[16,8192]{1,0:T(8,128)(2,1)S(1)} %copy-done.10, s32[12,128]{1,0:T(8,128)S(1)} %select_bitcast_fusion.rel_ref.refs_10_, bf16[16,5376]{1,0:T(8,128)(2,1)S(1)} %shard_map.104.after_ref.payload_ref), custom_call_target="tpu_custom_call" | custom-call | flops 1000000000 | bytes 1000000 | tf_op jit(solution)/shard_map/pallas_call | solution.py:188
  26.7 0.8 %collective-permute-done.2.received_ref.refs_2_ = bf16[16,5376]{1,0:T(8,128)(2,1)S(1)} collective-permute-done((bf16[16,5376]{1,0:T(8,128)(2,1)S(1)}, bf16[16,5376]{1,0:T(8,128)(2,1)S(1)}, u32[]{:S(2)}, u32[]{:S(2)}) %collective-permute-start.2) | collective-permute-done | bytes 172064 | tf_op jit(solution)/shard_map/ppermute | solution.py:754
  27.5 0.9 %shard_map.106.after_ref.payload_ref = bf16[16,5376]{1,0:T(8,128)(2,1)S(1)} custom-call(s32[8]{0:T(128)S(1)} %copy-done.9, bf16[16,6400]{1,0:T(8,128)(2,1)S(1)} %copy-done.3, bf16[16,5376]{1,0:T(8,128)(2,1)S(1)} %shard_map.104.after_ref.payload_ref, bf16[16,5376]{1,0:T(8,128)(2,1)S(1)} %collective-permute-done.2.received_ref.refs_2_, ...), custom_call_target="tpu_custom_call" | custom-call | flops 1000000 | bytes 400000 | tf_op jit(solution)/shard_map/pallas_call | solution.py:505
  28.3 1.9 %collective-permute-start.3 = (bf16[16,5376]{1,0:T(8,128)(2,1)S(1)}, bf16[16,5376]{1,0:T(8,128)(2,1)S(1)}, u32[]{:S(2)}, u32[]{:S(2)}) collective-permute-start(bf16[16,5376]{1,0:T(8,128)(2,1)S(1)} %shard_map.106.after_ref.payload_ref), channel_id=1, source_target_pairs={{0,8},{1,9},{2,10},{3,11},{4,12},{5,13},{6,14},{7,15},{8,0},{9,1},... | collective-permute-start | bytes 516104 | tf_op jit(solution)/shard_map/ppermute | solution.py:754
  30.3 3.4 %shard_map.107 = (f32[16,2560]{1,0:T(8,128)S(1)}, f32[8,128]{1,0:T(8,128)S(1)}) custom-call(f32[3,8192]{1,0:T(4,128)S(1)} %copy-done.8, bf16[16,8192]{1,0:T(8,128)(2,1)S(1)} %copy-done.10, s32[12,128]{1,0:T(8,128)S(1)} %select_bitcast_fusion.rel_ref.refs_10_, bf16[16,5376]{1,0:T(8,128)(2,1)S(1)} %shard_map.106.after_ref.payload_ref), custom_call_target="tpu_custom_call" | custom-call | flops 1000000000 | bytes 1000000 | tf_op jit(solution)/shard_map/pallas_call | solution.py:188
  33.7 0.0 collective-permute-done.3.received_ref.refs_3_
  33.8 0.9 %shard_map.108.after_ref.payload_ref = bf16[16,5376]{1,0:T(8,128)(2,1)S(1)} custom-call(s32[8]{0:T(128)S(1)} %copy-done.9, bf16[16,6400]{1,0:T(8,128)(2,1)S(1)} %copy-done.3, bf16[16,5376]{1,0:T(8,128)(2,1)S(1)} %shard_map.106.after_ref.payload_ref, bf16[16,5376]{1,0:T(8,128)(2,1)S(1)} %collective-permute-done.3.received_ref.refs_3_, ...), custom_call_target="tpu_custom_call" | custom-call | flops 1000000 | bytes 400000 | tf_op jit(solution)/shard_map/pallas_call | solution.py:505
  34.6 4.2 %collective-permute-start.4 = (bf16[16,5376]{1,0:T(8,128)(2,1)S(1)}, bf16[16,5376]{1,0:T(8,128)(2,1)S(1)}, u32[]{:S(2)}, u32[]{:S(2)}) collective-permute-start(bf16[16,5376]{1,0:T(8,128)(2,1)S(1)} %shard_map.108.after_ref.payload_ref), channel_id=1, source_target_pairs={{0,24},{1,25},{2,26},{3,27},{4,28},{5,29},{6,30},{7,31},{8,16},{9,... | collective-permute-start | bytes 516104 | tf_op jit(solution)/shard_map/ppermute | solution.py:754
  38.9 3.0 %shard_map.109 = (bf16[8,256,512]{2,1,0:T(8,128)(2,1)S(1)}, f32[8,128]{1,0:T(8,128)S(1)}) custom-call(bf16[128,16,1024]{2,1,0:T(8,128)(2,1)S(1)} %copy-done, bf16[16,5376]{1,0:T(8,128)(2,1)S(1)} %shard_map.108.after_ref.payload_ref), custom_call_target="tpu_custom_call" | custom-call | flops 600000000 | bytes 4200000 | tf_op jit(solution)/shard_map/pallas_call | solution.py:546
  41.8 0.4 collective-permute-done.4.received_ref.refs_4_
  42.2 0.9 %shard_map.110.after_ref.payload_ref = bf16[16,5376]{1,0:T(8,128)(2,1)S(1)} custom-call(s32[8]{0:T(128)S(1)} %copy-done.9, bf16[16,6400]{1,0:T(8,128)(2,1)S(1)} %copy-done.3, bf16[16,5376]{1,0:T(8,128)(2,1)S(1)} %shard_map.108.after_ref.payload_ref, bf16[16,5376]{1,0:T(8,128)(2,1)S(1)} %collective-permute-done.4.received_ref.refs_4_, ...), custom_call_target="tpu_custom_call" | custom-call | flops 1000000 | bytes 400000 | tf_op jit(solution)/shard_map/pallas_call | solution.py:505
  43.1 1.5 %collective-permute-start.5 = (bf16[16,5376]{1,0:T(8,128)(2,1)S(1)}, bf16[16,5376]{1,0:T(8,128)(2,1)S(1)}, u32[]{:S(2)}, u32[]{:S(2)}) collective-permute-start(bf16[16,5376]{1,0:T(8,128)(2,1)S(1)} %shard_map.110.after_ref.payload_ref), channel_id=1, source_target_pairs={{0,32},{1,33},{2,34},{3,35},{4,36},{5,37},{6,38},{7,39},{8,40},{9,... | collective-permute-start | bytes 516104 | tf_op jit(solution)/shard_map/ppermute | solution.py:754
  44.6 3.0 %shard_map.111 = (bf16[8,256,512]{2,1,0:T(8,128)(2,1)S(1)}, f32[8,128]{1,0:T(8,128)S(1)}) custom-call(bf16[128,16,1024]{2,1,0:T(8,128)(2,1)S(1)} %copy-done, bf16[16,5376]{1,0:T(8,128)(2,1)S(1)} %shard_map.110.after_ref.payload_ref), custom_call_target="tpu_custom_call" | custom-call | flops 600000000 | bytes 4200000 | tf_op jit(solution)/shard_map/pallas_call | solution.py:546
  47.6 0.9 %collective-permute-done.5.received_ref.refs_5_ = bf16[16,5376]{1,0:T(8,128)(2,1)S(1)} collective-permute-done((bf16[16,5376]{1,0:T(8,128)(2,1)S(1)}, bf16[16,5376]{1,0:T(8,128)(2,1)S(1)}, u32[]{:S(2)}, u32[]{:S(2)}) %collective-permute-start.5) | collective-permute-done | bytes 172064 | tf_op jit(solution)/shard_map/ppermute | solution.py:754
  48.5 0.6 shard_map.112.after_ref
  49.2 0.1 copy-start.5
  49.2 2.8 %collective-permute-start.6 = (bf16[16,5376]{1,0:T(8,128)(2,1)S(1)}, bf16[16,5376]{1,0:T(8,128)(2,1)S(1)}, u32[]{:S(2)}, u32[]{:S(2)}) collective-permute-start(bf16[16,5376]{1,0:T(8,128)(2,1)S(1)} %shard_map.112.after_ref), channel_id=1, source_target_pairs={{0,96},{1,97},{2,98},{3,99},{4,100},{5,101},{6,102},{7,103},{8,104... | collective-permute-start | bytes 516104 | tf_op jit(solution)/shard_map/ppermute | solution.py:754
  52.1 3.4 %shard_map.113 = (f32[16,2560]{1,0:T(8,128)S(1)}, f32[8,128]{1,0:T(8,128)}) custom-call(f32[3,8192]{1,0:T(4,128)S(1)} %copy-done.8, bf16[16,8192]{1,0:T(8,128)(2,1)S(1)} %copy-done.10, s32[12,128]{1,0:T(8,128)S(1)} %select_bitcast_fusion.rel_ref.refs_10_, bf16[16,5376]{1,0:T(8,128)(2,1)S(1)} %shard_map.112.after_ref), custom_call_target="tpu_custom_call" | custom-call | flops 1000000000 | bytes 1000000 | tf_op jit(solution)/shard_map/pallas_call | solution.py:188
  55.5 0.5 collective-permute-done.6.refs_6_
  55.9 0.0 copy-done.5
  55.9 10.5 %shard_map.114 = f32[16,8192]{1,0:T(8,128)} custom-call(s32[8]{0:T(128)S(1)} %copy-done.9, s32[2048]{0:T(1024)S(1)} %mul.30.rest_1_.index_ref, bf16[16,6400]{1,0:T(8,128)(2,1)S(1)} %copy-done.3, bf16[16,6400]{1,0:T(8,128)(2,1)S(1)} %collective-permute-done.received_ref.refs_0_, bf16[16,5376]{1,0:T(8,128)(2,1)S(1)} %collective-permute-done.1.received_ref.refs_1_, ...), custom_call_target="tpu_custom_call" | custom-call | flops 3000000000 | bytes 16000000 | tf_op jit(solution)/shard_map/pallas_call | solution.py:692
  (17 shorter events, 0.1 us)
Async XLA Ops:
  0.0 8.1 %copy-start.13 = (s32[6]{0:T(128)S(1)}, s32[6]{0:T(128)}, u32[]{:S(2)}) copy-start(s32[6]{0:T(128)} %constant.5.clone) | copy-start | bytes 76
  0.0 8.2 %copy-start.6 = (bf16[252,2,1024]{2,1,0:T(2,128)(2,1)S(1)}, bf16[252,2,1024]{2,1,0:T(2,128)(2,1)}, u32[]{:S(2)}) copy-start(bf16[252,2,1024]{2,1,0:T(2,128)(2,1)} %couple_ref.1) | copy-start | bytes 3096580
  0.0 8.2 %copy-start.7 = (bf16[254,1024]{1,0:T(8,128)(2,1)S(1)}, bf16[254,1024]{1,0:T(8,128)(2,1)}, u32[]{:S(2)}) copy-start(bf16[254,1024]{1,0:T(8,128)(2,1)} %transfer_ref.1) | copy-start | bytes 1560580
  0.5 10.1 %copy-start.11 = (s32[128,16]{0,1:T(8,128)S(1)}, s32[128,16]{0,1:T(8,128)}, u32[]{:S(2)}) copy-start(s32[128,16]{0,1:T(8,128)} %param.13) | copy-start | bytes 24580
  0.5 10.1 %copy-start.9 = (s32[8]{0:T(128)S(1)}, s32[8]{0:T(128)}, u32[]{:S(2)}) copy-start(s32[8]{0:T(128)} %compare_select_fusion.bits_ref) | copy-start | bytes 100
  0.5 13.8 %copy-start.8 = (f32[3,8192]{1,0:T(4,128)S(1)}, f32[3,8192]{1,0:T(4,128)}, u32[]{:S(2)}) copy-start(f32[3,8192]{1,0:T(4,128)} %refs_9_.1) | copy-start | bytes 294916
  0.5 13.8 %copy-start.10 = (bf16[16,8192]{1,0:T(8,128)(2,1)S(1)}, bf16[16,8192]{1,0:T(8,128)(2,1)}, u32[]{:S(2)}) copy-start(bf16[16,8192]{1,0:T(8,128)(2,1)} %points_ref.7) | copy-start | bytes 786436
  8.0 6.2 %copy-start.12 = (s32[128,12]{0,1:T(8,128)S(1)}, s32[128,12]{0,1:T(8,128)}, u32[]{:S(2)}) copy-start(s32[128,12]{0,1:T(8,128)} %param.15) | copy-start | bytes 18436
  8.0 2.7 %collective-permute-start = (bf16[16,6400]{1,0:T(8,128)(2,1)}, bf16[16,6400]{1,0:T(8,128)(2,1)S(1)}, u32[]{:S(2)}, u32[]{:S(2)}) collective-permute-start(bf16[16,6400]{1,0:T(8,128)(2,1)} %get-tuple-element.23.after_ref.first_ref.payload_ref), channel_id=1, source_target_pairs={{0,1},{1,0},{2,3},{3,2},{4,5},{5,4},{6,7},{7,6},{8,9},{9,8},{10,11... | collective-permute-start | bytes 614408 | tf_op jit(solution)/shard_map/ppermute | solution.py:754
  8.2 0.9 %copy-start.1 = (bf16[16,6400]{1,0:T(8,128)(2,1)S(1)}, bf16[16,6400]{1,0:T(8,128)(2,1)}, u32[]{:S(2)}) copy-start(bf16[16,6400]{1,0:T(8,128)(2,1)} %get-tuple-element.23.after_ref.first_ref.payload_ref) | copy-start | bytes 614404
  10.6 0.9 %copy-start.2 = (bf16[16,6400]{1,0:T(8,128)(2,1)S(1)}, bf16[16,6400]{1,0:T(8,128)(2,1)}, u32[]{:S(2)}) copy-start(bf16[16,6400]{1,0:T(8,128)(2,1)} %get-tuple-element.23.after_ref.first_ref.payload_ref) | copy-start | bytes 614404
  12.5 6.8 %collective-permute-start.1 = (bf16[16,5376]{1,0:T(8,128)(2,1)S(1)}, bf16[16,5376]{1,0:T(8,128)(2,1)S(1)}, u32[]{:S(2)}, u32[]{:S(2)}) collective-permute-start(bf16[16,5376]{1,0:T(8,128)(2,1)S(1)} %shard_map.102.after_ref.payload_ref), channel_id=1, source_target_pairs={{0,2},{1,3},{2,0},{3,1},{4,6},{5,7},{6,4},{7,5},{8,10},{9,11},{10,... | collective-permute-start | bytes 516104 | tf_op jit(solution)/shard_map/ppermute | solution.py:754
  14.4 4.9 %copy-start.3 = (bf16[16,6400]{1,0:T(8,128)(2,1)S(1)}, bf16[16,6400]{1,0:T(8,128)(2,1)}, u32[]{:S(2)}) copy-start(bf16[16,6400]{1,0:T(8,128)(2,1)} %get-tuple-element.23.after_ref.first_ref.payload_ref) | copy-start | bytes 614404
  20.1 7.4 %collective-permute-start.2 = (bf16[16,5376]{1,0:T(8,128)(2,1)S(1)}, bf16[16,5376]{1,0:T(8,128)(2,1)S(1)}, u32[]{:S(2)}, u32[]{:S(2)}) collective-permute-start(bf16[16,5376]{1,0:T(8,128)(2,1)S(1)} %shard_map.104.after_ref.payload_ref), channel_id=1, source_target_pairs={{0,6},{1,7},{2,4},{3,5},{4,2},{5,3},{6,0},{7,1},{8,14},{9,15},{10,... | collective-permute-start | bytes 516104 | tf_op jit(solution)/shard_map/ppermute | solution.py:754
  28.3 5.4 %collective-permute-start.3 = (bf16[16,5376]{1,0:T(8,128)(2,1)S(1)}, bf16[16,5376]{1,0:T(8,128)(2,1)S(1)}, u32[]{:S(2)}, u32[]{:S(2)}) collective-permute-start(bf16[16,5376]{1,0:T(8,128)(2,1)S(1)} %shard_map.106.after_ref.payload_ref), channel_id=1, source_target_pairs={{0,8},{1,9},{2,10},{3,11},{4,12},{5,13},{6,14},{7,15},{8,0},{9,1},... | collective-permute-start | bytes 516104 | tf_op jit(solution)/shard_map/ppermute | solution.py:754
  30.3 8.6 %copy-start = (bf16[128,16,1024]{2,1,0:T(8,128)(2,1)S(1)}, bf16[128,16,1024]{2,1,0:T(8,128)(2,1)}, u32[]{:S(2)}) copy-start(bf16[128,16,1024]{2,1,0:T(8,128)(2,1)} %c_ref.3) | copy-start | bytes 12582916
  34.6 7.6 %collective-permute-start.4 = (bf16[16,5376]{1,0:T(8,128)(2,1)S(1)}, bf16[16,5376]{1,0:T(8,128)(2,1)S(1)}, u32[]{:S(2)}, u32[]{:S(2)}) collective-permute-start(bf16[16,5376]{1,0:T(8,128)(2,1)S(1)} %shard_map.108.after_ref.payload_ref), channel_id=1, source_target_pairs={{0,24},{1,25},{2,26},{3,27},{4,28},{5,29},{6,30},{7,31},{8,16},{9,... | collective-permute-start | bytes 516104 | tf_op jit(solution)/shard_map/ppermute | solution.py:754
  43.1 5.4 %collective-permute-start.5 = (bf16[16,5376]{1,0:T(8,128)(2,1)S(1)}, bf16[16,5376]{1,0:T(8,128)(2,1)S(1)}, u32[]{:S(2)}, u32[]{:S(2)}) collective-permute-start(bf16[16,5376]{1,0:T(8,128)(2,1)S(1)} %shard_map.110.after_ref.payload_ref), channel_id=1, source_target_pairs={{0,32},{1,33},{2,34},{3,35},{4,36},{5,37},{6,38},{7,39},{8,40},{9,... | collective-permute-start | bytes 516104 | tf_op jit(solution)/shard_map/ppermute | solution.py:754
  49.2 6.8 %copy-start.4 = (bf16[17,256,256]{2,1,0:T(8,128)(2,1)S(1)}, bf16[17,256,256]{2,1,0:T(8,128)(2,1)}, u32[]{:S(2)}) copy-start(bf16[17,256,256]{2,1,0:T(8,128)(2,1)} %get-tuple-element.32.refs_11_) | copy-start | bytes 6684676
  49.2 6.8 %copy-start.5 = (bf16[16,256,256]{2,1,0:T(8,128)(2,1)S(1)}, bf16[16,256,256]{2,1,0:T(8,128)(2,1)}, u32[]{:S(2)}) copy-start(bf16[16,256,256]{2,1,0:T(8,128)(2,1)} %get-tuple-element.35.refs_14_) | copy-start | bytes 6291460
  49.2 6.7 %collective-permute-start.6 = (bf16[16,5376]{1,0:T(8,128)(2,1)S(1)}, bf16[16,5376]{1,0:T(8,128)(2,1)S(1)}, u32[]{:S(2)}, u32[]{:S(2)}) collective-permute-start(bf16[16,5376]{1,0:T(8,128)(2,1)S(1)} %shard_map.112.after_ref), channel_id=1, source_target_pairs={{0,96},{1,97},{2,98},{3,99},{4,100},{5,101},{6,102},{7,103},{8,104... | collective-permute-start | bytes 516104 | tf_op jit(solution)/shard_map/ppermute | solution.py:754
